TPU v7x, 32 devices: a whole 2x2x4 slice. The times are simulated.
32 devices in a mesh: grp: 2 (over x), tile: 16 (over z, y, core).
Axes of the slice: x: 2, y: 2, z: 4, core: 2. Of those that a mesh axis runs over, the one named last changes fastest.
Arguments:
- x_tiles: bfloat16 [32, 16, 16, 256], P(('grp', 'tile')), parts along dimension 0, may hold values from -6 to 6
- h_tiles: bfloat16 [32, 16, 16, 256], P(('grp', 'tile')), parts along dimension 0, may hold values from -6 to 6
- grad_out: bfloat16 [32, 16, 16, 256], P(('grp', 'tile')), parts along dimension 0, may hold values from -6 to 6
- w_gate: bfloat16 [4608, 512], replicated, may hold values from -0.09375 to 0.09375
- b_gate: float32 [512], replicated, may hold values from -3 to 3
- w_cand: bfloat16 [4608, 256], replicated, may hold values from -0.09375 to 0.09375
- b_cand: float32 [256], replicated, may hold values from -3 to 3
- partner_edge: int32 [16, 4], replicated, may hold values from 0 to 63, as said below
- edge_flip: int32 [16, 4], replicated, may hold values from 0 to 1, as said below
- tile_slot: int32 [16], replicated, may hold values from 0 to 15, as said below
Outputs:
- grad_x: bfloat16 [32, 16, 16, 256], P(('grp', 'tile')), parts along dimension 0
- grad_h: bfloat16 [32, 16, 16, 256], P(('grp', 'tile')), parts along dimension 0
- grad_w_gate: float32 [9216, 512], P(('grp', 'tile')), parts along dimension 0
- grad_w_cand: float32 [9216, 256], P(('grp', 'tile')), parts along dimension 0
There are 2 independent parts, one for each index of `grp`. A program takes and returns all parts, laid end to end along the dimension named above; an argument that names none is the same for every part. Nothing has to cross between parts.
Inputs may be any that keep to these rules, and one draw needn't show every extreme that they name: `partner_edge`: the matching is an involution over all 64 tile edges and never joins a tile to itself; of each tile's four edges, two meet edges of the tile in the next slot and two meet edges of the tile in the previous slot, slots counted cyclically. `edge_flip`: equal at both edges of a matched pair. `tile_slot`: A permutation of the slots.
All inputs are finite; a program needn't handle non-finite values.
Results may differ from a plain program's by a relative error of at most 0.0051.
Values may be sent and summed in bfloat16 or wider, within the bound.
No kernel may reach another device: no remote copies, remote signals or barrier semaphores. Data moves between devices by JAX's collectives and lax.ppermute only.
A program may use at most 128 MiB of HBM per device.

v0:
```python
import jax
import jax.numpy as jnp
from jax import lax
from jax.sharding import PartitionSpec as P


def with_halo(array, sides, width):
    for axis, dim in sides:
        size, length = (lax.axis_size(axis), array.shape[dim])
        up = [(i, (i + 1) % size) for i in range(size)]
        down = [(j, i) for i, j in up]
        last = lax.slice_in_dim(array, length - width, length, axis=dim)
        initial = lax.slice_in_dim(array, 0, width, axis=dim)
        before = lax.ppermute(last, axis, up)
        after = lax.ppermute(initial, axis, down)
        array = jnp.concatenate([before, array, after], axis=dim)
    return array


def edge_strips(single):
    return jnp.stack([single[0], single[:, -1], single[-1], single[:, 0]], axis=0)


def select_strips(extended, chooser, flip_bits):
    flat_rows = extended.reshape(extended.shape[0], -1)
    if extended.dtype == jnp.bfloat16:
        picked = jnp.dot(
            chooser.astype(jnp.bfloat16), flat_rows, preferred_element_type=jnp.float32
        ).astype(jnp.bfloat16)
    else:
        picked = jnp.dot(chooser.astype(jnp.float32), flat_rows, precision=lax.Precision.HIGHEST)
    picked = picked.reshape((4,) + extended.shape[1:])
    return jnp.where(flip_bits[:, None, None] == 1, picked[:, ::-1], picked)


def framed(single, arrived):
    padded = jnp.pad(single, ((1, 1), (1, 1), (0, 0)))
    padded = padded.at[0, 1:-1].set(arrived[0])
    padded = padded.at[1:-1, -1].set(arrived[1])
    padded = padded.at[-1, 1:-1].set(arrived[2])
    padded = padded.at[1:-1, 0].set(arrived[3])
    return padded


def patches_of(padded):
    tile_side = padded.shape[0] - 2
    columns = [
        padded[row_tap : row_tap + tile_side, col_tap : col_tap + tile_side]
        for row_tap in range(3)
        for col_tap in range(3)
    ]
    return jnp.concatenate(columns, axis=-1).reshape(tile_side * tile_side, 9 * padded.shape[-1])


def unpatch(dpatch, tile_side, channels):
    dpatch = dpatch.reshape(tile_side, tile_side, 9, channels)
    result = jnp.zeros((tile_side + 2, tile_side + 2, channels), jnp.float32)
    for row_tap in range(3):
        for col_tap in range(3):
            result = result.at[row_tap : row_tap + tile_side, col_tap : col_tap + tile_side].add(
                dpatch[:, :, row_tap * 3 + col_tap]
            )
    return result


def rim_of(padded):
    return jnp.stack([padded[0, 1:-1], padded[1:-1, -1], padded[-1, 1:-1], padded[1:-1, 0]], axis=0)


def settle(padded, arrived):
    interior = padded[1:-1, 1:-1]
    interior = interior.at[0].add(arrived[0])
    interior = interior.at[:, -1].add(arrived[1])
    interior = interior.at[-1].add(arrived[2])
    interior = interior.at[:, 0].add(arrived[3])
    return interior


def contract(patch_rows, grad_rows):
    return jnp.einsum("ck,co->ko", patch_rows, grad_rows, preferred_element_type=jnp.float32)


def shards(
    x_tiles, h_tiles, grad_out, w_gate, b_gate, w_cand, b_cand, partner_edge, edge_flip, tile_slot
):
    tile_side = x_tiles.shape[1]
    channels = x_tiles.shape[3]
    tile_count = lax.axis_size("tile")
    my_slot = lax.axis_index("tile")
    slot_range = jnp.arange(tile_count, dtype=jnp.int32)
    holder = jnp.sum(jnp.where(tile_slot == my_slot, slot_range, 0))
    partners = lax.dynamic_index_in_dim(partner_edge, holder, 0, keepdims=False)
    flip_bits = lax.dynamic_index_in_dim(edge_flip, holder, 0, keepdims=False)
    partner_slot = jnp.sum(
        jnp.where(slot_range[None, :] == (partners // 4)[:, None], tile_slot[None, :], 0), axis=1
    )
    offset = (partner_slot - my_slot + 1) % tile_count
    pick_index = offset * 4 + partners % 4
    chooser = jnp.arange(12, dtype=jnp.int32)[None, :] == pick_index[:, None]
    x_single = x_tiles[0]
    h_single = h_tiles[0]
    joined = jnp.concatenate([x_single, h_single], axis=-1)
    extended = with_halo(edge_strips(joined), (("tile", 0),), 4)
    padded_gate = framed(joined, select_strips(extended, chooser, flip_bits))
    patch_gate = patches_of(padded_gate)
    gate_act = jax.nn.sigmoid(
        jnp.dot(patch_gate, w_gate, preferred_element_type=jnp.float32) + b_gate
    )
    update_gate = gate_act[:, :channels]
    reset_gate = gate_act[:, channels:]
    h_flat = h_single.reshape(-1, channels).astype(jnp.float32)
    reset_h = (reset_gate * h_flat).astype(jnp.bfloat16).reshape(tile_side, tile_side, channels)
    extended_reset = with_halo(edge_strips(reset_h), (("tile", 0),), 4)
    padded_reset = framed(reset_h, select_strips(extended_reset, chooser, flip_bits))
    patch_cand = patches_of(jnp.concatenate([padded_gate[..., :channels], padded_reset], axis=-1))
    candidate = jnp.tanh(jnp.dot(patch_cand, w_cand, preferred_element_type=jnp.float32) + b_cand)
    grad_flat = grad_out[0].reshape(-1, channels).astype(jnp.float32)
    d_update = grad_flat * (candidate - h_flat)
    d_cand_pre = (grad_flat * update_gate * (1.0 - candidate * candidate)).astype(jnp.bfloat16)
    grad_w_cand = lax.psum_scatter(
        contract(patch_cand, d_cand_pre), "tile", scatter_dimension=0, tiled=True
    )
    grid_cand = unpatch(
        jnp.dot(d_cand_pre, w_cand.T, preferred_element_type=jnp.float32), tile_side, 2 * channels
    )
    extended_cand = with_halo(rim_of(grid_cand).astype(jnp.bfloat16), (("tile", 0),), 4).astype(
        jnp.float32
    )
    back_cand = settle(grid_cand, select_strips(extended_cand, chooser, flip_bits))
    dx_cand = back_cand[..., :channels]
    d_rh = back_cand[..., channels:]
    d_rh = d_rh.reshape(-1, channels)
    d_gate_pre = jnp.concatenate(
        [
            d_update * update_gate * (1.0 - update_gate),
            d_rh * h_flat * reset_gate * (1.0 - reset_gate),
        ],
        axis=-1,
    ).astype(jnp.bfloat16)
    grid_gate = unpatch(
        jnp.dot(d_gate_pre, w_gate.T, preferred_element_type=jnp.float32), tile_side, 2 * channels
    )
    rim_gate = rim_of(grid_gate)
    extended_gate = with_halo(rim_gate.astype(jnp.bfloat16), (("tile", 0),), 4).astype(
        rim_gate.dtype
    )
    back_gate = settle(grid_gate, select_strips(extended_gate, chooser, flip_bits))
    grad_w_gate = lax.psum_scatter(
        contract(patch_gate, d_gate_pre), "tile", scatter_dimension=0, tiled=True
    )
    grad_x = (dx_cand + back_gate[..., :channels]).astype(jnp.bfloat16)
    direct = (grad_flat * (1.0 - update_gate) + d_rh * reset_gate).reshape(
        tile_side, tile_side, channels
    )
    grad_h = (direct + back_gate[..., channels:]).astype(jnp.bfloat16)
    return (grad_x[None], grad_h[None], grad_w_gate, grad_w_cand)


def solution(mesh):
    in_specs = (
        P(("grp", "tile"), None, None, None),
        P(("grp", "tile"), None, None, None),
        P(("grp", "tile"), None, None, None),
        P(),
        P(),
        P(),
        P(),
        P(),
        P(),
        P(),
    )
    out_specs = (
        P(("grp", "tile"), None, None, None),
        P(("grp", "tile"), None, None, None),
        P(("grp", "tile"), None),
        P(("grp", "tile"), None),
    )
    return jax.shard_map(shards, mesh=mesh, in_specs=in_specs, out_specs=out_specs, check_vma=False)
```

profile of v0, /device:TPU:0, one launch (start us, length us, event | category | flops | bytes accessed | tf_op | source)
XLA Modules:
  0.0 246.2 jit_solution(2090281797576076672)
XLA Ops:
  9.2 5.5 %collective-permute-start.1 = (bf16[4,16,512]{2,1,0:T(8,128)(2,1)S(1)}, bf16[4,16,512]{2,1,0:T(8,128)(2,1)S(1)}, u32[]{:S(2)}, u32[]{:S(2)}) collective-permute-start(bf16[4,16,512]{2,1,0:T(8,128)(2,1)S(1)} %pad_maximum_fusion.5), channel_id=1, source_target_pairs={{1,0},{2,1},{3,2},{4,3},{5,4},{6,5},{7,6},{8,7},{9,8},{10,9},{11,1... | collective-permute-start | bytes 196616 | tf_op jit(solution)/shard_map/ppermute | solution.py:15
  25.9 2.5 %copy-done.2 = bf16[4608,512]{1,0:T(8,128)(2,1)S(1)} copy-done((bf16[4608,512]{1,0:T(8,128)(2,1)S(1)}, bf16[4608,512]{1,0:T(8,128)(2,1)}, u32[]{:S(2)}) %copy-start.2) | copy-done | bytes 4718616
  30.1 4.5 %collective-permute-start.3 = (bf16[4,16,256]{2,1,0:T(8,128)(2,1)S(1)}, bf16[4,16,256]{2,1,0:T(8,128)(2,1)S(1)}, u32[]{:S(2)}, u32[]{:S(2)}) collective-permute-start(bf16[4,16,256]{2,1,0:T(8,128)(2,1)S(1)} %pad_maximum_fusion.8), channel_id=1, source_target_pairs={{1,0},{2,1},{3,2},{4,3},{5,4},{6,5},{7,6},{8,7},{9,8},{10,9},{11,1... | collective-permute-start | bytes 98312 | tf_op jit(solution)/shard_map/ppermute | solution.py:15
  36.2 4.4 %collective-permute-done.2 = bf16[4,16,256]{2,1,0:T(8,128)(2,1)S(1)} collective-permute-done((bf16[4,16,256]{2,1,0:T(8,128)(2,1)S(1)}, bf16[4,16,256]{2,1,0:T(8,128)(2,1)S(1)}, u32[]{:S(2)}, u32[]{:S(2)}) %collective-permute-start.2) | collective-permute-done | bytes 32800 | tf_op jit(solution)/shard_map/ppermute | solution.py:14
  45.1 3.0 %fusion.80 = f32[4608,256]{1,0:T(8,128)} fusion(bf16[256,4608]{1,0:T(8,128)(2,1)S(1)} %bitcast.218, bf16[256,256]{1,0:T(8,128)(2,1)S(1)} %get-tuple-element.435), kind=kOutput, calls=%fused_computation.211 | convolution fusion | flops 603979776 | bytes 7208960 | tf_op jit(solution)/shard_map/ck,co->ko/dot_general | solution.py:80
  49.7 3.0 %fusion.79 = f32[256,4608]{1,0:T(8,128)} fusion(bf16[256,256]{1,0:T(8,128)(2,1)S(1)} %get-tuple-element.435, bf16[4608,256]{1,0:T(8,128)(2,1)S(1)} %copy-done), kind=kOutput, calls=%fused_computation.210 | convolution fusion | flops 603979776 | bytes 7208960 | tf_op jit(solution)/shard_map/dot_general | solution.py:124
  52.7 7.2 %reshape.1272 = f32[16,16,9,512]{3,2,1,0:T(8,128)} reshape(f32[256,4608]{1,0:T(8,128)} %fusion.79) | data formatting | bytes 9437184 | tf_op jit(solution)/shard_map/reshape | solution.py:56
  59.9 17.2 %fusion.69 = (f32[16,16,1,512]{3,2,1,0:T(1,128)S(1)}, f32[16,16,1,512]{3,2,1,0:T(1,128)S(1)}, f32[16,16,1,512]{3,2,1,0:T(1,128)}, f32[16,16,1,512]{3,2,1,0:T(1,1...) fusion(f32[16,16,9,512]{3,2,1,0:T(8,128)} %reshape.1272), kind=kLoop, calls=%fused_computation.200 | loop fusion | bytes 9437184 | tf_op jit(solution)/shard_map/slice | solution.py:61
  77.5 2.4 fusion.6
  79.9 3.8 %scatter-add.89 = f32[18,18,512]{2,0,1:T(8,128)S(1)} dynamic-update-slice(f32[18,18,512]{2,0,1:T(8,128)S(1)} %scatter-add.86, f32[16,16,512]{2,0,1:T(8,128)} %fusion.6, s32[]{:T(128)} %bitcast.7, s32[]{:T(128)} %bitcast.8, s32[]{:T(128)} %constant.877.clone.1) | dynamic-update-slice | bytes 1048580 | tf_op jit(solution)/shard_map/scatter-add | solution.py:60
  83.7 3.9 %add_select_fusion.1 = f32[16,16,512]{2,0,1:T(8,128)} fusion(f32[16,16,1,512]{3,2,1,0:T(1,128)} %get-tuple-element.431, f32[18,18,512]{2,0,1:T(8,128)S(1)} %scatter-add.89, s32[]{:T(128)} %bitcast.23, s32[]{:T(128)} %bitcast.24, pred[]{:T(512)} %and_reduce_fusion), kind=kLoop, calls=%fused_computation.26 | loop fusion | flops 262144 | bytes 1572873 | tf_op jit(solution)/shard_map/select.44
  87.6 3.6 %scatter-add.90 = f32[18,18,512]{2,0,1:T(8,128)S(1)} dynamic-update-slice(f32[18,18,512]{2,0,1:T(8,128)S(1)} %scatter-add.89, f32[16,16,512]{2,0,1:T(8,128)} %add_select_fusion.1, s32[]{:T(128)} %bitcast.23, s32[]{:T(128)} %bitcast.24, s32[]{:T(128)} %constant.877.clone.1) | dynamic-update-slice | bytes 1048580 | tf_op jit(solution)/shard_map/scatter-add | solution.py:60
  92.4 2.4 scatter-add.91
  97.0 2.4 scatter-add.94
  101.6 2.4 scatter-add.95
  105.2 2.4 scatter-add.96
  111.0 2.8 %collective-permute-done.5 = bf16[4,16,512]{2,0,1:T(4,128)(2,1)S(1)} collective-permute-done((bf16[4,16,512]{2,0,1:T(4,128)(2,1)S(1)}, bf16[4,16,512]{2,0,1:T(4,128)(2,1)S(1)}, u32[]{:S(2)}, u32[]{:S(2)}) %collective-permute-start.5) | collective-permute-done | bytes 65568 | tf_op jit(solution)/shard_map/ppermute | solution.py:15
  113.8 4.6 %collective-permute-done.4 = bf16[4,16,512]{2,0,1:T(4,128)(2,1)S(1)} collective-permute-done((bf16[4,16,512]{2,0,1:T(4,128)(2,1)S(1)}, bf16[4,16,512]{2,0,1:T(4,128)(2,1)S(1)}, u32[]{:S(2)}, u32[]{:S(2)}) %collective-permute-start.4) | collective-permute-done | bytes 65568 | tf_op jit(solution)/shard_map/ppermute | solution.py:14
  121.1 6.8 %fusion.40 = f32[4608,512]{1,0:T(8,128)} fusion(bf16[256,4608]{1,0:T(8,128)(2,1)} %bitcast.224, bf16[256,256]{1,0:T(8,128)(2,1)S(1)} %get-tuple-element.437, bf16[256,256]{1,0:T(8,128)(2,1)S(1)} %get-tuple-element.434), kind=kOutput, calls=%fused_computation.125 | convolution fusion | flops 1208483840 | bytes 12058624 | tf_op jit(solution)/shard_map/ck,co->ko/dot_general | solution.py:80
  127.9 6.0 %fusion.41 = f32[256,4608]{1,0:T(8,128)} fusion(bf16[4608,512]{1,0:T(8,128)(2,1)} %param.81, bf16[256,256]{1,0:T(8,128)(2,1)S(1)} %get-tuple-element.437, bf16[256,256]{1,0:T(8,128)(2,1)S(1)} %get-tuple-element.434), kind=kOutput, calls=%fused_computation.126 | convolution fusion | flops 1208483840 | bytes 9699328 | tf_op jit(solution)/shard_map/dot_general | solution.py:141
  133.9 7.2 %reshape.1287 = f32[16,16,9,512]{3,2,1,0:T(8,128)} reshape(f32[256,4608]{1,0:T(8,128)} %fusion.41) | data formatting | bytes 9437184 | tf_op jit(solution)/shard_map/reshape | solution.py:56
  141.1 17.8 %fusion.68 = (f32[16,16,1,512]{3,2,1,0:T(1,128)S(1)}, f32[16,16,1,512]{3,2,1,0:T(1,128)S(1)}, f32[16,16,1,512]{3,2,1,0:T(1,128)S(1)}, f32[16,16,1,512]{3,2,1,0:T...) fusion(f32[16,16,9,512]{3,2,1,0:T(8,128)} %reshape.1287), kind=kLoop, calls=%fused_computation.199 | loop fusion | bytes 9437184 | tf_op jit(solution)/shard_map/slice | solution.py:61
  159.3 2.5 %fusion.5 = f32[16,16,512]{2,0,1:T(8,128)} fusion(f32[16,16,1,512]{3,2,1,0:T(1,128)S(1)} %get-tuple-element.423, s32[]{:T(128)} %bitcast.7, s32[]{:T(128)} %bitcast.8, f32[16,16,512]{2,0,1:T(8,128)S(1)} %bitcast.220), kind=kLoop, calls=%fused_computation.47 | loop fusion | flops 131072 | bytes 1572872 | tf_op jit(solution)/shard_map/add | solution.py:60
  161.8 3.7 %scatter-add.110 = f32[18,18,512]{2,0,1:T(8,128)S(1)} dynamic-update-slice(f32[18,18,512]{2,0,1:T(8,128)S(1)} %scatter-add.109, f32[16,16,512]{2,0,1:T(8,128)} %fusion.5, s32[]{:T(128)} %bitcast.7, s32[]{:T(128)} %bitcast.8, s32[]{:T(128)} %constant.877.clone.1) | dynamic-update-slice | bytes 1048580 | tf_op jit(solution)/shard_map/scatter-add | solution.py:60
  165.5 3.1 %add_select_fusion = f32[16,16,512]{2,0,1:T(8,128)S(1)} fusion(f32[16,16,1,512]{3,2,1,0:T(1,128)} %get-tuple-element.422, f32[18,18,512]{2,0,1:T(8,128)S(1)} %scatter-add.110, s32[]{:T(128)} %bitcast.23, s32[]{:T(128)} %bitcast.24, pred[]{:T(512)} %and_reduce_fusion), kind=kLoop, calls=%fused_computation.25 | loop fusion | flops 262144 | bytes 1572873 | tf_op jit(solution)/shard_map/select.57
  170.7 2.3 slice_add_fusion.5
  173.0 2.4 scatter-add.114
  177.5 2.4 scatter-add.115
  181.1 2.4 scatter-add.116
  189.5 2.5 %collective-permute-done.7 = bf16[4,16,512]{2,0,1:T(4,128)(2,1)S(1)} collective-permute-done((bf16[4,16,512]{2,0,1:T(4,128)(2,1)S(1)}, bf16[4,16,512]{2,0,1:T(4,128)(2,1)S(1)}, u32[]{:S(2)}, u32[]{:S(2)}) %collective-permute-start.7) | collective-permute-done | bytes 65568 | tf_op jit(solution)/shard_map/ppermute | solution.py:15
  192.6 4.1 %collective-permute-done.6 = bf16[4,16,512]{2,0,1:T(4,128)(2,1)} collective-permute-done((bf16[4,16,512]{2,0,1:T(4,128)(2,1)S(1)}, bf16[4,16,512]{2,0,1:T(4,128)(2,1)}, u32[]{:S(2)}, u32[]{:S(2)}) %collective-permute-start.6) | collective-permute-done | bytes 65568 | tf_op jit(solution)/shard_map/ppermute | solution.py:14
  210.9 28.4 %reduce-scatter.3.cloned.1.call-done = f32[288,512]{1,0:T(8,128)} async-done(((f32[4608,512]{1,0:T(8,128)}), f32[288,512]{1,0:T(8,128)}) %reduce-scatter.3.cloned.1.call-update) | async-done | bytes 589840 | tf_op jit(solution)/shard_map/reduce_scatter | solution.py:148
  (197 shorter events, 59.5 us)
Async XLA Ops:
  7.2 36.6 %copy-start = (bf16[4608,256]{1,0:T(8,128)(2,1)S(1)}, bf16[4608,256]{1,0:T(8,128)(2,1)}, u32[]{:S(2)}) copy-start(bf16[4608,256]{1,0:T(8,128)(2,1)} %param.83) | copy-start | bytes 7077892
  7.2 203.7 %reduce-scatter.5.cloned.1.call-start = ((), (), s32[]{:S(2)}) async-start(), calls=%async_computation.3 | async-start | bytes 5013504 | tf_op jit(solution)/shard_map/reduce_scatter | solution.py:120
  9.2 13.1 %collective-permute-start.1 = (bf16[4,16,512]{2,1,0:T(8,128)(2,1)S(1)}, bf16[4,16,512]{2,1,0:T(8,128)(2,1)S(1)}, u32[]{:S(2)}, u32[]{:S(2)}) collective-permute-start(bf16[4,16,512]{2,1,0:T(8,128)(2,1)S(1)} %pad_maximum_fusion.5), channel_id=1, source_target_pairs={{1,0},{2,1},{3,2},{4,3},{5,4},{6,5},{7,6},{8,7},{9,8},{10,9},{11,1... | collective-permute-start | bytes 196616 | tf_op jit(solution)/shard_map/ppermute | solution.py:15
  14.7 7.7 %collective-permute-start = (bf16[4,16,512]{2,1,0:T(8,128)(2,1)S(1)}, bf16[4,16,512]{2,1,0:T(8,128)(2,1)S(1)}, u32[]{:S(2)}, u32[]{:S(2)}) collective-permute-start(bf16[4,16,512]{2,1,0:T(8,128)(2,1)S(1)} %pad_maximum_fusion.5), channel_id=1, source_target_pairs={{0,1},{1,2},{2,3},{3,4},{4,5},{5,6},{6,7},{7,8},{8,9},{9,10},{10,1... | collective-permute-start | bytes 196616 | tf_op jit(solution)/shard_map/ppermute | solution.py:14
  25.1 0.9 copy-start.20
  25.2 3.2 %copy-start.2 = (bf16[4608,512]{1,0:T(8,128)(2,1)S(1)}, bf16[4608,512]{1,0:T(8,128)(2,1)}, u32[]{:S(2)}) copy-start(bf16[4608,512]{1,0:T(8,128)(2,1)} %param.81) | copy-start | bytes 14155780
  25.9 4.0 %copy-start.3 = (bf16[16,16,4608]{2,1,0:T(8,128)(2,1)}, bf16[16,16,4608]{2,1,0:T(8,128)(2,1)S(1)}, u32[]{:S(2)}) copy-start(bf16[16,16,4608]{2,1,0:T(8,128)(2,1)S(1)} %slice_dynamic-update-slice_fusion) | copy-start | bytes 7077892
  28.4 1.5 copy-start.4
  29.9 4.7 %copy-start.9 = (f32[256,512]{1,0:T(8,128)}, f32[256,512]{1,0:T(8,128)S(1)}, u32[]{:S(2)}) copy-start(f32[256,512]{1,0:T(8,128)S(1)} %fusion.3) | copy-start | bytes 1572868
  30.1 6.1 %collective-permute-start.3 = (bf16[4,16,256]{2,1,0:T(8,128)(2,1)S(1)}, bf16[4,16,256]{2,1,0:T(8,128)(2,1)S(1)}, u32[]{:S(2)}, u32[]{:S(2)}) collective-permute-start(bf16[4,16,256]{2,1,0:T(8,128)(2,1)S(1)} %pad_maximum_fusion.8), channel_id=1, source_target_pairs={{1,0},{2,1},{3,2},{4,3},{5,4},{6,5},{7,6},{8,7},{9,8},{10,9},{11,1... | collective-permute-start | bytes 98312 | tf_op jit(solution)/shard_map/ppermute | solution.py:15
  34.6 6.0 %collective-permute-start.2 = (bf16[4,16,256]{2,1,0:T(8,128)(2,1)S(1)}, bf16[4,16,256]{2,1,0:T(8,128)(2,1)S(1)}, u32[]{:S(2)}, u32[]{:S(2)}) collective-permute-start(bf16[4,16,256]{2,1,0:T(8,128)(2,1)S(1)} %pad_maximum_fusion.8), channel_id=1, source_target_pairs={{0,1},{1,2},{2,3},{3,4},{4,5},{5,6},{6,7},{7,8},{8,9},{9,10},{10,1... | collective-permute-start | bytes 98312 | tf_op jit(solution)/shard_map/ppermute | solution.py:14
  43.2 1.0 copy-start.10
  43.2 1.1 copy-start.17
  43.2 1.0 copy-start.21
  48.1 0.8 copy-start.19
  48.1 191.2 %reduce-scatter.3.cloned.1.call-start = ((), (), s32[]{:S(2)}) async-start(), calls=%async_computation.2 | async-start | bytes 10027008 | tf_op jit(solution)/shard_map/reduce_scatter | solution.py:148
  79.9 11.3 %copy-start.8 = (f32[16,16,1,512]{3,2,1,0:T(1,128)S(1)}, f32[16,16,1,512]{3,2,1,0:T(1,128)}, u32[]{:S(2)}) copy-start(f32[16,16,1,512]{3,2,1,0:T(1,128)} %get-tuple-element.430) | copy-start | bytes 1572868
  94.8 9.2 %copy-start.7 = (f32[16,16,1,512]{3,2,1,0:T(1,128)S(1)}, f32[16,16,1,512]{3,2,1,0:T(1,128)}, u32[]{:S(2)}) copy-start(f32[16,16,1,512]{3,2,1,0:T(1,128)} %get-tuple-element.427) | copy-start | bytes 1572868
  110.4 3.4 %collective-permute-start.5 = (bf16[4,16,512]{2,0,1:T(4,128)(2,1)S(1)}, bf16[4,16,512]{2,0,1:T(4,128)(2,1)S(1)}, u32[]{:S(2)}, u32[]{:S(2)}) collective-permute-start(bf16[4,16,512]{2,0,1:T(4,128)(2,1)S(1)} %pad_maximum_fusion.6), channel_id=1, source_target_pairs={{1,0},{2,1},{3,2},{4,3},{5,4},{6,5},{7,6},{8,7},{9,8},{10,9},{11,1... | collective-permute-start | bytes 196616 | tf_op jit(solution)/shard_map/ppermute | solution.py:15
  110.8 7.7 %collective-permute-start.4 = (bf16[4,16,512]{2,0,1:T(4,128)(2,1)S(1)}, bf16[4,16,512]{2,0,1:T(4,128)(2,1)S(1)}, u32[]{:S(2)}, u32[]{:S(2)}) collective-permute-start(bf16[4,16,512]{2,0,1:T(4,128)(2,1)S(1)} %pad_maximum_fusion.6), channel_id=1, source_target_pairs={{0,1},{1,2},{2,3},{3,4},{4,5},{5,6},{6,7},{7,8},{8,9},{9,10},{10,1... | collective-permute-start | bytes 196616 | tf_op jit(solution)/shard_map/ppermute | solution.py:14
  111.0 9.3 %copy-start.11 = (f32[256,512]{1,0:T(8,128)S(1)}, f32[256,512]{1,0:T(8,128)}, u32[]{:S(2)}) copy-start(f32[256,512]{1,0:T(8,128)} %copy-done.9) | copy-start | bytes 1572868
  120.3 7.6 %copy-start.5 = (f32[16,16,512]{2,1,0:T(8,128)}, f32[16,16,512]{2,1,0:T(8,128)S(1)}, u32[]{:S(2)}) copy-start(f32[16,16,512]{2,1,0:T(8,128)S(1)} %scatter-add.106) | copy-start | bytes 1572868
  170.7 9.3 %copy-start.6 = (f32[16,16,1,512]{3,2,1,0:T(1,128)S(1)}, f32[16,16,1,512]{3,2,1,0:T(1,128)}, u32[]{:S(2)}) copy-start(f32[16,16,1,512]{3,2,1,0:T(1,128)} %get-tuple-element.419) | copy-start | bytes 1572868
  187.2 4.7 %copy-start.14 = (bf16[1,16,512]{2,0,1:T(2,128)(2,1)}, bf16[1,16,512]{2,0,1:T(2,128)(2,1)S(1)}, u32[]{:S(2)}) copy-start(bf16[1,16,512]{2,0,1:T(2,128)(2,1)S(1)} %copy.202) | copy-start | bytes 49156
  187.3 4.6 %copy-start.15 = (bf16[1,16,512]{2,0,1:T(2,128)(2,1)}, bf16[1,16,512]{2,0,1:T(2,128)(2,1)S(1)}, u32[]{:S(2)}) copy-start(bf16[1,16,512]{2,0,1:T(2,128)(2,1)S(1)} %get-tuple-element.440) | copy-start | bytes 49156
  187.3 4.6 %copy-start.16 = (bf16[1,16,512]{2,0,1:T(2,128)(2,1)}, bf16[1,16,512]{2,0,1:T(2,128)(2,1)S(1)}, u32[]{:S(2)}) copy-start(bf16[1,16,512]{2,0,1:T(2,128)(2,1)S(1)} %get-tuple-element.441) | copy-start | bytes 49156
  187.5 4.4 %collective-permute-start.7 = (bf16[4,16,512]{2,0,1:T(4,128)(2,1)S(1)}, bf16[4,16,512]{2,0,1:T(4,128)(2,1)S(1)}, u32[]{:S(2)}, u32[]{:S(2)}) collective-permute-start(bf16[4,16,512]{2,0,1:T(4,128)(2,1)S(1)} %pad_maximum_fusion.7), channel_id=1, source_target_pairs={{1,0},{2,1},{3,2},{4,3},{5,4},{6,5},{7,6},{8,7},{9,8},{10,9},{11,1... | collective-permute-start | bytes 196616 | tf_op jit(solution)/shard_map/ppermute | solution.py:15
  188.6 8.1 %collective-permute-start.6 = (bf16[4,16,512]{2,0,1:T(4,128)(2,1)S(1)}, bf16[4,16,512]{2,0,1:T(4,128)(2,1)}, u32[]{:S(2)}, u32[]{:S(2)}) collective-permute-start(bf16[4,16,512]{2,0,1:T(4,128)(2,1)S(1)} %pad_maximum_fusion.7), channel_id=1, source_target_pairs={{0,1},{1,2},{2,3},{3,4},{4,5},{5,6},{6,7},{7,8},{8,9},{9,10},{10,1... | collective-permute-start | bytes 196616 | tf_op jit(solution)/shard_map/ppermute | solution.py:14
  192.0 0.6 copy-start.18
  196.7 42.6 %copy-start.1 = (bf16[4608,256]{1,0:T(8,128)(2,1)S(1)}, bf16[4608,256]{1,0:T(8,128)(2,1)}, u32[]{:S(2)}) copy-start(bf16[4608,256]{1,0:T(8,128)(2,1)} %param.83) | copy-start | bytes 7077892
  198.9 10.3 %copy-start.12 = (f32[256,256]{1,0:T(8,128)S(1)}, f32[256,256]{1,0:T(8,128)}, u32[]{:S(2)}) copy-start(f32[256,256]{1,0:T(8,128)} %get-tuple-element.436) | copy-start | bytes 786436
  199.3 0.7 copy-start.13
Sparse Core Ops, SparseCore 0:
  48.3 73.3 reduce-scatter.4
  128.0 111.2 reduce-scatter.2
where the time goes:
time: 248 us; the launch traced here: 246 us
  local copies, waits for them, and re-layouts  106 us (43%)
  waiting for transfers between devices  48.3 us (19%)
  other arithmetic  40.9 us (16%)
  matrix products  22 us (9%)
  between operations  17.1 us (7%)
  starting transfers between devices  11.9 us (5%)
    slice x2, local copies, waits for them, and re-layouts, unpatch(): dpatch[:, :, row_tap * 3 + col_tap]  34.9 us
    scatter-add x18, local copies, waits for them, and re-layouts, unpatch(): result.at[row_tap:row_tap + tile_side, col_tap:col_tap + tile_side]  34.4 us
    reduce_scatter x1, waiting for transfers between devices, shards(): lax.psum_scatter(contract(patch_gate, d_gate_pre), 'tile', scatter_dimens...  28.4 us
    add x14, other arithmetic, unpatch(): result.at[row_tap:row_tap + tile_side, col_tap:col_tap + tile_side]  18.9 us
    reshape x2, local copies, waits for them, and re-layouts, unpatch(): dpatch = dpatch.reshape(tile_side, tile_side, 9, channels)  14.4 us
    ppermute x4, waiting for transfers between devices, with_halo(): before = lax.ppermute(last, axis, up)  13.1 us
    ppermute x4, starting transfers between devices, with_halo(): after = lax.ppermute(initial, axis, down)  11.4 us
    dot_general x2, matrix products, contract(): jnp.einsum('ck,co->ko', patch_rows, grad_rows, preferred_element_type=jnp...  9.76 us
  transfers between devices with their start and end apart: 10, of which 7 were waited for; matrix products, arithmetic and copies ran while one was open for 62% of the time, Pallas kernels for 0%

commit v1 on v0

v1 whole, which is shorter than its diff:
```python
import functools

import jax
import jax.numpy as jnp
import numpy as np
from jax import lax
from jax.experimental import pallas as pl
from jax.experimental.pallas import tpu as pltpu
from jax.sharding import PartitionSpec as P

BF = jnp.bfloat16
F32 = jnp.float32


def dot(a, b):
    return jnp.dot(a, b, preferred_element_type=F32)


def dot_nt(a, b):
    return lax.dot_general(a, b, (((1,), (1,)), ((), ())), preferred_element_type=F32)


def dot_tn(a, b):
    return lax.dot_general(a, b, (((0,), (0,)), ((), ())), preferred_element_type=F32)


def call(body, outs, *args, flops=0, smem=(), mib=24):
    vmem = pl.BlockSpec(memory_space=pltpu.VMEM)
    in_specs = [pl.BlockSpec(memory_space=pltpu.SMEM) if i in smem else vmem for i in range(len(args))]
    size = sum(a.size * a.dtype.itemsize for a in args)
    size += sum(int(np.prod(s)) * jnp.dtype(d).itemsize for s, d in outs)
    return pl.pallas_call(
        body,
        out_shape=[jax.ShapeDtypeStruct(s, d) for s, d in outs],
        in_specs=in_specs,
        out_specs=[vmem] * len(outs),
        compiler_params=pltpu.CompilerParams(vmem_limit_bytes=mib * 2**20),
        cost_estimate=pl.CostEstimate(flops=int(flops), bytes_accessed=int(size), transcendentals=0),
    )(*args)


def frame_matrices(side):
    cells = side * side
    out = np.zeros((3, (side + 2) * side, cells + 4 * side), np.float32)
    for b in range(3):
        for r in range(side + 2):
            for j in range(side):
                c = j + b
                inner_r, inner_c = 1 <= r <= side, 1 <= c <= side
                if inner_r and inner_c:
                    src = (r - 1) * side + c - 1
                elif inner_c:
                    src = cells + (0 if r == 0 else 2) * side + c - 1
                elif inner_r:
                    src = cells + (3 if c == 0 else 1) * side + r - 1
                else:
                    continue
                out[b, r * side + j, src] = 1
    return out


def choose(index, values):
    out = jnp.full(index.shape, values[0], jnp.int32)
    for k in range(1, 4):
        out = jnp.where(index == k, values[k], out)
    return out


def edge_cell(edge, i, side):
    last = side - 1
    return jnp.where(
        edge == 0, i, jnp.where(edge == 1, i * side + last, jnp.where(edge == 2, last * side + i, i * side))
    )


def route_kernel(side, tiles, partner, flip, slot, x, h, send_next, send_prev, sel, place, turn, rim_sel):
    me = lax.axis_index("tile")
    after = jnp.where(me == tiles - 1, 0, me + 1)
    holder = lax.fori_loop(0, tiles, lambda t, a: a + jnp.where(slot[t] == me, t, 0), jnp.int32(0))
    q, fl, up = [], [], []
    for e in range(4):
        p = partner[holder, e]
        q.append(p & 3)
        fl.append(flip[holder, e])
        up.append((slot[p >> 2] == after).astype(jnp.int32))
    out_at, in_at = [], []
    for e in range(4):
        before = sum([jnp.where(up[o] == up[e], 1, 0) for o in range(e)], jnp.int32(0))
        lower = sum(
            [jnp.where((up[o] == up[e]) & (q[o] < q[e]), 1, 0) for o in range(4) if o != e], jnp.int32(0)
        )
        out_at.append(before + 2 * (1 - up[e]))
        in_at.append(lower + 2 * up[e])
    send_edge = [sum(jnp.where(out_at[e] == k, e, 0) for e in range(4)) for k in range(4)]
    recv_edge = [sum(jnp.where(in_at[e] == k, e, 0) for e in range(4)) for k in range(4)]
    recv_flip = [sum(jnp.where(in_at[e] == k, fl[e], 0) for e in range(4)) for k in range(4)]
    cells, rim = side * side, 4 * side

    def parts(shape, dim):
        at = lax.broadcasted_iota(jnp.int32, shape, dim)
        return at // side, at % side

    def one_hot(shape, dim, where_to):
        hit = lax.broadcasted_iota(jnp.int32, shape, dim) == where_to
        return jnp.where(hit, 1.0, 0.0).astype(BF)

    k, i = parts((rim, cells), 0)
    chosen = one_hot((rim, cells), 1, edge_cell(choose(k, send_edge), i, side))
    sel[...] = chosen
    for n, u in enumerate((x, h)):
        c = u.shape[1]
        picked = dot(chosen, u[...]).astype(BF)
        send_next[:, n * c : (n + 1) * c] = picked[: rim // 2]
        send_prev[:, n * c : (n + 1) * c] = picked[rim // 2 :]
    k, i = parts((cells, rim), 1)
    i = jnp.where(choose(k, recv_flip) == 1, side - 1 - i, i)
    place[...] = one_hot((cells, rim), 0, edge_cell(choose(k, recv_edge), i, side))
    k, i = parts((rim, rim), 1)
    i = jnp.where(choose(k, recv_flip) == 1, side - 1 - i, i)
    turn[...] = one_hot((rim, rim), 0, choose(k, recv_edge) * side + i)
    width = 2 * side + 2 * cells
    k, i = parts((rim, width), 0)
    e = choose(k, send_edge)
    at = jnp.where(
        e == 0,
        i,
        jnp.where(
            e == 2, side + i, jnp.where(e == 3, 2 * side + i * side, 2 * side + cells + i * side + side - 1)
        ),
    )
    rim_sel[...] = one_hot((rim, width), 1, at)


def frames(side, tile, strips, m0, m2, f):
    whole = jnp.concatenate([tile, strips], axis=0)
    f[0] = dot(m0[...], whole).astype(BF)
    f[1, :side] = strips[:side]
    f[1, side : side + side * side] = tile
    f[1, side + side * side :] = strips[2 * side : 3 * side]
    f[2] = dot(m2[...], whole).astype(BF)
    return whole


def conv(side, f, w, lo, hi):
    cells = side * side
    cols = [f[b, a * side : a * side + cells, :] for a in range(3) for b in range(3)]
    rows = [w[t, lo:hi, :] for t in range(9)]
    return dot(jnp.concatenate(cols, axis=1), jnp.concatenate(rows, axis=0))


def gate_kernel(side, x, h, rp, rn, turn, m0, m2, w, bias, sel, gate, rh, s_next, s_prev, f, whole):
    c = x.shape[1]
    rim = 4 * side
    strips = dot(turn[...], jnp.concatenate([rp[...], rn[...]], axis=0)).astype(BF)
    tile = jnp.concatenate([x[...], h[...]], axis=1)
    whole[...] = frames(side, tile, strips, m0, m2, f)
    act = jax.nn.sigmoid(conv(side, f, w, 0, 2 * c) + bias[...])
    gate[...] = act
    reset_h = (act[:, c:] * h[...].astype(F32)).astype(BF)
    rh[...] = reset_h
    picked = dot(sel[...], reset_h).astype(BF)
    s_next[...] = picked[: rim // 2]
    s_prev[...] = picked[rim // 2 :]


def cand_x_kernel(side, f, w, bias, out):
    c = w.shape[2]
    cells = side * side
    cols = [f[b, a * side : a * side + cells, :c] for a in range(3) for b in range(3)]
    rows = [w[t, :c, :] for t in range(9)]
    out[...] = dot(jnp.concatenate(cols, axis=1), jnp.concatenate(rows, axis=0)) + bias[...]


def cand_kernel(side, acc, rh, rp, rn, turn, m0, m2, w, gate, h, g, d, whole, f):
    c = rh.shape[1]
    strips = dot(turn[...], jnp.concatenate([rp[...], rn[...]], axis=0)).astype(BF)
    whole[...] = frames(side, rh[...], strips, m0, m2, f)
    candidate = jnp.tanh(acc[...] + conv(side, f, w, c, 2 * c))
    update = gate[:, :c]
    grad = g[...].astype(F32)
    d[:, :c] = (grad * update * (1.0 - candidate * candidate)).astype(BF)
    d[:, c:] = (grad * (candidate - h[...].astype(F32)) * update * (1.0 - update)).astype(BF)


def spread(side, acc, d, w, lo, hi, col_lo, col_hi, fresh):
    cells = side * side
    if fresh:
        acc[...] = jnp.zeros_like(acc)
    for a in range(3):
        for b in range(3):
            rows = slice(a * side, a * side + cells)
            acc[b, rows, :] += dot_nt(d, w[a * 3 + b, lo:hi, col_lo:col_hi])


def gather_frame(side, acc):
    cells, c = side * side, acc.shape[2]
    rows = (side + 2) * side
    col = lax.broadcasted_iota(jnp.int32, (rows, c), 0) % side
    left, right = acc[0], acc[2]
    total = acc[1]
    total += jnp.where(col == side - 1, 0.0, pltpu.roll(left, rows - 1, 0))
    total += jnp.where(col == 0, 0.0, pltpu.roll(right, 1, 0))
    rim = jnp.concatenate(
        [total[:side], total[side + cells :], left[side : side + cells], right[side : side + cells]], axis=0
    ).astype(BF)
    return total[side : side + cells], rim


def back_rh_kernel(side, d, w, rim_sel, inner, s_next, s_prev, acc):
    c = w.shape[2]
    rim = 4 * side
    spread(side, acc, d[:, :c], w, c, 2 * c, 0, c, True)
    own, edge = gather_frame(side, acc)
    inner[...] = own
    picked = dot(rim_sel[...], edge).astype(BF)
    s_next[...] = picked[: rim // 2]
    s_prev[...] = picked[rim // 2 :]


def back_early_kernel(side, d, wc, wg, acc):
    c = wc.shape[2]
    cells = side * side
    acc[...] = jnp.zeros_like(acc)
    for a in range(3):
        for b in range(3):
            rows = slice(a * side, a * side + cells)
            t = a * 3 + b
            acc[b, rows, :c] += dot_nt(d[:, :c], wc[t, :c, :]) + dot_nt(d[:, c:], wg[t, :c, :c])
            acc[b, rows, c:] += dot_nt(d[:, c:], wg[t, c:, :c])


def reset_kernel(side, inner, rp, rn, place, gate, h, g, d, direct):
    c = h.shape[1]
    d_rh = inner[...] + dot(place[...], jnp.concatenate([rp[...], rn[...]], axis=0))
    update, reset = gate[:, :c], gate[:, c:]
    d[...] = (d_rh * h[...].astype(F32) * reset * (1.0 - reset)).astype(BF)
    direct[...] = g[...].astype(F32) * (1.0 - update) + d_rh * reset


def back_gate_kernel(side, early, d, w, direct, rim_sel, inner, s_next, s_prev, acc):
    c = d.shape[1]
    rim = 4 * side
    acc[...] = early[...]
    spread(side, acc, d[...], w, 0, 2 * c, c, 2 * c, False)
    own, edge = gather_frame(side, acc)
    inner[:, :c] = own[:, :c]
    inner[:, c:] = own[:, c:] + direct[...]
    picked = dot(rim_sel[...], edge).astype(BF)
    s_next[...] = picked[: rim // 2]
    s_prev[...] = picked[rim // 2 :]


def final_kernel(inner, rp, rn, place, gx, gh):
    c = gx.shape[1]
    total = inner[...] + dot(place[...], jnp.concatenate([rp[...], rn[...]], axis=0))
    gx[...] = total[:, :c].astype(BF)
    gh[...] = total[:, c:].astype(BF)


def shards(
    x_tiles, h_tiles, grad_out, w_gate, b_gate, w_cand, b_cand, partner_edge, edge_flip, tile_slot
):
    side, c = x_tiles.shape[1], x_tiles.shape[3]
    tiles = lax.axis_size("tile")
    cells, rim = side * side, 4 * side
    half, band = rim // 2, (side + 2) * side
    x, h, g = (u.reshape(cells, c) for u in (x_tiles, h_tiles, grad_out))
    wg, wc = w_gate.reshape(9, 2 * c, 2 * c), w_cand.reshape(9, 2 * c, c)
    bg, bc = b_gate.reshape(1, 2 * c), b_cand.reshape(1, c)
    m = frame_matrices(side)
    m0, m2 = jnp.asarray(m[0], BF), jnp.asarray(m[2], BF)
    up = [(i, (i + 1) % tiles) for i in range(tiles)]
    down = [(j, i) for i, j in up]

    def exchange(s_next, s_prev):
        return lax.ppermute(s_next, "tile", up), lax.ppermute(s_prev, "tile", down)

    unit = 2 * cells * 9 * c * c
    with jax.named_scope("route"):
        s1n, s1p, sel, place, turn, rim_sel = call(
            functools.partial(route_kernel, side, tiles),
            [
                ((half, 2 * c), BF),
                ((half, 2 * c), BF),
                ((rim, cells), BF),
                ((cells, rim), BF),
                ((rim, rim), BF),
                ((rim, 2 * side + 2 * cells), BF),
            ],
            partner_edge, edge_flip, tile_slot, x, h, smem=(0, 1, 2),
        )
    r1p, r1n = exchange(s1n, s1p)
    with jax.named_scope("gate"):
        gate, rh, s2n, s2p, f, whole = call(
            functools.partial(gate_kernel, side),
            [
                ((cells, 2 * c), F32),
                ((cells, c), BF),
                ((half, c), BF),
                ((half, c), BF),
                ((3, band, 2 * c), BF),
                ((cells + rim, 2 * c), BF),
            ],
            x, h, r1p, r1n, turn, m0, m2, wg, bg, sel, flops=4 * unit,
        )
    r2p, r2n = exchange(s2n, s2p)
    with jax.named_scope("cand_x"):
        (acc_x,) = call(functools.partial(cand_x_kernel, side), [((cells, c), F32)], f, wc, bc, flops=unit)
    with jax.named_scope("cand"):
        d_cu, whole_rh, f_rh = call(
            functools.partial(cand_kernel, side),
            [((cells, 2 * c), BF), ((cells + rim, c), BF), ((3, band, c), BF)],
            acc_x, rh, r2p, r2n, turn, m0, m2, wc, gate, h, g, flops=unit,
        )
    with jax.named_scope("back_rh"):
        inner_rh, s3n, s3p, _ = call(
            functools.partial(back_rh_kernel, side),
            [((cells, c), F32), ((half, c), BF), ((half, c), BF), ((3, band, c), F32)],
            d_cu, wc, rim_sel, flops=unit,
        )
    r3p, r3n = exchange(s3n, s3p)
    with jax.named_scope("back_early"):
        (early,) = call(
            functools.partial(back_early_kernel, side), [((3, band, 2 * c), F32)], d_cu, wc, wg, flops=3 * unit
        )
    with jax.named_scope("reset"):
        d_r, direct = call(
            functools.partial(reset_kernel, side),
            [((cells, c), BF), ((cells, c), F32)],
            inner_rh, r3p, r3n, place, gate, h, g,
        )
    with jax.named_scope("back_gate"):
        inner, s4n, s4p, _ = call(
            functools.partial(back_gate_kernel, side),
            [((cells, 2 * c), F32), ((half, 2 * c), BF), ((half, 2 * c), BF), ((3, band, 2 * c), F32)],
            early, d_r, wg, direct, rim_sel, flops=2 * unit,
        )
    r4p, r4n = exchange(s4n, s4p)

    with jax.named_scope("weights"):
        def patch(u):
            return jnp.concatenate([u[b, a * side : a * side + cells] for a in range(3) for b in range(3)], axis=1)

        f_c = jnp.concatenate([f[:, :, :c], f_rh], axis=2)
        gwc = dot_tn(patch(f_c), d_cu[:, :c]).astype(BF)
        gwu = dot_tn(patch(f), d_cu[:, c:]).astype(BF)
        gwr = dot_tn(patch(f), d_r).astype(BF)
        first = lax.psum_scatter(
            jnp.concatenate([gwc, gwu], axis=1), "tile", scatter_dimension=0, tiled=True
        ).astype(F32)
        second = lax.psum_scatter(gwr, "tile", scatter_dimension=0, tiled=True).astype(F32)
        grad_w_cand = first[:, :c]
        grad_w_gate = jnp.concatenate([first[:, c:], second], axis=1)

    with jax.named_scope("final"):
        gx, gh = call(final_kernel, [((cells, c), BF), ((cells, c), BF)], inner, r4p, r4n, place)
    shape = (1, side, side, c)
    return gx.reshape(shape), gh.reshape(shape), grad_w_gate, grad_w_cand


def solution(mesh):
    tile = P(("grp", "tile"), None, None, None)
    rows = P(("grp", "tile"), None)
    return jax.shard_map(
        shards,
        mesh=mesh,
        in_specs=(tile, tile, tile) + (P(),) * 7,
        out_specs=(tile, tile, rows, rows),
        check_vma=False,
    )
```

time: 248 us -> 198 us (0.80)
  local copies, waits for them, and re-layouts: 106 us -> 27 us
  waiting for transfers between devices: 48.3 us -> 120 us
  other arithmetic: 40.9 us -> 2.74 us
  matrix products: 22 us -> 3.86 us
  Pallas kernels: 0 us -> 10.3 us
  starting transfers between devices: 11.9 us -> 19.1 us
  between operations: 17.1 us -> 14.4 us
    unnamed x2 -> x4, waiting for transfers between devices: 0.03 us -> 115 us
    scatter-add x26 -> x0, local copies, waits for them, and re-layouts: 40.2 us -> none  [the longest x18 34.4 us: unpatch(): result.at[row_tap:row_tap + tile_side, col_tap:col_tap + tile_side]]
    slice x13 -> x2, local copies, waits for them, and re-layouts: 36.1 us -> 1.1 us  [the longest x1 1.04 us: shards(): f_c = jnp.concatenate([f[:, :, :c], f_rh], axis=2)]
    reduce_scatter x2 -> x0, waiting for transfers between devices: 28.4 us -> none  [the longest x1 28.4 us: shards(): lax.psum_scatter(contract(patch_gate, d_gate_pre), 'tile', scatter_dimens...]
    add x20 -> x0, other arithmetic: 21.9 us -> none  [the longest x14 18.9 us: unpatch(): result.at[row_tap:row_tap + tile_side, col_tap:col_tap + tile_side]]
    unnamed x67 -> x57, local copies, waits for them, and re-layouts: 5.08 us -> 25.9 us
    dot_general x10 -> x3, matrix products: 22 us -> 3.86 us  [dot_tn(): lax.dot_general(a, b, (((0,), (0,)), ((), ())), preferred_element_type=F32)]
    ppermute x8, waiting for transfers between devices: 19.9 us -> 5.28 us  [the longest x4 5.1 us: exchange(): lax.ppermute(s_next, 'tile', up)]
  transfers between devices with their start and end apart: 10 -> 10, of which waited for: 7 -> 8; matrix products, arithmetic and copies ran while one was open for 62% -> 7% of each run, Pallas kernels for 0% -> 2%
where the time goes in v1:
time: 198 us; the launch traced here: 197 us
  waiting for transfers between devices  120 us (61%)
  local copies, waits for them, and re-layouts  27 us (14%)
  starting transfers between devices  19.1 us (10%)
  between operations  14.4 us (7%)
  Pallas kernels  10.3 us (5%)
  matrix products  3.86 us (2%)
  other arithmetic  2.74 us (1%)
    unnamed x4, waiting for transfers between devices  115 us
    unnamed x57, local copies, waits for them, and re-layouts  25.9 us
    ppermute x4, starting transfers between devices, exchange(): lax.ppermute(s_prev, 'tile', down)  18.4 us
    pallas_call x9, Pallas kernels, call(): pl.pallas_call(body, out_shape=[jax.ShapeDtypeStruct(s, d) for s, d in ou...  10.3 us
    ppermute x4, waiting for transfers between devices, exchange(): lax.ppermute(s_next, 'tile', up)  5.1 us
  transfers between devices with their start and end apart: 10, of which 8 were waited for; matrix products, arithmetic and copies ran while one was open for 7% of the time, Pallas kernels for 2%

profile of v1, /device:TPU:0, one launch (start us, length us, event | category | flops | bytes accessed | tf_op | source)
XLA Modules:
  0.0 197.5 jit_solution(6634882484756480432)
XLA Ops:
  8.7 0.9 copy-done.4
  9.6 0.9 copy-done.11
  11.2 1.2 route.1
  12.9 5.1 %collective-permute-start.1 = (bf16[32,512]{1,0:T(8,128)(2,1)S(1)}, bf16[32,512]{1,0:T(8,128)(2,1)S(1)}, u32[]{:S(2)}, u32[]{:S(2)}) collective-permute-start(bf16[32,512]{1,0:T(8,128)(2,1)S(1)} %get-tuple-element.28), channel_id=1, source_target_pairs={{1,0},{2,1},{3,2},{4,3},{5,4},{6,5},{7,6},{8,7},{9,8},{10,9},{11,1... | collective-permute-start | bytes 98312 | tf_op jit(solution)/shard_map/ppermute | solution.py:276
  17.9 1.5 collective-permute-done.rp
  19.5 2.3 %copy-done = bf16[4608,512]{1,0:T(8,128)(2,1)S(1)} copy-done((bf16[4608,512]{1,0:T(8,128)(2,1)S(1)}, bf16[4608,512]{1,0:T(8,128)(2,1)}, u32[]{:S(2)}) %copy-start) | copy-done | bytes 4718616
  21.9 0.9 copy-done.6
  22.8 0.9 copy-done.8
  24.4 1.9 gate.1
  26.4 4.5 %collective-permute-start.3 = (bf16[32,256]{1,0:T(8,128)(2,1)S(1)}, bf16[32,256]{1,0:T(8,128)(2,1)S(1)}, u32[]{:S(2)}, u32[]{:S(2)}) collective-permute-start(bf16[32,256]{1,0:T(8,128)(2,1)S(1)} %get-tuple-element.34), channel_id=1, source_target_pairs={{1,0},{2,1},{3,2},{4,3},{5,4},{6,5},{7,6},{8,7},{9,8},{10,9},{11,1... | collective-permute-start | bytes 49160 | tf_op jit(solution)/shard_map/ppermute | solution.py:276
  32.4 0.9 cand.1
  33.2 1.5 back_rh.1
  34.8 4.4 %collective-permute-start.5 = (bf16[32,256]{1,0:T(8,128)(2,1)S(1)}, bf16[32,256]{1,0:T(8,128)(2,1)S(1)}, u32[]{:S(2)}, u32[]{:S(2)}) collective-permute-start(bf16[32,256]{1,0:T(8,128)(2,1)S(1)} %get-tuple-element.40), channel_id=1, source_target_pairs={{1,0},{2,1},{3,2},{4,3},{5,4},{6,5},{7,6},{8,7},{9,8},{10,9},{11,1... | collective-permute-start | bytes 49160 | tf_op jit(solution)/shard_map/ppermute | solution.py:276
  39.2 1.4 collective-permute-done.4.rp
  41.6 2.2 %convolution_convert_fusion = bf16[4608,256]{1,0:T(8,128)(2,1)} fusion(bf16[256,4608]{1,0:T(8,128)(2,1)S(1)} %bitcast_dynamic-update-slice_fusion, bf16[256,256]{1,0:T(8,128)(2,1)S(1)} %get-tuple-element.42.d), kind=kOutput, calls=%fused_computation | convolution fusion | flops 605159424 | bytes 4849664 | tf_op jit(solution)/shard_map/weights/dot_general | solution.py:24
  43.8 1.0 slice.78
  45.1 1.5 copy-done.18
  48.4 2.5 %pad_maximum_fusion = bf16[4608,512]{0,1:T(8,128)(2,1)} fusion(bf16[4608,256]{0,1:T(8,128)(2,1)S(1)} %convolution_convert_fusion.1, bf16[4608,256]{0,1:T(8,128)(2,1)S(1)} %convolution_convert_fusion.2), kind=kLoop, calls=%fused_computation.3 | loop fusion | flops 9437184 | bytes 9437184 | tf_op jit(solution)/shard_map/weights/concatenate | solution.py:349
  50.8 6.7 %copy.26 = bf16[4608,512]{1,0:T(8,128)(2,1)} copy(bf16[4608,512]{0,1:T(8,128)(2,1)} %pad_maximum_fusion) | data formatting | bytes 9437184
  57.5 2.5 %copy-done.1 = bf16[4608,512]{1,0:T(8,128)(2,1)S(1)} copy-done((bf16[4608,512]{1,0:T(8,128)(2,1)S(1)}, bf16[4608,512]{1,0:T(8,128)(2,1)}, u32[]{:S(2)}) %copy-start.1) | copy-done | bytes 4718616
  60.1 1.1 back_early.1.early
  61.2 1.2 slice-done.1
  62.4 2.2 %back_gate.1 = (f32[256,512]{1,0:T(8,128)S(1)}, bf16[32,512]{1,0:T(8,128)(2,1)S(1)}, bf16[32,512]{1,0:T(8,128)(2,1)S(1)}, f32[3,288,512]{2,1,0:T(8,128)}) custom-call(f32[3,288,512]{2,1,0:T(8,128)S(1)} %back_early.1.early, bf16[256,256]{1,0:T(8,128)(2,1)S(1)} %get-tuple-element.42.d, bf16[9,512,512]{2,1,0:T(8,128)(2,1)S(1)} %bitcast.73, ...), custom_call_target="tpu_custom_call" | custom-call | flops 603979776 | bytes 9310208 | tf_op jit(solution)/shard_map/back_gate/pallas_call | solution.py:32
  64.6 4.4 %collective-permute-start.7 = (bf16[32,512]{1,0:T(8,128)(2,1)S(1)}, bf16[32,512]{1,0:T(8,128)(2,1)S(1)}, u32[]{:S(2)}, u32[]{:S(2)}) collective-permute-start(bf16[32,512]{1,0:T(8,128)(2,1)S(1)} %get-tuple-element.46), channel_id=1, source_target_pairs={{1,0},{2,1},{3,2},{4,3},{5,4},{6,5},{7,6},{8,7},{9,8},{10,9},{11,1... | collective-permute-start | bytes 98312 | tf_op jit(solution)/shard_map/ppermute | solution.py:276
  69.0 1.6 collective-permute-done.6.rp
  70.6 0.9 final.1
  71.5 36.9 %reduce-scatter.9.cloned.1.call-done = bf16[288,256]{1,0:T(8,128)(2,1)} async-done(((bf16[4608,256]{1,0:T(8,128)(2,1)}), bf16[288,256]{1,0:T(8,128)(2,1)}) %reduce-scatter.9.cloned.1.call-update) | async-done | bytes 147472
  108.4 1.1 copy.29
  109.6 77.9 %reduce-scatter.7.cloned.1.call-done = bf16[288,512]{1,0:T(8,128)(2,1)} async-done(((bf16[4608,512]{1,0:T(8,128)(2,1)}), bf16[288,512]{1,0:T(8,128)(2,1)}) %reduce-scatter.7.cloned.1.call-update) | async-done | bytes 294928
  187.4 1.2 copy.27
  188.7 1.1 copy.24
  189.8 0.9 copy.25
  (75 shorter events, 7.9 us)
Async XLA Ops:
  7.2 101.3 %reduce-scatter.9.cloned.1.call-start = ((), (), s32[]{:S(2)}) async-start(), calls=%async_computation.3 | async-start | bytes 2506752
  8.7 0.9 copy-start.4
  9.6 0.9 copy-start.11
  10.5 0.7 copy-start.16
  12.4 7.1 %collective-permute-start = (bf16[32,512]{1,0:T(8,128)(2,1)S(1)}, bf16[32,512]{1,0:T(8,128)(2,1)S(1)}, u32[]{:S(2)}, u32[]{:S(2)}) collective-permute-start(bf16[32,512]{1,0:T(8,128)(2,1)S(1)} %get-tuple-element.27), channel_id=1, source_target_pairs={{0,1},{1,2},{2,3},{3,4},{4,5},{5,6},{6,7},{7,8},{8,9},{9,10},{10,1... | collective-permute-start | bytes 98312 | tf_op jit(solution)/shard_map/ppermute | solution.py:276
  12.9 6.7 %collective-permute-start.1 = (bf16[32,512]{1,0:T(8,128)(2,1)S(1)}, bf16[32,512]{1,0:T(8,128)(2,1)S(1)}, u32[]{:S(2)}, u32[]{:S(2)}) collective-permute-start(bf16[32,512]{1,0:T(8,128)(2,1)S(1)} %get-tuple-element.28), channel_id=1, source_target_pairs={{1,0},{2,1},{3,2},{4,3},{5,4},{6,5},{7,6},{8,7},{9,8},{10,9},{11,1... | collective-permute-start | bytes 98312 | tf_op jit(solution)/shard_map/ppermute | solution.py:276
  19.5 2.3 %copy-start = (bf16[4608,512]{1,0:T(8,128)(2,1)S(1)}, bf16[4608,512]{1,0:T(8,128)(2,1)}, u32[]{:S(2)}) copy-start(bf16[4608,512]{1,0:T(8,128)(2,1)} %param.15) | copy-start | bytes 14155780
  21.9 0.9 copy-start.6
  22.8 0.9 copy-start.8
  23.7 0.7 copy-start.14
  26.3 12.9 %copy-start.3 = (bf16[3,288,512]{2,1,0:T(8,128)(2,1)}, bf16[3,288,512]{2,1,0:T(8,128)(2,1)S(1)}, u32[]{:S(2)}) copy-start(bf16[3,288,512]{2,1,0:T(8,128)(2,1)S(1)} %get-tuple-element.31.f) | copy-start | bytes 2654212
  26.3 4.8 %copy-start.2 = (bf16[4608,256]{1,0:T(8,128)(2,1)S(1)}, bf16[4608,256]{1,0:T(8,128)(2,1)}, u32[]{:S(2)}) copy-start(bf16[4608,256]{1,0:T(8,128)(2,1)} %param.17) | copy-start | bytes 7077892
  26.3 4.8 %copy-start.15 = (f32[256]{0:T(256)S(1)}, f32[256]{0:T(256)}, u32[]{:S(2)}) copy-start(f32[256]{0:T(256)} %param.18) | copy-start | bytes 3076
  26.3 5.9 %collective-permute-start.2 = (bf16[32,256]{1,0:T(8,128)(2,1)S(1)}, bf16[32,256]{1,0:T(8,128)(2,1)S(1)}, u32[]{:S(2)}, u32[]{:S(2)}) collective-permute-start(bf16[32,256]{1,0:T(8,128)(2,1)S(1)} %get-tuple-element.33), channel_id=1, source_target_pairs={{0,1},{1,2},{2,3},{3,4},{4,5},{5,6},{6,7},{7,8},{8,9},{9,10},{10,1... | collective-permute-start | bytes 49160 | tf_op jit(solution)/shard_map/ppermute | solution.py:276
  26.4 5.9 %collective-permute-start.3 = (bf16[32,256]{1,0:T(8,128)(2,1)S(1)}, bf16[32,256]{1,0:T(8,128)(2,1)S(1)}, u32[]{:S(2)}, u32[]{:S(2)}) collective-permute-start(bf16[32,256]{1,0:T(8,128)(2,1)S(1)} %get-tuple-element.34), channel_id=1, source_target_pairs={{1,0},{2,1},{3,2},{4,3},{5,4},{6,5},{7,6},{8,7},{9,8},{10,9},{11,1... | collective-permute-start | bytes 49160 | tf_op jit(solution)/shard_map/ppermute | solution.py:276
  31.1 1.3 copy-start.5
  31.1 1.3 copy-start.7
  31.1 1.3 copy-start.9
  31.1 1.3 copy-start.10
  34.7 5.9 %collective-permute-start.4 = (bf16[32,256]{1,0:T(8,128)(2,1)S(1)}, bf16[32,256]{1,0:T(8,128)(2,1)S(1)}, u32[]{:S(2)}, u32[]{:S(2)}) collective-permute-start(bf16[32,256]{1,0:T(8,128)(2,1)S(1)} %get-tuple-element.39), channel_id=1, source_target_pairs={{0,1},{1,2},{2,3},{3,4},{4,5},{5,6},{6,7},{7,8},{8,9},{9,10},{10,1... | collective-permute-start | bytes 49160 | tf_op jit(solution)/shard_map/ppermute | solution.py:276
  34.8 5.9 %collective-permute-start.5 = (bf16[32,256]{1,0:T(8,128)(2,1)S(1)}, bf16[32,256]{1,0:T(8,128)(2,1)S(1)}, u32[]{:S(2)}, u32[]{:S(2)}) collective-permute-start(bf16[32,256]{1,0:T(8,128)(2,1)S(1)} %get-tuple-element.40), channel_id=1, source_target_pairs={{1,0},{2,1},{3,2},{4,3},{5,4},{6,5},{7,6},{8,7},{9,8},{10,9},{11,1... | collective-permute-start | bytes 49160 | tf_op jit(solution)/shard_map/ppermute | solution.py:276
  39.2 2.3 %copy-start.17 = (bf16[256,4608]{1,0:T(8,128)(2,1)}, bf16[256,4608]{1,0:T(8,128)(2,1)S(1)}, u32[]{:S(2)}) copy-start(bf16[256,4608]{1,0:T(8,128)(2,1)S(1)} %bitcast_dynamic-update-slice_fusion) | copy-start | bytes 7077892
  40.9 0.7 copy-start.12
  43.8 143.6 %reduce-scatter.7.cloned.1.call-start = ((), (), s32[]{:S(2)}) async-start(), calls=%async_computation.2 | async-start | bytes 5013504
  45.0 1.7 copy-start.18
  57.5 3.7 %slice-start = ((s8[4718592]{0:T(1024)(128)(4,1)}), s8[524288]{0:T(1024)(128)(4,1)S(1)}, s32[]{:S(2)}) async-start(s8[4718592]{0:T(1024)(128)(4,1)} %bitcast.71), calls=%async_computation.4 | async-start | bytes 1048576
  57.5 2.5 %copy-start.1 = (bf16[4608,512]{1,0:T(8,128)(2,1)S(1)}, bf16[4608,512]{1,0:T(8,128)(2,1)}, u32[]{:S(2)}) copy-start(bf16[4608,512]{1,0:T(8,128)(2,1)} %param.15) | copy-start | bytes 14155780
  60.1 2.3 %slice-start.1 = ((s8[4718592]{0:T(1024)(128)(4,1)}), s8[4194304]{0:T(1024)(128)(4,1)S(1)}, s32[]{:S(2)}) async-start(s8[4718592]{0:T(1024)(128)(4,1)} %bitcast.71), calls=%async_computation.5 | async-start | bytes 8388608
  60.1 2.4 %copy-start.13 = (f32[256,256]{1,0:T(8,128)S(1)}, f32[256,256]{1,0:T(8,128)}, u32[]{:S(2)}) copy-start(f32[256,256]{1,0:T(8,128)} %copy-done.12) | copy-start | bytes 786436
  64.6 6.0 %collective-permute-start.6 = (bf16[32,512]{1,0:T(8,128)(2,1)S(1)}, bf16[32,512]{1,0:T(8,128)(2,1)S(1)}, u32[]{:S(2)}, u32[]{:S(2)}) collective-permute-start(bf16[32,512]{1,0:T(8,128)(2,1)S(1)} %get-tuple-element.45), channel_id=1, source_target_pairs={{0,1},{1,2},{2,3},{3,4},{4,5},{5,6},{6,7},{7,8},{8,9},{9,10},{10,1... | collective-permute-start | bytes 98312 | tf_op jit(solution)/shard_map/ppermute | solution.py:276
  64.6 6.0 %collective-permute-start.7 = (bf16[32,512]{1,0:T(8,128)(2,1)S(1)}, bf16[32,512]{1,0:T(8,128)(2,1)S(1)}, u32[]{:S(2)}, u32[]{:S(2)}) collective-permute-start(bf16[32,512]{1,0:T(8,128)(2,1)S(1)} %get-tuple-element.46), channel_id=1, source_target_pairs={{1,0},{2,1},{3,2},{4,3},{5,4},{6,5},{7,6},{8,7},{9,8},{10,9},{11,1... | collective-permute-start | bytes 98312 | tf_op jit(solution)/shard_map/ppermute | solution.py:276
Sparse Core Ops, SparseCore 0:
  43.9 64.4 reduce-scatter.8
  112.8 74.5 reduce-scatter.6

commit v2 on v1

--- a/solution.py
+++ b/solution.py
@@ -24,7 +24,7 @@
     return lax.dot_general(a, b, (((0,), (0,)), ((), ())), preferred_element_type=F32)
 
 
-def call(body, outs, *args, flops=0, smem=(), mib=24):
+def call(body, outs, *args, flops=0, smem=(), mib=24, scratch=()):
     vmem = pl.BlockSpec(memory_space=pltpu.VMEM)
     in_specs = [pl.BlockSpec(memory_space=pltpu.SMEM) if i in smem else vmem for i in range(len(args))]
     size = sum(a.size * a.dtype.itemsize for a in args)
@@ -34,6 +34,7 @@
         out_shape=[jax.ShapeDtypeStruct(s, d) for s, d in outs],
         in_specs=in_specs,
         out_specs=[vmem] * len(outs),
+        scratch_shapes=[pltpu.VMEM(s, d) for s, d in scratch],
         compiler_params=pltpu.CompilerParams(vmem_limit_bytes=mib * 2**20),
         cost_estimate=pl.CostEstimate(flops=int(flops), bytes_accessed=int(size), transcendentals=0),
     )(*args)
@@ -59,6 +60,12 @@
     return out
 
 
+def tap_matrices(side):
+    m, cells = frame_matrices(side), side * side
+    taps = [m[b, a * side : a * side + cells].T for a in range(3) for b in range(3)]
+    return np.stack(taps)
+
+
 def choose(index, values):
     out = jnp.full(index.shape, values[0], jnp.int32)
     for k in range(1, 4):
@@ -73,7 +80,7 @@
     )
 
 
-def route_kernel(side, tiles, partner, flip, slot, x, h, send_next, send_prev, sel, place, turn, rim_sel):
+def route_kernel(side, tiles, partner, flip, slot, x, h, xh, send_next, send_prev, sel, place, turn, rim_sel):
     me = lax.axis_index("tile")
     after = jnp.where(me == tiles - 1, 0, me + 1)
     holder = lax.fori_loop(0, tiles, lambda t, a: a + jnp.where(slot[t] == me, t, 0), jnp.int32(0))
@@ -112,6 +119,7 @@
         picked = dot(chosen, u[...]).astype(BF)
         send_next[:, n * c : (n + 1) * c] = picked[: rim // 2]
         send_prev[:, n * c : (n + 1) * c] = picked[rim // 2 :]
+        xh[:, n * c : (n + 1) * c] = u[...]
     k, i = parts((cells, rim), 1)
     i = jnp.where(choose(k, recv_flip) == 1, side - 1 - i, i)
     place[...] = one_hot((cells, rim), 0, edge_cell(choose(k, recv_edge), i, side))
@@ -138,7 +146,6 @@
     f[1, side : side + side * side] = tile
     f[1, side + side * side :] = strips[2 * side : 3 * side]
     f[2] = dot(m2[...], whole).astype(BF)
-    return whole
 
 
 def conv(side, f, w, lo, hi):
@@ -148,16 +155,17 @@
     return dot(jnp.concatenate(cols, axis=1), jnp.concatenate(rows, axis=0))
 
 
-def gate_kernel(side, x, h, rp, rn, turn, m0, m2, w, bias, sel, gate, rh, s_next, s_prev, f, whole):
-    c = x.shape[1]
-    rim = 4 * side
+def gate_kernel(side, xh, rp, rn, turn, m0, m2, w, bias, sel, gate, pack, s_next, s_prev, f):
+    c = xh.shape[1] // 2
+    cells, rim = side * side, 4 * side
     strips = dot(turn[...], jnp.concatenate([rp[...], rn[...]], axis=0)).astype(BF)
-    tile = jnp.concatenate([x[...], h[...]], axis=1)
-    whole[...] = frames(side, tile, strips, m0, m2, f)
+    frames(side, xh[...], strips, m0, m2, f)
     act = jax.nn.sigmoid(conv(side, f, w, 0, 2 * c) + bias[...])
     gate[...] = act
-    reset_h = (act[:, c:] * h[...].astype(F32)).astype(BF)
-    rh[...] = reset_h
+    reset_h = (act[:, c:] * xh[:, c:].astype(F32)).astype(BF)
+    pack[:cells] = reset_h
+    pack[cells : cells + rim] = strips[:, :c]
+    pack[cells + rim :] = strips[:, c:]
     picked = dot(sel[...], reset_h).astype(BF)
     s_next[...] = picked[: rim // 2]
     s_prev[...] = picked[rim // 2 :]
@@ -171,15 +179,18 @@
     out[...] = dot(jnp.concatenate(cols, axis=1), jnp.concatenate(rows, axis=0)) + bias[...]
 
 
-def cand_kernel(side, acc, rh, rp, rn, turn, m0, m2, w, gate, h, g, d, whole, f):
-    c = rh.shape[1]
+def cand_kernel(side, acc, pack, rp, rn, turn, m0, m2, w, gate, h, g, d, f):
+    c = h.shape[1]
+    cells, half = side * side, 2 * side
     strips = dot(turn[...], jnp.concatenate([rp[...], rn[...]], axis=0)).astype(BF)
-    whole[...] = frames(side, rh[...], strips, m0, m2, f)
+    frames(side, pack[:cells], strips, m0, m2, f)
+    d[cells:, :c] = strips[:half]
+    d[cells:, c:] = strips[half:]
     candidate = jnp.tanh(acc[...] + conv(side, f, w, c, 2 * c))
     update = gate[:, :c]
     grad = g[...].astype(F32)
-    d[:, :c] = (grad * update * (1.0 - candidate * candidate)).astype(BF)
-    d[:, c:] = (grad * (candidate - h[...].astype(F32)) * update * (1.0 - update)).astype(BF)
+    d[:cells, :c] = (grad * update * (1.0 - candidate * candidate)).astype(BF)
+    d[:cells, c:] = (grad * (candidate - h[...].astype(F32)) * update * (1.0 - update)).astype(BF)
 
 
 def spread(side, acc, d, w, lo, hi, col_lo, col_hi, fresh):
@@ -209,7 +220,7 @@
 def back_rh_kernel(side, d, w, rim_sel, inner, s_next, s_prev, acc):
     c = w.shape[2]
     rim = 4 * side
-    spread(side, acc, d[:, :c], w, c, 2 * c, 0, c, True)
+    spread(side, acc, d[: side * side, :c], w, c, 2 * c, 0, c, True)
     own, edge = gather_frame(side, acc)
     inner[...] = own
     picked = dot(rim_sel[...], edge).astype(BF)
@@ -225,8 +236,8 @@
         for b in range(3):
             rows = slice(a * side, a * side + cells)
             t = a * 3 + b
-            acc[b, rows, :c] += dot_nt(d[:, :c], wc[t, :c, :]) + dot_nt(d[:, c:], wg[t, :c, :c])
-            acc[b, rows, c:] += dot_nt(d[:, c:], wg[t, c:, :c])
+            acc[b, rows, :c] += dot_nt(d[:cells, :c], wc[t, :c, :]) + dot_nt(d[:cells, c:], wg[t, :c, :c])
+            acc[b, rows, c:] += dot_nt(d[:cells, c:], wg[t, c:, :c])
 
 
 def reset_kernel(side, inner, rp, rn, place, gate, h, g, d, direct):
@@ -257,6 +268,74 @@
     gh[...] = total[:, c:].astype(BF)
 
 
+def lhs_kernel(side, rows, tiles, cand, *refs):
+    xh, packs, ds = refs[:4], refs[4:8], refs[8:12]
+    taps, out, src = refs[-3:]
+    cells, rim, half = side * side, 4 * side, 2 * side
+    c = packs[0].shape[1]
+    per_tap = 2 * c // 128
+    for n in range(4):
+        lanes = slice(n * 128, (n + 1) * 128)
+        for k in range(per_tap):
+            at = slice(k * 128, (k + 1) * 128)
+            if k < per_tap // 2 or not cand:
+                src[k, :cells, lanes] = xh[n][:, at]
+                col = slice(at.start % c, at.start % c + 128)
+                first = cells if at.start < c else cells + rim
+                src[k, cells:, lanes] = packs[n][first : first + rim, col]
+            else:
+                col = slice(at.start - c, at.start - c + 128)
+                src[k, :cells, lanes] = packs[n][:cells, col]
+                src[k, cells : cells + half, lanes] = ds[n][cells:, col]
+                src[k, cells + half :, lanes] = ds[n][cells:, at]
+    me = lax.axis_index("tile")
+    for t in range(out.shape[0]):
+        target = me ^ (8 * (t // 2) + t % 2)
+        for n in range(out.shape[1] // 128):
+            block = jnp.minimum(target * rows // 128 + n, 9 * per_tap - 1)
+            part = dot_tn(src[block % per_tap], taps[block // per_tap]).astype(BF)
+            for k in range(4):
+                out[t, n * 128 : (n + 1) * 128, k * cells : (k + 1) * cells] = part[k * 128 : (k + 1) * 128]
+
+
+def weight_kernel(side, rows, n_lhs, *refs):
+    lhs, ds, (keep, send, acc) = refs[:n_lhs], refs[n_lhs : n_lhs + 4], refs[-3:]
+    cells = side * side
+    me = lax.axis_index("tile")
+    c = ds[0].shape[1] // n_lhs
+    right = jnp.concatenate([d[:cells] for d in ds], axis=0)
+    for t in range(lhs[0].shape[0]):
+        target = me ^ (8 * (t // 2) + t % 2)
+        first = pl.multiple_of(target * rows % 128, 8)
+        for k in range(n_lhs):
+            acc[t % 2, :, k * c : (k + 1) * c] = dot(lhs[k][t], right[:, k * c : (k + 1) * c])
+        part = acc[t % 2, pl.ds(first, rows), :]
+        if t % 2 == 0:
+            keep[t // 2] = part
+        else:
+            send[t // 2] = part.astype(BF)
+
+
+def pair_kernel(keep, got, own, far):
+    own[...] = keep[0] + got[0].astype(F32)
+    for m in range(1, keep.shape[0]):
+        far[m - 1] = (keep[m] + got[m].astype(F32)).astype(BF)
+
+
+def sum_kernel(n_far, *refs):
+    first, second, (cand, gate) = refs[: n_far + 1], refs[n_far + 1 : -2], refs[-2:]
+    c = cand.shape[1]
+    total = first[0][...]
+    for r in first[1:]:
+        total += r[...].astype(F32)
+    cand[...] = total[:, :c]
+    gate[:, :c] = total[:, c:]
+    total = second[0][...]
+    for r in second[1:]:
+        total += r[...].astype(F32)
+    gate[:, c:] = total
+
+
 def shards(
     x_tiles, h_tiles, grad_out, w_gate, b_gate, w_cand, b_cand, partner_edge, edge_flip, tile_slot
 ):
@@ -264,22 +343,33 @@
     tiles = lax.axis_size("tile")
     cells, rim = side * side, 4 * side
     half, band = rim // 2, (side + 2) * side
+    rows = 18 * c // tiles
+    groups = tiles // 8
+    blocks = max((rows * j + rows - 1) // 128 - rows * j // 128 + 1 for j in range(tiles)) * 128
     x, h, g = (u.reshape(cells, c) for u in (x_tiles, h_tiles, grad_out))
     wg, wc = w_gate.reshape(9, 2 * c, 2 * c), w_cand.reshape(9, 2 * c, c)
     bg, bc = b_gate.reshape(1, 2 * c), b_cand.reshape(1, c)
     m = frame_matrices(side)
     m0, m2 = jnp.asarray(m[0], BF), jnp.asarray(m[2], BF)
+    taps = jnp.asarray(tap_matrices(side), BF)
     up = [(i, (i + 1) % tiles) for i in range(tiles)]
     down = [(j, i) for i, j in up]
 
     def exchange(s_next, s_prev):
         return lax.ppermute(s_next, "tile", up), lax.ppermute(s_prev, "tile", down)
 
+    def swap(u, k):
+        return lax.ppermute(u, "tile", [(i, i ^ k) for i in range(tiles)])
+
+    def near(u):
+        return [u] + [swap(u, k) for k in (2, 4, 6)]
+
     unit = 2 * cells * 9 * c * c
     with jax.named_scope("route"):
-        s1n, s1p, sel, place, turn, rim_sel = call(
+        xh, s1n, s1p, sel, place, turn, rim_sel = call(
             functools.partial(route_kernel, side, tiles),
             [
+                ((cells, 2 * c), BF),
                 ((half, 2 * c), BF),
                 ((half, 2 * c), BF),
                 ((rim, cells), BF),
@@ -290,28 +380,30 @@
             partner_edge, edge_flip, tile_slot, x, h, smem=(0, 1, 2),
         )
     r1p, r1n = exchange(s1n, s1p)
+    xh_near = near(xh)
     with jax.named_scope("gate"):
-        gate, rh, s2n, s2p, f, whole = call(
+        gate, pack, s2n, s2p, f = call(
             functools.partial(gate_kernel, side),
             [
                 ((cells, 2 * c), F32),
-                ((cells, c), BF),
+                ((cells + 2 * rim, c), BF),
                 ((half, c), BF),
                 ((half, c), BF),
                 ((3, band, 2 * c), BF),
-                ((cells + rim, 2 * c), BF),
             ],
-            x, h, r1p, r1n, turn, m0, m2, wg, bg, sel, flops=4 * unit,
+            xh, r1p, r1n, turn, m0, m2, wg, bg, sel, flops=4 * unit,
         )
     r2p, r2n = exchange(s2n, s2p)
+    pack_near = near(pack)
     with jax.named_scope("cand_x"):
         (acc_x,) = call(functools.partial(cand_x_kernel, side), [((cells, c), F32)], f, wc, bc, flops=unit)
     with jax.named_scope("cand"):
-        d_cu, whole_rh, f_rh = call(
+        d_cu, _ = call(
             functools.partial(cand_kernel, side),
-            [((cells, 2 * c), BF), ((cells + rim, c), BF), ((3, band, c), BF)],
-            acc_x, rh, r2p, r2n, turn, m0, m2, wc, gate, h, g, flops=unit,
-        )
+            [((cells + half, 2 * c), BF), ((3, band, c), BF)],
+            acc_x, pack, r2p, r2n, turn, m0, m2, wc, gate, h, g, flops=unit,
+        )
+    d_near = near(d_cu)
     with jax.named_scope("back_rh"):
         inner_rh, s3n, s3p, _ = call(
             functools.partial(back_rh_kernel, side),
@@ -329,6 +421,7 @@
             [((cells, c), BF), ((cells, c), F32)],
             inner_rh, r3p, r3n, place, gate, h, g,
         )
+    r_near = near(d_r)
     with jax.named_scope("back_gate"):
         inner, s4n, s4p, _ = call(
             functools.partial(back_gate_kernel, side),
@@ -337,21 +430,43 @@
         )
     r4p, r4n = exchange(s4n, s4p)
 
-    with jax.named_scope("weights"):
-        def patch(u):
-            return jnp.concatenate([u[b, a * side : a * side + cells] for a in range(3) for b in range(3)], axis=1)
-
-        f_c = jnp.concatenate([f[:, :, :c], f_rh], axis=2)
-        gwc = dot_tn(patch(f_c), d_cu[:, :c]).astype(BF)
-        gwu = dot_tn(patch(f), d_cu[:, c:]).astype(BF)
-        gwr = dot_tn(patch(f), d_r).astype(BF)
-        first = lax.psum_scatter(
-            jnp.concatenate([gwc, gwu], axis=1), "tile", scatter_dimension=0, tiled=True
-        ).astype(F32)
-        second = lax.psum_scatter(gwr, "tile", scatter_dimension=0, tiled=True).astype(F32)
-        grad_w_cand = first[:, :c]
-        grad_w_gate = jnp.concatenate([first[:, c:], second], axis=1)
-
+    def lhs_of(cand, *args):
+        return call(
+            functools.partial(lhs_kernel, side, rows, tiles, cand),
+            [((2 * groups, blocks, 4 * cells), BF)],
+            *args, taps,
+            flops=2 * 2 * groups * blocks * 4 * cells * (cells + rim),
+            scratch=[((2 * c // 128, cells + rim, 512), BF)],
+        )[0]
+
+    def partial_sums(lhs, ds):
+        n = len(lhs)
+        keep, send = call(
+            functools.partial(weight_kernel, side, rows, n),
+            [((groups, rows, n * c), F32), ((groups, rows, n * c), BF)],
+            *lhs, *ds,
+            flops=2 * 2 * groups * blocks * 4 * cells * n * c,
+            scratch=[((2, blocks, n * c), F32)],
+        )
+        own, far = call(
+            pair_kernel, [((rows, n * c), F32), ((groups - 1, rows, n * c), BF)], keep, swap(send, 1)
+        )
+        return [own] + [swap(far[k - 1], 8 * k) for k in range(1, groups)]
+
+    with jax.named_scope("lhs_gate"):
+        lhs_gate = lhs_of(False, *xh_near, *pack_near)
+    with jax.named_scope("lhs_cand"):
+        lhs_cand = lhs_of(True, *xh_near, *pack_near, *d_near)
+    with jax.named_scope("weights_first"):
+        first = partial_sums([lhs_cand, lhs_gate], d_near)
+    with jax.named_scope("weights_second"):
+        second = partial_sums([lhs_gate], r_near)
+    with jax.named_scope("weights_sum"):
+        grad_w_cand, grad_w_gate = call(
+            functools.partial(sum_kernel, groups - 1),
+            [((rows, c), F32), ((rows, 2 * c), F32)],
+            *first, *second,
+        )
     with jax.named_scope("final"):
         gx, gh = call(final_kernel, [((cells, c), BF), ((cells, c), BF)], inner, r4p, r4n, place)
     shape = (1, side, side, c)

time: 198 us -> 108 us (0.55)
  waiting for transfers between devices: 120 us -> 48.6 us
  local copies, waits for them, and re-layouts: 27 us -> 8.91 us
  between operations: 14.4 us -> 0.84 us
  starting transfers between devices: 19.1 us -> 29.8 us
  Pallas kernels: 10.3 us -> 19 us
  matrix products: 3.86 us -> 0 us
  other arithmetic: 2.74 us -> 0.01 us
    unnamed x4 -> x0, waiting for transfers between devices: 115 us -> none
    ppermute x0 -> x16, waiting for transfers between devices: none -> 30.1 us  [swap(): return lax.ppermute(u, 'tile', [(i, i ^ k) for i in range(tiles)])]
    unnamed x57 -> x32, local copies, waits for them, and re-layouts: 25.9 us -> 8.91 us
    ppermute x0 -> x16, starting transfers between devices: none -> 15 us  [swap(): return lax.ppermute(u, 'tile', [(i, i ^ k) for i in range(tiles)])]
    ppermute x4, waiting for transfers between devices: 5.1 us -> 17 us  [exchange(): lax.ppermute(s_next, 'tile', up)]
    pallas_call x9 -> x16, Pallas kernels: 10.3 us -> 19 us  [call(): pl.pallas_call(body, out_shape=[jax.ShapeDtypeStruct(s, d) for s, d in ou...]
    ppermute x4, starting transfers between devices: 18.4 us -> 13.8 us  [exchange(): lax.ppermute(s_prev, 'tile', down)]
    dot_general x3 -> x0, matrix products: 3.86 us -> none  [dot_tn(): lax.dot_general(a, b, (((0,), (0,)), ((), ())), preferred_element_type=F32)]
  transfers between devices with their start and end apart: 10 -> 24, of which waited for: 8 -> 15; matrix products, arithmetic and copies ran while one was open for 7% -> 0% of each run, Pallas kernels for 2% -> 12%
where the time goes in v2:
time: 108 us; the launch traced here: 107 us
  waiting for transfers between devices  48.6 us (45%)
  starting transfers between devices  29.8 us (28%)
  Pallas kernels  19 us (18%)
  local copies, waits for them, and re-layouts  8.91 us (8%)
    ppermute x16, waiting for transfers between devices, swap(): return lax.ppermute(u, 'tile', [(i, i ^ k) for i in range(tiles)])  30.1 us
    pallas_call x16, Pallas kernels, call(): pl.pallas_call(body, out_shape=[jax.ShapeDtypeStruct(s, d) for s, d in ou...  19 us
    ppermute x4, waiting for transfers between devices, exchange(): lax.ppermute(s_next, 'tile', up)  17 us
    ppermute x16, starting transfers between devices, swap(): return lax.ppermute(u, 'tile', [(i, i ^ k) for i in range(tiles)])  15 us
    ppermute x4, starting transfers between devices, exchange(): lax.ppermute(s_prev, 'tile', down)  13.8 us
    unnamed x32, local copies, waits for them, and re-layouts  8.91 us
  transfers between devices with their start and end apart: 24, of which 15 were waited for; matrix products, arithmetic and copies ran while one was open for 0% of the time, Pallas kernels for 12%

profile of v2, /device:TPU:0, one launch (start us, length us, event | category | flops | bytes accessed | tf_op | source)
XLA Modules:
  0.0 107.2 jit_solution(10745811803912118749)
XLA Ops:
  4.6 1.2 %route.1 = (bf16[256,512]{1,0:T(8,128)(2,1)S(1)}, bf16[32,512]{1,0:T(8,128)(2,1)S(1)}, bf16[32,512]{1,0:T(8,128)(2,1)S(1)}, bf16[64,256]{1,0:T(8,128)(2,1)S(1)},...) custom-call(s32[16,4]{1,0:T(8,128)S(1)} %copy.17.partner, ...), custom_call_target="tpu_custom_call" | custom-call | bytes 733760 | tf_op jit(solution)/shard_map/route/pallas_call | solution.py:32
  6.3 5.1 %collective-permute-start.1 = (bf16[32,512]{1,0:T(8,128)(2,1)S(1)}, bf16[32,512]{1,0:T(8,128)(2,1)S(1)}, u32[]{:S(2)}, u32[]{:S(2)}) collective-permute-start(bf16[32,512]{1,0:T(8,128)(2,1)S(1)} %get-tuple-element.39), channel_id=1, source_target_pairs={{1,0},{2,1},{3,2},{4,3},{5,4},{6,5},{7,6},{8,7},{9,8},{10,9},{11,1... | collective-permute-start | bytes 98312 | tf_op jit(solution)/shard_map/ppermute | solution.py:359
  11.3 1.6 %collective-permute-done.rp = bf16[32,512]{1,0:T(8,128)(2,1)S(1)} collective-permute-done((bf16[32,512]{1,0:T(8,128)(2,1)S(1)}, bf16[32,512]{1,0:T(8,128)(2,1)S(1)}, u32[]{:S(2)}, u32[]{:S(2)}) %collective-permute-start) | collective-permute-done | bytes 32800 | tf_op jit(solution)/shard_map/ppermute | solution.py:359
  13.0 2.3 %copy-done = bf16[4608,512]{1,0:T(8,128)(2,1)S(1)} copy-done((bf16[4608,512]{1,0:T(8,128)(2,1)S(1)}, bf16[4608,512]{1,0:T(8,128)(2,1)}, u32[]{:S(2)}) %copy-start) | copy-done | bytes 4718616
  17.9 1.9 %gate.1 = (f32[256,512]{1,0:T(8,128)S(1)}, bf16[384,256]{1,0:T(8,128)(2,1)S(1)}, bf16[32,256]{1,0:T(8,128)(2,1)S(1)}, bf16[32,256]{1,0:T(8,128)(2,1)S(1)}, bf16[3,288,512]{2,1,0:T(8,128)(2,1)S(1)}) custom-call(bf16[256,512]{1,0:T(8,128)(2,1)S(1)} %get-tuple-element.37.xh.refs_0_, bf16[32,512]{1,0:T(8,128)(2,1)S(1)} %collective-permute-done.rp, ...), custom_call_target="tpu_custom_call" | custom-call | flops 1207959552 | bytes 7096320 | tf_op jit(solution)/shard_map/gate/pallas_call | solution.py:32
  20.7 2.6 %collective-permute-start.13 = (bf16[384,256]{1,0:T(8,128)(2,1)S(1)}, bf16[384,256]{1,0:T(8,128)(2,1)S(1)}, u32[]{:S(2)}, u32[]{:S(2)}) collective-permute-start(bf16[384,256]{1,0:T(8,128)(2,1)S(1)} %get-tuple-element.43.pack.refs_4_), channel_id=1, source_target_pairs={{0,6},{1,7},{2,4},{3,5},{4,2},{5,3},{6,0},{7,1},{8,14},{9,15},{10,... | collective-permute-start | bytes 589832 | tf_op jit(solution)/shard_map/ppermute | solution.py:362
  23.4 10.7 %collective-permute-done.2.rp = bf16[32,256]{1,0:T(8,128)(2,1)S(1)} collective-permute-done((bf16[32,256]{1,0:T(8,128)(2,1)S(1)}, bf16[32,256]{1,0:T(8,128)(2,1)S(1)}, u32[]{:S(2)}, u32[]{:S(2)}) %collective-permute-start.2) | collective-permute-done | bytes 16416 | tf_op jit(solution)/shard_map/ppermute | solution.py:359
  34.1 1.4 %collective-permute-done.3.rn = bf16[32,256]{1,0:T(8,128)(2,1)S(1)} collective-permute-done((bf16[32,256]{1,0:T(8,128)(2,1)S(1)}, bf16[32,256]{1,0:T(8,128)(2,1)S(1)}, u32[]{:S(2)}, u32[]{:S(2)}) %collective-permute-start.3) | collective-permute-done | bytes 16416 | tf_op jit(solution)/shard_map/ppermute | solution.py:359
  36.1 1.2 %cand.1 = (bf16[288,512]{1,0:T(8,128)(2,1)S(1)}, bf16[3,288,256]{2,1,0:T(8,128)(2,1)}) custom-call(f32[256,256]{1,0:T(8,128)S(1)} %cand_x.1.acc, bf16[384,256]{1,0:T(8,128)(2,1)S(1)} %get-tuple-element.43.pack.refs_4_, bf16[32,256]{1,0:T(8,128)(2,1)S(1)} %collective-permute-done.2.rp, bf16[32,256]{1,0:T(8,128)(2,1)S(1)} %collective-permute-done.3.rn, ...), custom_call_target="tpu_custom_call" | custom-call | flops 301989888 | bytes 4751360 | tf_op jit(solution)/shard_map/cand/pallas_call | solution.py:32
  37.3 3.5 %collective-permute-start.14 = (bf16[288,512]{1,0:T(8,128)(2,1)S(1)}, bf16[288,512]{1,0:T(8,128)(2,1)S(1)}, u32[]{:S(2)}, u32[]{:S(2)}) collective-permute-start(bf16[288,512]{1,0:T(8,128)(2,1)S(1)} %get-tuple-element.47.d.refs_8_.refs_2_), channel_id=1, source_target_pairs={{0,2},{1,3},{2,0},{3,1},{4,6},{5,7},{6,4},{7,5},{8,10},{9,11},{10,... | collective-permute-start | bytes 884744 | tf_op jit(solution)/shard_map/ppermute | solution.py:362
  40.7 1.5 %collective-permute-start.16 = (bf16[288,512]{1,0:T(8,128)(2,1)S(1)}, bf16[288,512]{1,0:T(8,128)(2,1)S(1)}, u32[]{:S(2)}, u32[]{:S(2)}) collective-permute-start(bf16[288,512]{1,0:T(8,128)(2,1)S(1)} %get-tuple-element.47.d.refs_8_.refs_2_), channel_id=1, source_target_pairs={{0,6},{1,7},{2,4},{3,5},{4,2},{5,3},{6,0},{7,1},{8,14},{9,15},{10,... | collective-permute-start | bytes 884744 | tf_op jit(solution)/shard_map/ppermute | solution.py:362
  42.3 2.4 %collective-permute-done.9.refs_2_ = bf16[256,512]{1,0:T(8,128)(2,1)S(1)} collective-permute-done((bf16[256,512]{1,0:T(8,128)(2,1)S(1)}, bf16[256,512]{1,0:T(8,128)(2,1)S(1)}, u32[]{:S(2)}, u32[]{:S(2)}) %collective-permute-start.9) | collective-permute-done | bytes 262176 | tf_op jit(solution)/shard_map/ppermute | solution.py:362
  44.7 3.1 %collective-permute-done.10.refs_3_ = bf16[256,512]{1,0:T(8,128)(2,1)S(1)} collective-permute-done((bf16[256,512]{1,0:T(8,128)(2,1)S(1)}, bf16[256,512]{1,0:T(8,128)(2,1)S(1)}, u32[]{:S(2)}, u32[]{:S(2)}) %collective-permute-start.10) | collective-permute-done | bytes 262176 | tf_op jit(solution)/shard_map/ppermute | solution.py:362
  47.9 2.1 %lhs_gate.1.refs_1_.refs_0_ = bf16[4,384,1024]{2,1,0:T(8,128)(2,1)S(1)} custom-call(bf16[256,512]{1,0:T(8,128)(2,1)S(1)} %get-tuple-element.37.xh.refs_0_, bf16[256,512]{1,0:T(8,128)(2,1)S(1)} %collective-permute-done.8.refs_1_, bf16[256,512]{1,0:T(8,128)(2,1)S(1)} %collective-permute-done.9.refs_2_, bf16[256,512]{1,0:T(8,128)(2,1)S(1)} %collective-permute-done.10.refs_3_, ...), custom_call_target="tpu_custom_call" | custom-call | flops 1006632960 | bytes 6455296 | tf_op jit(solution)/shard_map/lhs_gate/pallas_call | solution.py:32
  50.0 3.8 %collective-permute-done.14.refs_9_.refs_3_ = bf16[288,512]{1,0:T(8,128)(2,1)S(1)} collective-permute-done((bf16[288,512]{1,0:T(8,128)(2,1)S(1)}, bf16[288,512]{1,0:T(8,128)(2,1)S(1)}, u32[]{:S(2)}, u32[]{:S(2)}) %collective-permute-start.14) | collective-permute-done | bytes 294944 | tf_op jit(solution)/shard_map/ppermute | solution.py:362
  53.8 2.9 %collective-permute-done.15.refs_10_.refs_4_ = bf16[288,512]{1,0:T(8,128)(2,1)S(1)} collective-permute-done((bf16[288,512]{1,0:T(8,128)(2,1)S(1)}, bf16[288,512]{1,0:T(8,128)(2,1)S(1)}, u32[]{:S(2)}, u32[]{:S(2)}) %collective-permute-start.15) | collective-permute-done | bytes 294944 | tf_op jit(solution)/shard_map/ppermute | solution.py:362
  56.7 3.1 %collective-permute-done.16.refs_11_.refs_5_ = bf16[288,512]{1,0:T(8,128)(2,1)S(1)} collective-permute-done((bf16[288,512]{1,0:T(8,128)(2,1)S(1)}, bf16[288,512]{1,0:T(8,128)(2,1)S(1)}, u32[]{:S(2)}, u32[]{:S(2)}) %collective-permute-start.16) | collective-permute-done | bytes 294944 | tf_op jit(solution)/shard_map/ppermute | solution.py:362
  59.8 2.1 %lhs_cand.1.refs_0_ = bf16[4,384,1024]{2,1,0:T(8,128)(2,1)S(1)} custom-call(bf16[256,512]{1,0:T(8,128)(2,1)S(1)} %get-tuple-element.37.xh.refs_0_, bf16[256,512]{1,0:T(8,128)(2,1)S(1)} %collective-permute-done.8.refs_1_, bf16[256,512]{1,0:T(8,128)(2,1)S(1)} %collective-permute-done.9.refs_2_, bf16[256,512]{1,0:T(8,128)(2,1)S(1)} %collective-permute-done.10.refs_3_, ...), custom_call_target="tpu_custom_call" | custom-call | flops 1006632960 | bytes 7634944 | tf_op jit(solution)/shard_map/lhs_cand/pallas_call | solution.py:32
  61.9 1.9 %weights_first.2 = (f32[2,288,512]{2,1,0:T(8,128)S(1)}, bf16[2,288,512]{2,1,0:T(8,128)(2,1)S(1)}) custom-call(bf16[4,384,1024]{2,1,0:T(8,128)(2,1)S(1)} %lhs_cand.1.refs_0_, bf16[4,384,1024]{2,1,0:T(8,128)(2,1)S(1)} %lhs_gate.1.refs_1_.refs_0_, bf16[288,512]{1,0:T(8,128)(2,1)S(1)} %get-tuple-element.47.d.refs_8_.refs_2_, ...), custom_call_target="tpu_custom_call" | custom-call | flops 1610612736 | bytes 9240576 | tf_op jit(solution)/shard_map/weights_first/pallas_call | solution.py:32
  63.9 1.5 %back_rh.1 = (f32[256,256]{1,0:T(8,128)S(1)}, bf16[32,256]{1,0:T(8,128)(2,1)S(1)}, bf16[32,256]{1,0:T(8,128)(2,1)S(1)}, f32[3,288,256]{2,1,0:T(8,128)}) custom-call(bf16[288,512]{1,0:T(8,128)(2,1)S(1)} %get-tuple-element.47.d.refs_8_.refs_2_, bf16[9,512,256]{2,1,0:T(8,128)(2,1)S(1)} %bitcast.18, bf16[64,544]{1,0:T(8,128)(2,1)S(1)} %get-tuple-element.48.rim_sel), custom_call_target="tpu_custom_call" | custom-call | flops 301989888 | bytes 3903488 | tf_op jit(solution)/shard_map/back_rh/pallas_call | solution.py:32
  65.9 4.3 %collective-permute-start.5 = (bf16[32,256]{1,0:T(8,128)(2,1)S(1)}, bf16[32,256]{1,0:T(8,128)(2,1)S(1)}, u32[]{:S(2)}, u32[]{:S(2)}) collective-permute-start(bf16[32,256]{1,0:T(8,128)(2,1)S(1)} %get-tuple-element.51), channel_id=1, source_target_pairs={{1,0},{2,1},{3,2},{4,3},{5,4},{6,5},{7,6},{8,7},{9,8},{10,9},{11,1... | collective-permute-start | bytes 49160 | tf_op jit(solution)/shard_map/ppermute | solution.py:359
  70.2 1.4 %collective-permute-done.4.rp = bf16[32,256]{1,0:T(8,128)(2,1)S(1)} collective-permute-done((bf16[32,256]{1,0:T(8,128)(2,1)S(1)}, bf16[32,256]{1,0:T(8,128)(2,1)S(1)}, u32[]{:S(2)}, u32[]{:S(2)}) %collective-permute-start.4) | collective-permute-done | bytes 16416 | tf_op jit(solution)/shard_map/ppermute | solution.py:359
  72.8 2.7 %collective-permute-start.21 = (bf16[256,256]{1,0:T(8,128)(2,1)S(1)}, bf16[256,256]{1,0:T(8,128)(2,1)S(1)}, u32[]{:S(2)}, u32[]{:S(2)}) collective-permute-start(bf16[256,256]{1,0:T(8,128)(2,1)S(1)} %get-tuple-element.53.d.refs_1_), channel_id=1, source_target_pairs={{0,6},{1,7},{2,4},{3,5},{4,2},{5,3},{6,0},{7,1},{8,14},{9,15},{10,... | collective-permute-start | bytes 393224 | tf_op jit(solution)/shard_map/ppermute | solution.py:362
  75.5 2.6 %collective-permute-done.19.refs_2_ = bf16[256,256]{1,0:T(8,128)(2,1)S(1)} collective-permute-done((bf16[256,256]{1,0:T(8,128)(2,1)S(1)}, bf16[256,256]{1,0:T(8,128)(2,1)S(1)}, u32[]{:S(2)}, u32[]{:S(2)}) %collective-permute-start.19) | collective-permute-done | bytes 131104 | tf_op jit(solution)/shard_map/ppermute | solution.py:362
  78.8 3.2 %collective-permute-done.21.refs_4_ = bf16[256,256]{1,0:T(8,128)(2,1)S(1)} collective-permute-done((bf16[256,256]{1,0:T(8,128)(2,1)S(1)}, bf16[256,256]{1,0:T(8,128)(2,1)S(1)}, u32[]{:S(2)}, u32[]{:S(2)}) %collective-permute-start.21) | collective-permute-done | bytes 131104 | tf_op jit(solution)/shard_map/ppermute | solution.py:362
  83.3 1.1 %collective-permute-start.18 = (bf16[288,512]{1,0:T(8,128)(2,1)S(1)}, bf16[288,512]{1,0:T(8,128)(2,1)S(1)}, u32[]{:S(2)}, u32[]{:S(2)}) collective-permute-start(bf16[288,512]{1,0:T(8,128)(2,1)S(1)} %bitcast.28), channel_id=1, source_target_pairs={{0,8},{1,9},{2,10},{3,11},{4,12},{5,13},{6,14},{7,15},{8,0},{9,1},... | collective-permute-start | bytes 884744 | tf_op jit(solution)/shard_map/weights_first/ppermute | solution.py:362
  84.8 1.6 %collective-permute-start.23 = (bf16[288,256]{1,0:T(8,128)(2,1)S(1)}, bf16[288,256]{1,0:T(8,128)(2,1)S(1)}, u32[]{:S(2)}, u32[]{:S(2)}) collective-permute-start(bf16[288,256]{1,0:T(8,128)(2,1)S(1)} %bitcast.29), channel_id=1, source_target_pairs={{0,8},{1,9},{2,10},{3,11},{4,12},{5,13},{6,14},{7,15},{8,0},{9,1},... | collective-permute-start | bytes 442376 | tf_op jit(solution)/shard_map/weights_second/ppermute | solution.py:362
  86.4 1.1 %back_early.1.early = f32[3,288,512]{2,1,0:T(8,128)S(1)} custom-call(bf16[288,512]{1,0:T(8,128)(2,1)S(1)} %get-tuple-element.47.d.refs_8_.refs_2_, bf16[9,512,256]{2,1,0:T(8,128)(2,1)S(1)} %bitcast.19, bf16[9,512,512]{2,1,0:T(8,128)(2,1)S(1)} %bitcast.14), custom_call_target="tpu_custom_call" | custom-call | flops 905969664 | bytes 9142272 | tf_op jit(solution)/shard_map/back_early/pallas_call | solution.py:32
  87.6 2.2 %back_gate.1 = (f32[256,512]{1,0:T(8,128)S(1)}, bf16[32,512]{1,0:T(8,128)(2,1)S(1)}, bf16[32,512]{1,0:T(8,128)(2,1)S(1)}, f32[3,288,512]{2,1,0:T(8,128)}) custom-call(f32[3,288,512]{2,1,0:T(8,128)S(1)} %back_early.1.early, bf16[256,256]{1,0:T(8,128)(2,1)S(1)} %get-tuple-element.53.d.refs_1_, bf16[9,512,512]{2,1,0:T(8,128)(2,1)S(1)} %bitcast.15, ...), custom_call_target="tpu_custom_call" | custom-call | flops 603979776 | bytes 9310208 | tf_op jit(solution)/shard_map/back_gate/pallas_call | solution.py:32
  89.7 4.4 %collective-permute-start.7 = (bf16[32,512]{1,0:T(8,128)(2,1)S(1)}, bf16[32,512]{1,0:T(8,128)(2,1)S(1)}, u32[]{:S(2)}, u32[]{:S(2)}) collective-permute-start(bf16[32,512]{1,0:T(8,128)(2,1)S(1)} %get-tuple-element.57), channel_id=1, source_target_pairs={{1,0},{2,1},{3,2},{4,3},{5,4},{6,5},{7,6},{8,7},{9,8},{10,9},{11,1... | collective-permute-start | bytes 98312 | tf_op jit(solution)/shard_map/ppermute | solution.py:359
  94.2 3.2 %collective-permute-done.6.rp = bf16[32,512]{1,0:T(8,128)(2,1)S(1)} collective-permute-done((bf16[32,512]{1,0:T(8,128)(2,1)S(1)}, bf16[32,512]{1,0:T(8,128)(2,1)S(1)}, u32[]{:S(2)}, u32[]{:S(2)}) %collective-permute-start.6) | collective-permute-done | bytes 32800 | tf_op jit(solution)/shard_map/ppermute | solution.py:359
  98.3 7.9 %collective-permute-done.23.refs_3_ = bf16[288,256]{1,0:T(8,128)(2,1)S(1)} collective-permute-done((bf16[288,256]{1,0:T(8,128)(2,1)S(1)}, bf16[288,256]{1,0:T(8,128)(2,1)S(1)}, u32[]{:S(2)}, u32[]{:S(2)}) %collective-permute-start.23) | collective-permute-done | bytes 147488 | tf_op jit(solution)/shard_map/weights_second/ppermute | solution.py:362
  (65 shorter events, 14.5 us)
Async XLA Ops:
  5.8 7.2 %collective-permute-start = (bf16[32,512]{1,0:T(8,128)(2,1)S(1)}, bf16[32,512]{1,0:T(8,128)(2,1)S(1)}, u32[]{:S(2)}, u32[]{:S(2)}) collective-permute-start(bf16[32,512]{1,0:T(8,128)(2,1)S(1)} %get-tuple-element.38), channel_id=1, source_target_pairs={{0,1},{1,2},{2,3},{3,4},{4,5},{5,6},{6,7},{7,8},{8,9},{9,10},{10,1... | collective-permute-start | bytes 98312 | tf_op jit(solution)/shard_map/ppermute | solution.py:359
  6.3 6.7 %collective-permute-start.1 = (bf16[32,512]{1,0:T(8,128)(2,1)S(1)}, bf16[32,512]{1,0:T(8,128)(2,1)S(1)}, u32[]{:S(2)}, u32[]{:S(2)}) collective-permute-start(bf16[32,512]{1,0:T(8,128)(2,1)S(1)} %get-tuple-element.39), channel_id=1, source_target_pairs={{1,0},{2,1},{3,2},{4,3},{5,4},{6,5},{7,6},{8,7},{9,8},{10,9},{11,1... | collective-permute-start | bytes 98312 | tf_op jit(solution)/shard_map/ppermute | solution.py:359
  11.3 29.4 %collective-permute-start.8 = (bf16[256,512]{1,0:T(8,128)(2,1)S(1)}, bf16[256,512]{1,0:T(8,128)(2,1)S(1)}, u32[]{:S(2)}, u32[]{:S(2)}) collective-permute-start(bf16[256,512]{1,0:T(8,128)(2,1)S(1)} %get-tuple-element.37.xh.refs_0_), channel_id=1, source_target_pairs={{0,2},{1,3},{2,0},{3,1},{4,6},{5,7},{6,4},{7,5},{8,10},{9,11},{10,... | collective-permute-start | bytes 786440 | tf_op jit(solution)/shard_map/ppermute | solution.py:362
  17.9 17.7 %copy-start.1 = (bf16[4608,256]{1,0:T(8,128)(2,1)S(1)}, bf16[4608,256]{1,0:T(8,128)(2,1)}, u32[]{:S(2)}) copy-start(bf16[4608,256]{1,0:T(8,128)(2,1)} %param.18) | copy-start | bytes 7077892
  17.9 17.7 %copy-start.11 = (f32[256]{0:T(256)S(1)}, f32[256]{0:T(256)}, u32[]{:S(2)}) copy-start(f32[256]{0:T(256)} %param.19) | copy-start | bytes 3076
  19.8 16.3 %copy-start.4 = (bf16[1,16,16,256]{3,2,1,0:T(8,128)(2,1)S(1)}, bf16[1,16,16,256]{3,2,1,0:T(8,128)(2,1)}, u32[]{:S(2)}) copy-start(bf16[1,16,16,256]{3,2,1,0:T(8,128)(2,1)} %param.14) | copy-start | bytes 393220
  19.8 16.3 %copy-start.6 = (bf16[288,320]{1,0:T(8,128)(2,1)S(1)}, bf16[288,320]{1,0:T(8,128)(2,1)}, u32[]{:S(2)}) copy-start(bf16[288,320]{1,0:T(8,128)(2,1)} %constant.6.clone.m0) | copy-start | bytes 552964
  19.8 16.3 %copy-start.8 = (bf16[1,16,16,256]{3,2,1,0:T(8,128)(2,1)S(1)}, bf16[1,16,16,256]{3,2,1,0:T(8,128)(2,1)}, u32[]{:S(2)}) copy-start(bf16[1,16,16,256]{3,2,1,0:T(8,128)(2,1)} %param.15) | copy-start | bytes 393220
  19.8 15.8 %collective-permute-start.11 = (bf16[384,256]{1,0:T(8,128)(2,1)S(1)}, bf16[384,256]{1,0:T(8,128)(2,1)S(1)}, u32[]{:S(2)}, u32[]{:S(2)}) collective-permute-start(bf16[384,256]{1,0:T(8,128)(2,1)S(1)} %get-tuple-element.43.pack.refs_4_), channel_id=1, source_target_pairs={{0,2},{1,3},{2,0},{3,1},{4,6},{5,7},{6,4},{7,5},{8,10},{9,11},{10,... | collective-permute-start | bytes 589832 | tf_op jit(solution)/shard_map/ppermute | solution.py:362
  20.2 17.0 %collective-permute-start.12 = (bf16[384,256]{1,0:T(8,128)(2,1)S(1)}, bf16[384,256]{1,0:T(8,128)(2,1)S(1)}, u32[]{:S(2)}, u32[]{:S(2)}) collective-permute-start(bf16[384,256]{1,0:T(8,128)(2,1)S(1)} %get-tuple-element.43.pack.refs_4_), channel_id=1, source_target_pairs={{0,4},{1,5},{2,6},{3,7},{4,0},{5,1},{6,2},{7,3},{8,12},{9,13},{10,... | collective-permute-start | bytes 589832 | tf_op jit(solution)/shard_map/ppermute | solution.py:362
  20.7 20.0 %collective-permute-start.13 = (bf16[384,256]{1,0:T(8,128)(2,1)S(1)}, bf16[384,256]{1,0:T(8,128)(2,1)S(1)}, u32[]{:S(2)}, u32[]{:S(2)}) collective-permute-start(bf16[384,256]{1,0:T(8,128)(2,1)S(1)} %get-tuple-element.43.pack.refs_4_), channel_id=1, source_target_pairs={{0,6},{1,7},{2,4},{3,5},{4,2},{5,3},{6,0},{7,1},{8,14},{9,15},{10,... | collective-permute-start | bytes 589832 | tf_op jit(solution)/shard_map/ppermute | solution.py:362
  23.4 10.7 %collective-permute-start.2 = (bf16[32,256]{1,0:T(8,128)(2,1)S(1)}, bf16[32,256]{1,0:T(8,128)(2,1)S(1)}, u32[]{:S(2)}, u32[]{:S(2)}) collective-permute-start(bf16[32,256]{1,0:T(8,128)(2,1)S(1)} %get-tuple-element.44), channel_id=1, source_target_pairs={{0,1},{1,2},{2,3},{3,4},{4,5},{5,6},{6,7},{7,8},{8,9},{9,10},{10,1... | collective-permute-start | bytes 49160 | tf_op jit(solution)/shard_map/ppermute | solution.py:359
  34.1 1.4 %collective-permute-start.3 = (bf16[32,256]{1,0:T(8,128)(2,1)S(1)}, bf16[32,256]{1,0:T(8,128)(2,1)S(1)}, u32[]{:S(2)}, u32[]{:S(2)}) collective-permute-start(bf16[32,256]{1,0:T(8,128)(2,1)S(1)} %get-tuple-element.45), channel_id=1, source_target_pairs={{1,0},{2,1},{3,2},{4,3},{5,4},{6,5},{7,6},{8,7},{9,8},{10,9},{11,1... | collective-permute-start | bytes 49160 | tf_op jit(solution)/shard_map/ppermute | solution.py:359
  35.5 9.2 %collective-permute-start.9 = (bf16[256,512]{1,0:T(8,128)(2,1)S(1)}, bf16[256,512]{1,0:T(8,128)(2,1)S(1)}, u32[]{:S(2)}, u32[]{:S(2)}) collective-permute-start(bf16[256,512]{1,0:T(8,128)(2,1)S(1)} %get-tuple-element.37.xh.refs_0_), channel_id=1, source_target_pairs={{0,4},{1,5},{2,6},{3,7},{4,0},{5,1},{6,2},{7,3},{8,12},{9,13},{10,... | collective-permute-start | bytes 786440 | tf_op jit(solution)/shard_map/ppermute | solution.py:362
  35.5 12.3 %collective-permute-start.10 = (bf16[256,512]{1,0:T(8,128)(2,1)S(1)}, bf16[256,512]{1,0:T(8,128)(2,1)S(1)}, u32[]{:S(2)}, u32[]{:S(2)}) collective-permute-start(bf16[256,512]{1,0:T(8,128)(2,1)S(1)} %get-tuple-element.37.xh.refs_0_), channel_id=1, source_target_pairs={{0,6},{1,7},{2,4},{3,5},{4,2},{5,3},{6,0},{7,1},{8,14},{9,15},{10,... | collective-permute-start | bytes 786440 | tf_op jit(solution)/shard_map/ppermute | solution.py:362
  36.1 11.8 %copy-start.2 = (bf16[9,320,256]{2,1,0:T(8,128)(2,1)S(1)}, bf16[9,320,256]{2,1,0:T(8,128)(2,1)}, u32[]{:S(2)}) copy-start(bf16[9,320,256]{2,1,0:T(8,128)(2,1)} %constant.8.clone.refs_12_.refs_8_) | copy-start | bytes 4423684
  37.3 16.5 %collective-permute-start.14 = (bf16[288,512]{1,0:T(8,128)(2,1)S(1)}, bf16[288,512]{1,0:T(8,128)(2,1)S(1)}, u32[]{:S(2)}, u32[]{:S(2)}) collective-permute-start(bf16[288,512]{1,0:T(8,128)(2,1)S(1)} %get-tuple-element.47.d.refs_8_.refs_2_), channel_id=1, source_target_pairs={{0,2},{1,3},{2,0},{3,1},{4,6},{5,7},{6,4},{7,5},{8,10},{9,11},{10,... | collective-permute-start | bytes 884744 | tf_op jit(solution)/shard_map/ppermute | solution.py:362
  40.7 16.0 %collective-permute-start.15 = (bf16[288,512]{1,0:T(8,128)(2,1)S(1)}, bf16[288,512]{1,0:T(8,128)(2,1)S(1)}, u32[]{:S(2)}, u32[]{:S(2)}) collective-permute-start(bf16[288,512]{1,0:T(8,128)(2,1)S(1)} %get-tuple-element.47.d.refs_8_.refs_2_), channel_id=1, source_target_pairs={{0,4},{1,5},{2,6},{3,7},{4,0},{5,1},{6,2},{7,3},{8,12},{9,13},{10,... | collective-permute-start | bytes 884744 | tf_op jit(solution)/shard_map/ppermute | solution.py:362
  40.7 19.0 %collective-permute-start.16 = (bf16[288,512]{1,0:T(8,128)(2,1)S(1)}, bf16[288,512]{1,0:T(8,128)(2,1)S(1)}, u32[]{:S(2)}, u32[]{:S(2)}) collective-permute-start(bf16[288,512]{1,0:T(8,128)(2,1)S(1)} %get-tuple-element.47.d.refs_8_.refs_2_), channel_id=1, source_target_pairs={{0,6},{1,7},{2,4},{3,5},{4,2},{5,3},{6,0},{7,1},{8,14},{9,15},{10,... | collective-permute-start | bytes 884744 | tf_op jit(solution)/shard_map/ppermute | solution.py:362
  61.9 24.5 %slice-start = ((s8[4718592]{0:T(1024)(128)(4,1)}), s8[4194304]{0:T(1024)(128)(4,1)S(1)}, s32[]{:S(2)}) async-start(s8[4718592]{0:T(1024)(128)(4,1)} %bitcast.12), calls=%async_computation | async-start | bytes 8388608
  63.8 19.4 %collective-permute-start.17 = (bf16[2,288,512]{2,1,0:T(8,128)(2,1)S(1)}, bf16[2,288,512]{2,1,0:T(8,128)(2,1)S(1)}, u32[]{:S(2)}, u32[]{:S(2)}) collective-permute-start(bf16[2,288,512]{2,1,0:T(8,128)(2,1)S(1)} %get-tuple-element.61), channel_id=1, source_target_pairs={{0,1},{1,0},{2,3},{3,2},{4,5},{5,4},{6,7},{7,6},{8,9},{9,8},{10,11... | collective-permute-start | bytes 1769480 | tf_op jit(solution)/shard_map/weights_first/ppermute | solution.py:362
  63.8 22.6 %slice-start.1 = ((s8[4718592]{0:T(1024)(128)(4,1)}), s8[524288]{0:T(1024)(128)(4,1)S(1)}, s32[]{:S(2)}) async-start(s8[4718592]{0:T(1024)(128)(4,1)} %bitcast.12), calls=%async_computation.1 | async-start | bytes 1048576
  65.4 6.2 %collective-permute-start.4 = (bf16[32,256]{1,0:T(8,128)(2,1)S(1)}, bf16[32,256]{1,0:T(8,128)(2,1)S(1)}, u32[]{:S(2)}, u32[]{:S(2)}) collective-permute-start(bf16[32,256]{1,0:T(8,128)(2,1)S(1)} %get-tuple-element.50), channel_id=1, source_target_pairs={{0,1},{1,2},{2,3},{3,4},{4,5},{5,6},{6,7},{7,8},{8,9},{9,10},{10,1... | collective-permute-start | bytes 49160 | tf_op jit(solution)/shard_map/ppermute | solution.py:359
  65.9 5.8 %collective-permute-start.5 = (bf16[32,256]{1,0:T(8,128)(2,1)S(1)}, bf16[32,256]{1,0:T(8,128)(2,1)S(1)}, u32[]{:S(2)}, u32[]{:S(2)}) collective-permute-start(bf16[32,256]{1,0:T(8,128)(2,1)S(1)} %get-tuple-element.51), channel_id=1, source_target_pairs={{1,0},{2,1},{3,2},{4,3},{5,4},{6,5},{7,6},{8,7},{9,8},{10,9},{11,1... | collective-permute-start | bytes 49160 | tf_op jit(solution)/shard_map/ppermute | solution.py:359
  71.9 6.1 %collective-permute-start.19 = (bf16[256,256]{1,0:T(8,128)(2,1)S(1)}, bf16[256,256]{1,0:T(8,128)(2,1)S(1)}, u32[]{:S(2)}, u32[]{:S(2)}) collective-permute-start(bf16[256,256]{1,0:T(8,128)(2,1)S(1)} %get-tuple-element.53.d.refs_1_), channel_id=1, source_target_pairs={{0,2},{1,3},{2,0},{3,1},{4,6},{5,7},{6,4},{7,5},{8,10},{9,11},{10,... | collective-permute-start | bytes 393224 | tf_op jit(solution)/shard_map/ppermute | solution.py:362
  72.5 6.3 %collective-permute-start.20 = (bf16[256,256]{1,0:T(8,128)(2,1)S(1)}, bf16[256,256]{1,0:T(8,128)(2,1)S(1)}, u32[]{:S(2)}, u32[]{:S(2)}) collective-permute-start(bf16[256,256]{1,0:T(8,128)(2,1)S(1)} %get-tuple-element.53.d.refs_1_), channel_id=1, source_target_pairs={{0,4},{1,5},{2,6},{3,7},{4,0},{5,1},{6,2},{7,3},{8,12},{9,13},{10,... | collective-permute-start | bytes 393224 | tf_op jit(solution)/shard_map/ppermute | solution.py:362
  72.8 9.2 %collective-permute-start.21 = (bf16[256,256]{1,0:T(8,128)(2,1)S(1)}, bf16[256,256]{1,0:T(8,128)(2,1)S(1)}, u32[]{:S(2)}, u32[]{:S(2)}) collective-permute-start(bf16[256,256]{1,0:T(8,128)(2,1)S(1)} %get-tuple-element.53.d.refs_1_), channel_id=1, source_target_pairs={{0,6},{1,7},{2,4},{3,5},{4,2},{5,3},{6,0},{7,1},{8,14},{9,15},{10,... | collective-permute-start | bytes 393224 | tf_op jit(solution)/shard_map/ppermute | solution.py:362
  83.1 1.6 %collective-permute-start.22 = (bf16[2,288,256]{2,1,0:T(8,128)(2,1)S(1)}, bf16[2,288,256]{2,1,0:T(8,128)(2,1)S(1)}, u32[]{:S(2)}, u32[]{:S(2)}) collective-permute-start(bf16[2,288,256]{2,1,0:T(8,128)(2,1)S(1)} %get-tuple-element.65), channel_id=1, source_target_pairs={{0,1},{1,0},{2,3},{3,2},{4,5},{5,4},{6,7},{7,6},{8,9},{9,8},{10,11... | collective-permute-start | bytes 884744 | tf_op jit(solution)/shard_map/weights_second/ppermute | solution.py:362
  83.3 22.9 %collective-permute-start.18 = (bf16[288,512]{1,0:T(8,128)(2,1)S(1)}, bf16[288,512]{1,0:T(8,128)(2,1)S(1)}, u32[]{:S(2)}, u32[]{:S(2)}) collective-permute-start(bf16[288,512]{1,0:T(8,128)(2,1)S(1)} %bitcast.28), channel_id=1, source_target_pairs={{0,8},{1,9},{2,10},{3,11},{4,12},{5,13},{6,14},{7,15},{8,0},{9,1},... | collective-permute-start | bytes 884744 | tf_op jit(solution)/shard_map/weights_first/ppermute | solution.py:362
  84.8 21.4 %collective-permute-start.23 = (bf16[288,256]{1,0:T(8,128)(2,1)S(1)}, bf16[288,256]{1,0:T(8,128)(2,1)S(1)}, u32[]{:S(2)}, u32[]{:S(2)}) collective-permute-start(bf16[288,256]{1,0:T(8,128)(2,1)S(1)} %bitcast.29), channel_id=1, source_target_pairs={{0,8},{1,9},{2,10},{3,11},{4,12},{5,13},{6,14},{7,15},{8,0},{9,1},... | collective-permute-start | bytes 442376 | tf_op jit(solution)/shard_map/weights_second/ppermute | solution.py:362
  89.7 7.7 %collective-permute-start.6 = (bf16[32,512]{1,0:T(8,128)(2,1)S(1)}, bf16[32,512]{1,0:T(8,128)(2,1)S(1)}, u32[]{:S(2)}, u32[]{:S(2)}) collective-permute-start(bf16[32,512]{1,0:T(8,128)(2,1)S(1)} %get-tuple-element.56), channel_id=1, source_target_pairs={{0,1},{1,2},{2,3},{3,4},{4,5},{5,6},{6,7},{7,8},{8,9},{9,10},{10,1... | collective-permute-start | bytes 98312 | tf_op jit(solution)/shard_map/ppermute | solution.py:359
  89.7 7.7 %collective-permute-start.7 = (bf16[32,512]{1,0:T(8,128)(2,1)S(1)}, bf16[32,512]{1,0:T(8,128)(2,1)S(1)}, u32[]{:S(2)}, u32[]{:S(2)}) collective-permute-start(bf16[32,512]{1,0:T(8,128)(2,1)S(1)} %get-tuple-element.57), channel_id=1, source_target_pairs={{1,0},{2,1},{3,2},{4,3},{5,4},{6,5},{7,6},{8,7},{9,8},{10,9},{11,1... | collective-permute-start | bytes 98312 | tf_op jit(solution)/shard_map/ppermute | solution.py:359
  (7 other events, 7.4 us)

commit v3 on v1

v3 whole, which is shorter than its diff:
```python
import functools

import jax
import jax.numpy as jnp
import numpy as np
from jax import lax
from jax.experimental import pallas as pl
from jax.experimental.pallas import tpu as pltpu
from jax.sharding import PartitionSpec as P

BF = jnp.bfloat16
F32 = jnp.float32


def dot(a, b):
    return jnp.dot(a, b, preferred_element_type=F32)


def dot_nt(a, b):
    return lax.dot_general(a, b, (((1,), (1,)), ((), ())), preferred_element_type=F32)


def dot_tn(a, b):
    return lax.dot_general(a, b, (((0,), (0,)), ((), ())), preferred_element_type=F32)


def call(body, outs, *args, mib=24, scratch=(), hbm=(), pin=True, cost=0):
    vmem = pl.BlockSpec(memory_space=pltpu.VMEM)
    far = pl.BlockSpec(memory_space=pltpu.HBM)
    in_specs = [far if i in hbm else vmem for i in range(len(args))]
    args = [pltpu.with_memory_space_constraint(a, pltpu.HBM) if i in hbm else a for i, a in enumerate(args)]
    return pl.pallas_call(
        body,
        out_shape=[pltpu.VMEM(s, d) if pin else jax.ShapeDtypeStruct(s, d) for s, d in outs],
        in_specs=in_specs,
        out_specs=[vmem] * len(outs),
        scratch_shapes=list(scratch),
        compiler_params=pltpu.CompilerParams(vmem_limit_bytes=mib * 2**20),
        cost_estimate=pl.CostEstimate(flops=cost * 10**9, bytes_accessed=0, transcendentals=0),
    )(*args)


def frame_matrices(side):
    cells = side * side
    out = np.zeros((3, (side + 2) * side, cells + 4 * side), np.float32)
    for b in range(3):
        for r in range(side + 2):
            for j in range(side):
                c = j + b
                inner_r, inner_c = 1 <= r <= side, 1 <= c <= side
                if inner_r and inner_c:
                    src = (r - 1) * side + c - 1
                elif inner_c:
                    src = cells + (0 if r == 0 else 2) * side + c - 1
                elif inner_r:
                    src = cells + (3 if c == 0 else 1) * side + r - 1
                else:
                    continue
                out[b, r * side + j, src] = 1
    return out


def tap_matrices(side):
    m, cells = frame_matrices(side), side * side
    taps = [m[b, a * side : a * side + cells].T for a in range(3) for b in range(3)]
    return np.stack(taps)


def choose(index, values):
    out = jnp.full(index.shape, values[0], jnp.int32)
    for k in range(1, 4):
        out = jnp.where(index == k, values[k], out)
    return out


def edge_cell(edge, i, side):
    last = side - 1
    return jnp.where(
        edge == 0, i, jnp.where(edge == 1, i * side + last, jnp.where(edge == 2, last * side + i, i * side))
    )


def route_kernel(side, tiles, p_in, f_in, s_in, x, h, xh, s_first, s_second, sel, place, turn, rim_sel, partner, flip, slot, sems):
    c = x.shape[1]
    loads = [(p_in, partner), (f_in, flip), (s_in, slot), (x, xh.at[:, :c]), (h, xh.at[:, c:])]
    loads = [pltpu.make_async_copy(a, b, sems.at[n]) for n, (a, b) in enumerate(loads)]
    for copy in loads:
        copy.start()
    for copy in loads[:3]:
        copy.wait()
    me = lax.axis_index("tile")
    holder = lax.fori_loop(0, tiles, lambda t, a: a + jnp.where(slot[t] == me, t, 0), jnp.int32(0))
    q, fl, up = [], [], []
    for e in range(4):
        p = partner[e, holder]
        q.append(p & 3)
        fl.append(flip[e, holder])
        up.append((slot[p >> 2] == (me ^ 1)).astype(jnp.int32))
    out_at, in_at = [], []
    for e in range(4):
        before = sum([jnp.where(up[o] == up[e], 1, 0) for o in range(e)], jnp.int32(0))
        lower = sum(
            [jnp.where((up[o] == up[e]) & (q[o] < q[e]), 1, 0) for o in range(4) if o != e], jnp.int32(0)
        )
        out_at.append(before + 2 * (1 - up[e]))
        in_at.append(lower + 2 * (1 - up[e]))
    send_edge = [sum(jnp.where(out_at[e] == k, e, 0) for e in range(4)) for k in range(4)]
    recv_edge = [sum(jnp.where(in_at[e] == k, e, 0) for e in range(4)) for k in range(4)]
    recv_flip = [sum(jnp.where(in_at[e] == k, fl[e], 0) for e in range(4)) for k in range(4)]
    cells, rim = side * side, 4 * side

    def parts(shape, dim):
        at = lax.broadcasted_iota(jnp.int32, shape, dim)
        return at // side, at % side

    def one_hot(shape, dim, where_to):
        hit = lax.broadcasted_iota(jnp.int32, shape, dim) == where_to
        return jnp.where(hit, 1.0, 0.0).astype(BF)

    k, i = parts((rim, cells), 0)
    chosen = one_hot((rim, cells), 1, edge_cell(choose(k, send_edge), i, side))
    sel[...] = chosen
    for copy in loads[3:]:
        copy.wait()
    picked = dot(chosen, xh[...]).astype(BF)
    s_first[...] = picked[: rim // 2]
    s_second[...] = picked[rim // 2 :]
    k, i = parts((cells, rim), 1)
    i = jnp.where(choose(k, recv_flip) == 1, side - 1 - i, i)
    place[...] = one_hot((cells, rim), 0, edge_cell(choose(k, recv_edge), i, side))
    k, i = parts((rim, rim), 1)
    i = jnp.where(choose(k, recv_flip) == 1, side - 1 - i, i)
    turn[...] = one_hot((rim, rim), 0, choose(k, recv_edge) * side + i)
    width = 2 * side + 2 * cells
    k, i = parts((rim, width), 0)
    e = choose(k, send_edge)
    at = jnp.where(
        e == 0,
        i,
        jnp.where(
            e == 2, side + i, jnp.where(e == 3, 2 * side + i * side, 2 * side + cells + i * side + side - 1)
        ),
    )
    rim_sel[...] = one_hot((rim, width), 1, at)


def frames(side, tile, strips, m0, m2, f):
    whole = jnp.concatenate([tile, strips], axis=0)
    f[0] = dot(m0[...], whole).astype(BF)
    f[1, :side] = strips[:side]
    f[1, side : side + side * side] = tile
    f[1, side + side * side :] = strips[2 * side : 3 * side]
    f[2] = dot(m2[...], whole).astype(BF)


def conv(side, f, w, lo, hi, col_lo=0, col_hi=None):
    cells = side * side
    cols = [f[b, a * side : a * side + cells, :] for a in range(3) for b in range(3)]
    rows = [w[t, lo:hi, col_lo:col_hi] for t in range(9)]
    return dot(jnp.concatenate(cols, axis=1), jnp.concatenate(rows, axis=0))


def gate_kernel(side, xh, rp, rn, turn, m0, m2, w, bias, sel, gate, rh, pack, s_next, s_prev, f):
    c = xh.shape[1] // 2
    cells, rim = side * side, 4 * side
    strips = dot(turn[...], jnp.concatenate([rp[...], rn[...]], axis=0)).astype(BF)
    frames(side, xh[...], strips, m0, m2, f)
    act = jax.nn.sigmoid(conv(side, f, w, 0, 2 * c) + bias[...])
    gate[...] = act
    reset_h = (act[:, c:] * xh[:, c:].astype(F32)).astype(BF)
    rh[...] = reset_h
    pack[:cells] = xh[:, c:]
    pack[cells : cells + rim] = strips[:, :c]
    pack[cells + rim :] = strips[:, c:]
    picked = dot(sel[...], reset_h).astype(BF)
    s_next[...] = picked[: rim // 2]
    s_prev[...] = picked[rim // 2 :]


def load_kernel(n, *refs):
    sems = refs[-1]
    copies = [pltpu.make_async_copy(refs[k], refs[n + k], sems.at[k]) for k in range(n)]
    for copy in copies:
        copy.start()
    for copy in copies:
        copy.wait()


def cand_x_kernel(side, f, w, bias, out):
    c = w.shape[2]
    cells = side * side
    cols = [f[b, a * side : a * side + cells, :c] for a in range(3) for b in range(3)]
    rows = [w[t, :c, :] for t in range(9)]
    out[...] = dot(jnp.concatenate(cols, axis=1), jnp.concatenate(rows, axis=0)) + bias[...]


def cand_kernel(side, acc, rh, rp, rn, turn, m0, m2, w, gate, h, g, d, f):
    c = g.shape[1]
    cells = side * side
    strips = dot(turn[...], jnp.concatenate([rp[...], rn[...]], axis=0)).astype(BF)
    frames(side, rh[...], strips, m0, m2, f)
    d[2 * cells :] = strips
    candidate = jnp.tanh(acc[...] + conv(side, f, w, c, 2 * c))
    update = gate[:, :c]
    grad = g[...].astype(F32)
    d[:cells] = (grad * update * (1.0 - candidate * candidate)).astype(BF)
    d[cells : 2 * cells] = (grad * (candidate - h[:, c:].astype(F32)) * update * (1.0 - update)).astype(BF)


def spread(side, acc, d, w, lo, hi, col_lo, col_hi, fresh):
    cells = side * side
    if fresh:
        acc[...] = jnp.zeros_like(acc)
    for a in range(3):
        for b in range(3):
            rows = slice(a * side, a * side + cells)
            acc[b, rows, :] += dot_nt(d, w[a * 3 + b, lo:hi, col_lo:col_hi])


def gather_frame(side, acc):
    cells, c = side * side, acc.shape[2]
    rows = (side + 2) * side
    col = lax.broadcasted_iota(jnp.int32, (rows, c), 0) % side
    left, right = acc[0], acc[2]
    total = acc[1]
    total += jnp.where(col == side - 1, 0.0, pltpu.roll(left, rows - 1, 0))
    total += jnp.where(col == 0, 0.0, pltpu.roll(right, 1, 0))
    rim = jnp.concatenate(
        [total[:side], total[side + cells :], left[side : side + cells], right[side : side + cells]], axis=0
    ).astype(BF)
    return total[side : side + cells], rim


def back_rh_kernel(side, d, w, rim_sel, inner, s_next, s_prev, acc):
    c = w.shape[2]
    rim = 4 * side
    spread(side, acc, d[: side * side], w, c, 2 * c, 0, c, True)
    own, edge = gather_frame(side, acc)
    inner[...] = own
    picked = dot(rim_sel[...], edge).astype(BF)
    s_next[...] = picked[: rim // 2]
    s_prev[...] = picked[rim // 2 :]


def back_early_kernel(side, d, wc, wg, acc):
    c = wc.shape[2]
    cells = side * side
    acc[...] = jnp.zeros_like(acc)
    for a in range(3):
        for b in range(3):
            rows = slice(a * side, a * side + cells)
            t = a * 3 + b
            acc[b, rows, :c] += dot_nt(d[:cells], wc[t, :c, :]) + dot_nt(d[cells : 2 * cells], wg[t, :c, :c])
            acc[b, rows, c:] += dot_nt(d[cells : 2 * cells], wg[t, c:, :c])


def reset_kernel(side, inner, rp, rn, place, gate, h, g, d_cu, d, direct):
    c = g.shape[1]
    d_rh = inner[...] + dot(place[...], jnp.concatenate([rp[...], rn[...]], axis=0))
    update, reset = gate[:, :c], gate[:, c:]
    cells = side * side
    d[: 2 * cells] = d_cu[: 2 * cells]
    d[3 * cells :] = d_cu[2 * cells :]
    d[2 * cells : 3 * cells] = (d_rh * h[:, c:].astype(F32) * reset * (1.0 - reset)).astype(BF)
    direct[...] = g[...].astype(F32) * (1.0 - update) + d_rh * reset


def back_gate_kernel(side, early, d, w, direct, rim_sel, inner, s_next, s_prev, acc):
    c = d.shape[1]
    rim = 4 * side
    acc[...] = early[...]
    cells = side * side
    spread(side, acc, d[2 * cells : 3 * cells], w, 0, 2 * c, c, 2 * c, False)
    own, edge = gather_frame(side, acc)
    inner[:, :c] = own[:, :c]
    inner[:, c:] = own[:, c:] + direct[...]
    picked = dot(rim_sel[...], edge).astype(BF)
    s_next[...] = picked[: rim // 2]
    s_prev[...] = picked[rim // 2 :]


def final_kernel(inner, rp, rn, place, gx, gh):
    c = gx.shape[1]
    total = inner[...] + dot(place[...], jnp.concatenate([rp[...], rn[...]], axis=0))
    gx[...] = total[:, :c].astype(BF)
    gh[...] = total[:, c:].astype(BF)


def near_reset_kernel(side, *refs):
    x, packs, (m0, m2, w, bias, out, f) = refs[1:4], refs[5:8], refs[8:]
    cells, rim, c = side * side, 4 * side, out.shape[2]
    for n in range(3):
        h = packs[n][:cells]
        tile = jnp.concatenate([x[n][...], h], axis=1)
        strips = jnp.concatenate([packs[n][cells : cells + rim], packs[n][cells + rim :]], axis=1)
        frames(side, tile, strips, m0, m2, f)
        reset = jax.nn.sigmoid(conv(side, f, w, 0, 2 * c, c, 2 * c) + bias[:, c:])
        out[n] = (reset * h.astype(F32)).astype(BF)


def lhs_kernel(side, rows, tiles, cand, *refs):
    x, packs, more = refs[:4], refs[4:8], refs[8:-3]
    me = lax.axis_index("tile")
    taps, out, src = refs[-3:]
    cells, rim = side * side, 4 * side
    c = packs[0].shape[1]
    per_tap = 2 * c // 128
    for n in range(4):
        lanes = slice(n * 128, (n + 1) * 128)
        for k in range(per_tap):
            at = slice(k * 128, (k + 1) * 128)
            col = slice(at.start % c, at.start % c + 128)
            if at.start < c:
                src[k, :cells, lanes] = x[n][:, col]
                src[k, cells:, lanes] = packs[n][cells : cells + rim, col]
            elif cand:
                rh, rh_near, ds = more[0], more[1], more[2:]
                src[k, :cells, lanes] = rh[:, col] if n == 0 else rh_near[n - 1, :, col]
                src[k, cells:, lanes] = ds[n][3 * cells :, col]
            else:
                src[k, :cells, lanes] = packs[n][:cells, col]
                src[k, cells:, lanes] = packs[n][cells + rim :, col]
    for t in range(out.shape[0]):
        target = me ^ (8 * (t // 2) + t % 2)
        for n in range(out.shape[1] // 128):
            block = jnp.minimum(target * rows // 128 + n, 9 * per_tap - 1)
            part = dot_tn(src[block % per_tap], taps[block // per_tap]).astype(BF)
            for k in range(4):
                out[t, n * 128 : (n + 1) * 128, k * cells : (k + 1) * cells] = part[k * 128 : (k + 1) * 128]


def weight_kernel(side, rows, parts, lhs, d0, d1, d2, d3, keep, *refs):
    sends, acc = refs[:-1], refs[-1]
    cells = side * side
    me = lax.axis_index("tile")
    width = sends[0].shape[2]
    right = [jnp.concatenate([d[k * cells : (k + 1) * cells] for k in parts], axis=1) for d in (d0, d1, d2, d3)]
    right = jnp.concatenate(right, axis=0)
    for t in range(lhs.shape[0]):
        target = me ^ (8 * (t // 2) + t % 2)
        first = pl.multiple_of(target * rows % 128, 8)
        acc[t % 2] = dot(lhs[t], right)
        part = acc[t % 2, pl.ds(first, rows), :]
        if t % 2 == 0:
            keep[t // 2] = part
        else:
            for k, send in enumerate(sends):
                send[t // 2] = part[:, k * width : (k + 1) * width].astype(BF)


def pair_kernel(keep, *refs):
    got, (own, far) = refs[:-2], refs[-2:]
    width = got[0].shape[2]
    for k, part in enumerate(got):
        at = slice(k * width, (k + 1) * width)
        own[:, at] = keep[0, :, at] + part[0].astype(F32)
        for m in range(1, keep.shape[0]):
            far[m - 1, :, at] = (keep[m, :, at] + part[m].astype(F32)).astype(BF)


def sum_kernel(own, *refs):
    total = own[...]
    for r in refs[:-1]:
        total += r[...].astype(F32)
    refs[-1][...] = total


def shards(
    x_tiles, h_tiles, grad_out, w_gate, b_gate, w_cand, b_cand, partner_edge, edge_flip, tile_slot
):
    side, c = x_tiles.shape[1], x_tiles.shape[3]
    tiles = lax.axis_size("tile")
    cells, rim = side * side, 4 * side
    half, band = rim // 2, (side + 2) * side
    rows = 18 * c // tiles
    groups = tiles // 8
    blocks = max((rows * j + rows - 1) // 128 - rows * j // 128 + 1 for j in range(tiles)) * 128
    x, h, g = (u.reshape(cells, c) for u in (x_tiles, h_tiles, grad_out))
    wg, wc = w_gate.reshape(9, 2 * c, 2 * c), w_cand.reshape(9, 2 * c, c)
    bg, bc = b_gate.reshape(1, 2 * c), b_cand.reshape(1, c)
    m = frame_matrices(side)
    m0, m2 = jnp.asarray(m[0], BF), jnp.asarray(m[2], BF)
    taps = jnp.asarray(tap_matrices(side), BF)
    cross = [(i, (i + 1) % tiles if i % 2 else (i - 1) % tiles) for i in range(tiles)]
    ran = []

    def run(name, body, outs, *args, **options):
        if ran:
            args = (after(args[0], ran[-1]),) + args[1:]
        with jax.named_scope(name):
            results = call(body, outs, *args, **options)
        ran.append(results[0])
        return results

    def load(name, *args):
        n = len(args)
        return run(
            name, functools.partial(load_kernel, n), [(a.shape, a.dtype) for a in args], *args,
            hbm=range(n), scratch=[pltpu.SemaphoreType.DMA((n,))],
        )

    def after(u, *others):
        return lax.optimization_barrier((u,) + others)[0]

    def swap(u, k):
        return lax.ppermute(u, "tile", [(i, i ^ k) for i in range(tiles)])

    def exchange(s_first, s_second):
        return swap(s_first, 1), lax.ppermute(s_second, "tile", cross)

    def near(u):
        return [u] + [swap(u, k) for k in (2, 4, 6)]

    def lhs_of(name, cand, *args):
        return run(
            name, functools.partial(lhs_kernel, side, rows, tiles, cand),
            [((2 * groups, blocks, 4 * cells), BF)],
            *args, taps_v,
            scratch=[pltpu.VMEM((2 * c // 128, cells + rim, 512), BF)],
        )[0]

    def products(name, parts, lhs, ds):
        n = len(parts)
        keep, *sends = run(
            name, functools.partial(weight_kernel, side, rows, parts),
            [((groups, rows, n * c), F32)] + [((groups, rows, n * c // 2), BF)] * 2,
            lhs, *ds,
            scratch=[pltpu.VMEM((2, blocks, n * c), F32)],
        )
        return keep, [swap(u, 1) for u in sends]

    def pair(name, keep, got):
        n = keep.shape[2]
        own, far = run(name, pair_kernel, [((rows, n), F32), ((groups - 1, rows, n), BF)], keep, *got)
        return [own] + [swap(far[k - 1], 8 * k) for k in range(1, groups)]

    xh, s1n, s1p, sel, place, turn, rim_sel = run(
        "route", functools.partial(route_kernel, side, tiles),
        [
            ((cells, 2 * c), BF),
            ((half, 2 * c), BF),
            ((half, 2 * c), BF),
            ((rim, cells), BF),
            ((cells, rim), BF),
            ((rim, rim), BF),
            ((rim, 2 * side + 2 * cells), BF),
        ],
        partner_edge.T, edge_flip.T, tile_slot, x, h,
        hbm=(0, 1, 2, 3, 4),
        scratch=[
            pltpu.SMEM((4, tiles), jnp.int32),
            pltpu.SMEM((4, tiles), jnp.int32),
            pltpu.SMEM((tiles,), jnp.int32),
            pltpu.SemaphoreType.DMA((5,)),
        ],
    )
    r1p, r1n = exchange(s1n, s1p)
    wg_v, m0, m2, bg_v = load("load_gate", wg, m0, m2, bg)
    x_near = near(after(x, bg_v))
    gate, rh, pack, s2n, s2p, f = run(
        "gate", functools.partial(gate_kernel, side),
        [
            ((cells, 2 * c), F32),
            ((cells, c), BF),
            ((cells + 2 * rim, c), BF),
            ((half, c), BF),
            ((half, c), BF),
            ((3, band, 2 * c), BF),
        ],
        xh, r1p, r1n, turn, m0, m2, wg_v, bg_v, sel, cost=5,
    )
    r2p, r2n = exchange(s2n, s2p)
    wc_v, bc_v, g_v = load("load_cand", wc, bc, g)
    pack_near = near(after(pack, *x_near))
    (acc_x,) = run("cand_x", functools.partial(cand_x_kernel, side), [((cells, c), F32)], f, wc_v, bc_v)
    d_cu, _ = run(
        "cand", functools.partial(cand_kernel, side),
        [((2 * cells + rim, c), BF), ((3, band, c), BF)],
        acc_x, rh, r2p, r2n, turn, m0, m2, wc_v, gate, xh, g_v, cost=3,
    )
    inner_rh, s3n, s3p, _ = run(
        "back_rh", functools.partial(back_rh_kernel, side),
        [((cells, c), F32), ((half, c), BF), ((half, c), BF), ((3, band, c), F32)],
        d_cu, wc_v, rim_sel,
    )
    r3p, r3n = exchange(s3n, s3p)
    (early,) = run(
        "back_early", functools.partial(back_early_kernel, side), [((3, band, 2 * c), F32)], d_cu, wc_v, wg_v
    )
    (taps_v,) = load("load_taps", taps)
    d, direct = run(
        "reset", functools.partial(reset_kernel, side),
        [((3 * cells + rim, c), BF), ((cells, c), F32)],
        inner_rh, r3p, r3n, place, gate, xh, g_v, d_cu,
    )
    d_near = near(after(d, *pack_near))
    lhs_gate = lhs_of("lhs_gate", False, *x_near, *pack_near)
    (rh_near,) = run(
        "near_reset", functools.partial(near_reset_kernel, side), [((3, cells, c), BF)],
        *x_near, *pack_near, m0, m2, wg_v, bg_v,
        scratch=[pltpu.VMEM((3, band, 2 * c), BF)],
    )
    inner, s4n, s4p, _ = run(
        "back_gate", functools.partial(back_gate_kernel, side),
        [((cells, 2 * c), F32), ((half, 2 * c), BF), ((half, 2 * c), BF), ((3, band, 2 * c), F32)],
        early, d, wg_v, direct, rim_sel,
    )
    r4p, r4n = exchange(s4n, s4p)
    keep_g, got_g = products("weights_gate", (1, 2), lhs_gate, d_near)
    gx, gh = run(
        "final", final_kernel, [((cells, c), BF), ((cells, c), BF)], inner, r4p, r4n, place, pin=False, cost=5
    )
    parts_g = pair("pair_gate", keep_g, got_g)
    lhs_cand = lhs_of("lhs_cand", True, *x_near, *pack_near, rh, rh_near, *d_near)
    keep_c, got_c = products("weights_cand", (0,), lhs_cand, d_near)
    parts_c = pair("pair_cand", keep_c, got_c)
    (grad_w_gate,) = run("sum_gate", sum_kernel, [((rows, 2 * c), F32)], *parts_g, pin=False, cost=2)
    (grad_w_cand,) = run("sum_cand", sum_kernel, [((rows, c), F32)], *parts_c, pin=False)
    shape = (1, side, side, c)
    return gx.reshape(shape), gh.reshape(shape), grad_w_gate, grad_w_cand


def solution(mesh):
    tile = P(("grp", "tile"), None, None, None)
    rows = P(("grp", "tile"), None)
    return jax.shard_map(
        shards,
        mesh=mesh,
        in_specs=(tile, tile, tile) + (P(),) * 7,
        out_specs=(tile, tile, rows, rows),
        check_vma=False,
    )
```

time: 198 us -> 81.7 us (0.41)
  waiting for transfers between devices: 120 us -> 25.2 us
  local copies, waits for them, and re-layouts: 27 us -> 0.01 us
  Pallas kernels: 10.3 us -> 29.2 us
  between operations: 14.4 us -> 0.86 us
  starting transfers between devices: 19.1 us -> 26.3 us
  matrix products: 3.86 us -> 0 us
  other arithmetic: 2.74 us -> 0 us
    unnamed x4 -> x0, waiting for transfers between devices: 115 us -> none
    unnamed x57 -> x2, local copies, waits for them, and re-layouts: 25.9 us -> 0.01 us
    ppermute x8 -> x23, waiting for transfers between devices: 5.28 us -> 25.2 us  [the longest x19 23 us: swap(): return lax.ppermute(u, 'tile', [(i, i ^ k) for i in range(tiles)])]
    pallas_call x9 -> x21, Pallas kernels: 10.3 us -> 29.2 us  [call(): pl.pallas_call(body, out_shape=[pltpu.VMEM(s, d) if pin else jax.ShapeDty...]
    ppermute x8 -> x23, starting transfers between devices: 19 us -> 26.3 us  [the longest x19 15.6 us: swap(): return lax.ppermute(u, 'tile', [(i, i ^ k) for i in range(tiles)])]
    dot_general x3 -> x0, matrix products: 3.86 us -> none  [dot_tn(): lax.dot_general(a, b, (((0,), (0,)), ((), ())), preferred_element_type=F32)]
    concatenate x3 -> x0, other arithmetic: 2.55 us -> none  [the longest x1 2.48 us: shards(): jnp.concatenate([gwc, gwu], axis=1)]
  transfers between devices with their start and end apart: 10 -> 23, of which waited for: 8 -> 8; matrix products, arithmetic and copies ran while one was open for 7% -> 0% of each run, Pallas kernels for 2% -> 33%
where the time goes in v3:
time: 81.7 us; the launch traced here: 81.5 us
  Pallas kernels  29.2 us (36%)
  starting transfers between devices  26.3 us (32%)
  waiting for transfers between devices  25.2 us (31%)
  between operations  0.86 us (1%)
    pallas_call x21, Pallas kernels, call(): pl.pallas_call(body, out_shape=[pltpu.VMEM(s, d) if pin else jax.ShapeDty...  29.2 us
    ppermute x19, waiting for transfers between devices, swap(): return lax.ppermute(u, 'tile', [(i, i ^ k) for i in range(tiles)])  23 us
    ppermute x19, starting transfers between devices, swap(): return lax.ppermute(u, 'tile', [(i, i ^ k) for i in range(tiles)])  15.6 us
    ppermute x4, starting transfers between devices, exchange(): return (swap(s_first, 1), lax.ppermute(s_second, 'tile', cross))  10.7 us
    ppermute x4, waiting for transfers between devices, exchange(): return (swap(s_first, 1), lax.ppermute(s_second, 'tile', cross))  2.19 us
  transfers between devices with their start and end apart: 23, of which 8 were waited for; matrix products, arithmetic and copies ran while one was open for 0% of the time, Pallas kernels for 33%

profile of v3, /device:TPU:0, one launch (start us, length us, event | category | flops | bytes accessed | tf_op | source)
XLA Modules:
  0.0 81.5 jit_solution(4991943095947744588)
XLA Ops:
  0.6 1.2 %route.1 = (bf16[256,512]{1,0:T(8,128)(2,1)S(1)}, bf16[32,512]{1,0:T(8,128)(2,1)S(1)}, bf16[32,512]{1,0:T(8,128)(2,1)S(1)}, bf16[64,256]{1,0:T(8,128)(2,1)S(1)},...) custom-call(s32[4,16]{1,0:T(4,128)} %bitcast.26, s32[4,16]{1,0:T(4,128)} %bitcast.27, ...), custom_call_target="tpu_custom_call" | custom-call | tf_op jit(solution)/shard_map/route/pallas_call | solution.py:32
  1.9 0.5 collective-permute-start
  2.4 5.7 %collective-permute-start.1 = (bf16[32,512]{1,0:T(8,128)(2,1)S(1)}, bf16[32,512]{1,0:T(8,128)(2,1)S(1)}, u32[]{:S(2)}, u32[]{:S(2)}) collective-permute-start(bf16[32,512]{1,0:T(8,128)(2,1)S(1)} %get-tuple-element.70), channel_id=1, source_target_pairs={{0,15},{1,2},{2,1},{3,4},{4,3},{5,6},{6,5},{7,8},{8,7},{9,10},{10,... | collective-permute-start | bytes 98312 | tf_op jit(solution)/shard_map/ppermute | solution.py:409
  8.1 2.5 %load_gate.1 = (bf16[9,512,512]{2,1,0:T(8,128)(2,1)S(1)}, bf16[288,320]{1,0:T(8,128)(2,1)S(1)}, bf16[288,320]{1,0:T(8,128)(2,1)S(1)}, f32[1,512]{1,0:T(1,128)S(1)}) custom-call(bf16[9,512,512]{2,1,0:T(8,128)(2,1)} %bitcast.22, bf16[288,320]{1,0:T(8,128)(2,1)} %constant.6.clone.refs_1_, bf16[288,320]{1,0:T(8,128)(2,1)} %constant.7.clone.refs_2_, ...), custom_call_target="tpu_custom_call" | custom-call | tf_op jit(solution)/shard_map/load_gate/pallas_call | solution.py:32
  10.7 3.4 %collective-permute-start.8 = (bf16[256,256]{1,0:T(8,128)(2,1)S(1)}, bf16[256,256]{1,0:T(8,128)(2,1)S(1)}, u32[]{:S(2)}, u32[]{:S(2)}) collective-permute-start(bf16[256,256]{1,0:T(8,128)(2,1)S(1)} %bitcast.16), channel_id=1, source_target_pairs={{0,6},{1,7},{2,4},{3,5},{4,2},{5,3},{6,0},{7,1},{8,14},{9,15},{10,... | collective-permute-start | bytes 393224 | tf_op jit(solution)/shard_map/ppermute | solution.py:406
  14.1 1.9 %gate.1 = (f32[256,512]{1,0:T(8,128)S(1)}, bf16[256,256]{1,0:T(8,128)(2,1)S(1)}, bf16[384,256]{1,0:T(8,128)(2,1)S(1)}, bf16[32,256]{1,0:T(8,128)(2,1)S(1)}, bf16...) custom-call(bf16[256,512]{1,0:T(8,128)(2,1)S(1)} %get-tuple-element.68.xh.h, ...), custom_call_target="tpu_custom_call" | custom-call | flops 5000000000 | tf_op jit(solution)/shard_map/gate/pallas_call | solution.py:32
  16.0 0.6 collective-permute-start.3
  16.6 1.7 %load_cand.1 = (bf16[9,512,256]{2,1,0:T(8,128)(2,1)S(1)}, f32[1,256]{1,0:T(1,128)S(1)}, bf16[256,256]{1,0:T(8,128)(2,1)S(1)}) custom-call(bf16[9,512,256]{2,1,0:T(8,128)(2,1)} %bitcast.23, f32[1,256]{1,0:T(1,128)} %bitcast.29, bf16[256,256]{1,0:T(8,128)(2,1)} %bitcast.24), custom_call_target="tpu_custom_call" | custom-call | tf_op jit(solution)/shard_map/load_cand/pallas_call | solution.py:32
  18.9 1.6 %collective-permute-start.9 = (bf16[384,256]{1,0:T(8,128)(2,1)S(1)}, bf16[384,256]{1,0:T(8,128)(2,1)S(1)}, u32[]{:S(2)}, u32[]{:S(2)}) collective-permute-start(bf16[384,256]{1,0:T(8,128)(2,1)S(1)} %get-tuple-element.100.refs_4_), channel_id=1, source_target_pairs={{0,2},{1,3},{2,0},{3,1},{4,6},{5,7},{6,4},{7,5},{8,10},{9,11},{10,... | collective-permute-start | bytes 589832 | tf_op jit(solution)/shard_map/ppermute | solution.py:406
  20.7 1.8 %collective-permute-start.11 = (bf16[384,256]{1,0:T(8,128)(2,1)S(1)}, bf16[384,256]{1,0:T(8,128)(2,1)S(1)}, u32[]{:S(2)}, u32[]{:S(2)}) collective-permute-start(bf16[384,256]{1,0:T(8,128)(2,1)S(1)} %get-tuple-element.100.refs_4_), channel_id=1, source_target_pairs={{0,6},{1,7},{2,4},{3,5},{4,2},{5,3},{6,0},{7,1},{8,14},{9,15},{10,... | collective-permute-start | bytes 589832 | tf_op jit(solution)/shard_map/ppermute | solution.py:406
  22.4 1.2 %cand.1 = (bf16[576,256]{1,0:T(8,128)(2,1)S(1)}, bf16[3,288,256]{2,1,0:T(8,128)(2,1)}) custom-call(f32[256,256]{1,0:T(8,128)S(1)} %cand_x.1.acc, bf16[256,256]{1,0:T(8,128)(2,1)S(1)} %get-tuple-element.82.rh.refs_8_, bf16[32,256]{1,0:T(8,128)(2,1)S(1)} %collective-permute-done.2.rp, bf16[32,256]{1,0:T(8,128)(2,1)S(1)} %collective-permute-done.3.rn, ...), custom_call_target="tpu_custom_call" | custom-call | flops 3000000000 | tf_op jit(solution)/shard_map/cand/pallas_call | solution.py:32
  23.6 1.5 %back_rh.1 = (f32[256,256]{1,0:T(8,128)S(1)}, bf16[32,256]{1,0:T(8,128)(2,1)S(1)}, bf16[32,256]{1,0:T(8,128)(2,1)S(1)}, f32[3,288,256]{2,1,0:T(8,128)}) custom-call(bf16[576,256]{1,0:T(8,128)(2,1)S(1)} %get-tuple-element.90.d.d_cu, bf16[9,512,256]{2,1,0:T(8,128)(2,1)S(1)} %get-tuple-element.79.w.wc, bf16[64,544]{1,0:T(8,128)(2,1)S(1)} %get-tuple-element.88.rim_sel), custom_call_target="tpu_custom_call" | custom-call | tf_op jit(solution)/shard_map/back_rh/pallas_call | solution.py:32
  25.1 3.0 %collective-permute-start.5 = (bf16[32,256]{1,0:T(8,128)(2,1)S(1)}, bf16[32,256]{1,0:T(8,128)(2,1)S(1)}, u32[]{:S(2)}, u32[]{:S(2)}) collective-permute-start(bf16[32,256]{1,0:T(8,128)(2,1)S(1)} %get-tuple-element.95), channel_id=1, source_target_pairs={{0,15},{1,2},{2,1},{3,4},{4,3},{5,6},{6,5},{7,8},{8,7},{9,10},{10,... | collective-permute-start | bytes 49160 | tf_op jit(solution)/shard_map/ppermute | solution.py:409
  28.1 1.1 %back_early.1.early = f32[3,288,512]{2,1,0:T(8,128)S(1)} custom-call(bf16[576,256]{1,0:T(8,128)(2,1)S(1)} %get-tuple-element.90.d.d_cu, bf16[9,512,256]{2,1,0:T(8,128)(2,1)S(1)} %get-tuple-element.79.w.wc, bf16[9,512,512]{2,1,0:T(8,128)(2,1)S(1)} %get-tuple-element.67.w.wg.refs_10_), custom_call_target="tpu_custom_call" | custom-call | tf_op jit(solution)/shard_map/back_early/pallas_call | solution.py:32
  29.3 1.4 %load_taps.1.refs_8_.refs_14_ = bf16[9,320,256]{2,1,0:T(8,128)(2,1)S(1)} custom-call(bf16[9,320,256]{2,1,0:T(8,128)(2,1)} %constant.8.clone.refs_0_), custom_call_target="tpu_custom_call" | custom-call | tf_op jit(solution)/shard_map/load_taps/pallas_call | solution.py:32
  30.7 2.2 %collective-permute-done.5.rn = bf16[32,256]{1,0:T(8,128)(2,1)S(1)} collective-permute-done((bf16[32,256]{1,0:T(8,128)(2,1)S(1)}, bf16[32,256]{1,0:T(8,128)(2,1)S(1)}, u32[]{:S(2)}, u32[]{:S(2)}) %collective-permute-start.5) | collective-permute-done | bytes 16416 | tf_op jit(solution)/shard_map/ppermute | solution.py:409
  33.3 3.4 %collective-permute-start.14 = (bf16[832,256]{1,0:T(8,128)(2,1)S(1)}, bf16[832,256]{1,0:T(8,128)(2,1)S(1)}, u32[]{:S(2)}, u32[]{:S(2)}) collective-permute-start(bf16[832,256]{1,0:T(8,128)(2,1)S(1)} %get-tuple-element.106.d.d0.refs_10_), channel_id=1, source_target_pairs={{0,6},{1,7},{2,4},{3,5},{4,2},{5,3},{6,0},{7,1},{8,14},{9,15},{10,... | collective-permute-start | bytes 1277960 | tf_op jit(solution)/shard_map/ppermute | solution.py:406
  36.7 2.1 %lhs_gate.1.lhs = bf16[4,384,1024]{2,1,0:T(8,128)(2,1)S(1)} custom-call(bf16[256,256]{1,0:T(8,128)(2,1)S(1)} %bitcast.17, bf16[256,256]{1,0:T(8,128)(2,1)S(1)} %collective-permute-done.6.refs_1_, bf16[256,256]{1,0:T(8,128)(2,1)S(1)} %collective-permute-done.7.refs_2_, bf16[256,256]{1,0:T(8,128)(2,1)S(1)} %collective-permute-done.8.refs_3_, ...), custom_call_target="tpu_custom_call" | custom-call | tf_op jit(solution)/shard_map/lhs_gate/pallas_call | solution.py:32
  38.8 4.1 %near_reset.1.refs_9_ = bf16[3,256,256]{2,1,0:T(8,128)(2,1)S(1)} custom-call(bf16[256,256]{1,0:T(8,128)(2,1)S(1)} %bitcast.18, bf16[256,256]{1,0:T(8,128)(2,1)S(1)} %collective-permute-done.6.refs_1_, bf16[256,256]{1,0:T(8,128)(2,1)S(1)} %collective-permute-done.7.refs_2_, bf16[256,256]{1,0:T(8,128)(2,1)S(1)} %collective-permute-done.8.refs_3_, ...), custom_call_target="tpu_custom_call" | custom-call | tf_op jit(solution)/shard_map/near_reset/pallas_call | solution.py:32
  42.9 2.1 %back_gate.1 = (f32[256,512]{1,0:T(8,128)S(1)}, bf16[32,512]{1,0:T(8,128)(2,1)S(1)}, bf16[32,512]{1,0:T(8,128)(2,1)S(1)}, f32[3,288,512]{2,1,0:T(8,128)}) custom-call(f32[3,288,512]{2,1,0:T(8,128)S(1)} %back_early.1.early, bf16[832,256]{1,0:T(8,128)(2,1)S(1)} %get-tuple-element.106.d.d0.refs_10_, bf16[9,512,512]{2,1,0:T(8,128)(2,1)S(1)} %get-tuple-element.67.w.wg.refs_10_, ...), custom_call_target="tpu_custom_call" | custom-call | tf_op jit(solution)/shard_map/back_gate/pallas_call | solution.py:32
  45.0 1.4 %collective-permute-start.16 = (bf16[32,512]{1,0:T(8,128)(2,1)S(1)}, bf16[32,512]{1,0:T(8,128)(2,1)S(1)}, u32[]{:S(2)}, u32[]{:S(2)}) collective-permute-start(bf16[32,512]{1,0:T(8,128)(2,1)S(1)} %get-tuple-element.110), channel_id=1, source_target_pairs={{0,15},{1,2},{2,1},{3,4},{4,3},{5,6},{6,5},{7,8},{8,7},{9,10},{10,... | collective-permute-start | bytes 98312 | tf_op jit(solution)/shard_map/ppermute | solution.py:409
  46.4 7.2 %collective-permute-done.14.d3.refs_13_ = bf16[832,256]{1,0:T(8,128)(2,1)S(1)} collective-permute-done((bf16[832,256]{1,0:T(8,128)(2,1)S(1)}, bf16[832,256]{1,0:T(8,128)(2,1)S(1)}, u32[]{:S(2)}, u32[]{:S(2)}) %collective-permute-start.14) | collective-permute-done | bytes 426016 | tf_op jit(solution)/shard_map/ppermute | solution.py:406
  53.6 1.8 %weights_gate.1 = (f32[2,288,512]{2,1,0:T(8,128)S(1)}, bf16[2,288,256]{2,1,0:T(8,128)(2,1)S(1)}, bf16[2,288,256]{2,1,0:T(8,128)(2,1)S(1)}) custom-call(bf16[4,384,1024]{2,1,0:T(8,128)(2,1)S(1)} %lhs_gate.1.lhs, bf16[832,256]{1,0:T(8,128)(2,1)S(1)} %get-tuple-element.106.d.d0.refs_10_, bf16[832,256]{1,0:T(8,128)(2,1)S(1)} %collective-permute-done.12.d1.refs_11_, ...), custom_call_target="tpu_custom_call" | custom-call | tf_op jit(solution)/shard_map/weights_gate/pallas_call | solution.py:32
  56.3 0.9 %final.1 = (bf16[256,256]{1,0:T(8,128)(2,1)}, bf16[256,256]{1,0:T(8,128)(2,1)}) custom-call(f32[256,512]{1,0:T(8,128)S(1)} %get-tuple-element.108.inner, bf16[32,512]{1,0:T(8,128)(2,1)S(1)} %collective-permute-done.15.rp, bf16[32,512]{1,0:T(8,128)(2,1)S(1)} %collective-permute-done.16.rn, bf16[256,64]{1,0:T(8,128)(2,1)S(1)} %get-tuple-element.96.place), custom_call_target="tpu_custom_call" | custom-call | flops 5000000000 | tf_op jit(solution)/shard_map/final/pallas_call | solution.py:32
  57.8 3.0 %collective-permute-start.21 = (bf16[288,512]{1,0:T(8,128)(2,1)S(1)}, bf16[288,512]{1,0:T(8,128)(2,1)S(1)}, u32[]{:S(2)}, u32[]{:S(2)}) collective-permute-start(bf16[288,512]{1,0:T(8,128)(2,1)S(1)} %bitcast.20), channel_id=1, source_target_pairs={{0,8},{1,9},{2,10},{3,11},{4,12},{5,13},{6,14},{7,15},{8,0},{9,1},... | collective-permute-start | bytes 884744 | tf_op jit(solution)/shard_map/ppermute | solution.py:406
  60.8 2.1 %lhs_cand.1.lhs = bf16[4,384,1024]{2,1,0:T(8,128)(2,1)S(1)} custom-call(bf16[256,256]{1,0:T(8,128)(2,1)S(1)} %bitcast.19, bf16[256,256]{1,0:T(8,128)(2,1)S(1)} %collective-permute-done.6.refs_1_, bf16[256,256]{1,0:T(8,128)(2,1)S(1)} %collective-permute-done.7.refs_2_, bf16[256,256]{1,0:T(8,128)(2,1)S(1)} %collective-permute-done.8.refs_3_, ...), custom_call_target="tpu_custom_call" | custom-call | tf_op jit(solution)/shard_map/lhs_cand/pallas_call | solution.py:32
  63.0 1.1 %weights_cand.1 = (f32[2,288,256]{2,1,0:T(8,128)S(1)}, bf16[2,288,128]{2,1,0:T(8,128)(2,1)S(1)}, bf16[2,288,128]{2,1,0:T(8,128)(2,1)S(1)}) custom-call(bf16[4,384,1024]{2,1,0:T(8,128)(2,1)S(1)} %lhs_cand.1.lhs, bf16[832,256]{1,0:T(8,128)(2,1)S(1)} %get-tuple-element.106.d.d0.refs_10_, bf16[832,256]{1,0:T(8,128)(2,1)S(1)} %collective-permute-done.12.d1.refs_11_, ...), custom_call_target="tpu_custom_call" | custom-call | tf_op jit(solution)/shard_map/weights_cand/pallas_call | solution.py:32
  64.6 0.9 %collective-permute-done.19.refs_0_ = bf16[2,288,128]{2,1,0:T(8,128)(2,1)S(1)} collective-permute-done((bf16[2,288,128]{2,1,0:T(8,128)(2,1)S(1)}, bf16[2,288,128]{2,1,0:T(8,128)(2,1)S(1)}, u32[]{:S(2)}, u32[]{:S(2)}) %collective-permute-start.19) | collective-permute-done | bytes 147488 | tf_op jit(solution)/shard_map/ppermute | solution.py:406
  65.9 12.3 %collective-permute-done.21.refs_0_ = bf16[288,512]{1,0:T(8,128)(2,1)S(1)} collective-permute-done((bf16[288,512]{1,0:T(8,128)(2,1)S(1)}, bf16[288,512]{1,0:T(8,128)(2,1)S(1)}, u32[]{:S(2)}, u32[]{:S(2)}) %collective-permute-start.21) | collective-permute-done | bytes 294944 | tf_op jit(solution)/shard_map/ppermute | solution.py:406
  78.1 0.9 %sum_gate.1 = f32[288,512]{1,0:T(8,128)} custom-call(f32[288,512]{1,0:T(8,128)S(1)} %get-tuple-element.122.own, bf16[288,512]{1,0:T(8,128)(2,1)S(1)} %collective-permute-done.21.refs_0_), custom_call_target="tpu_custom_call" | custom-call | flops 2000000000 | tf_op jit(solution)/shard_map/sum_gate/pallas_call | solution.py:32
  79.0 1.8 %collective-permute-done.22.refs_0_ = bf16[288,256]{1,0:T(8,128)(2,1)S(1)} collective-permute-done((bf16[288,256]{1,0:T(8,128)(2,1)S(1)}, bf16[288,256]{1,0:T(8,128)(2,1)S(1)}, u32[]{:S(2)}, u32[]{:S(2)}) %collective-permute-start.22) | collective-permute-done | bytes 147488 | tf_op jit(solution)/shard_map/ppermute | solution.py:406
  80.8 0.7 sum_cand.1
  (37 shorter events, 3.6 us)
Async XLA Ops:
  1.9 12.3 %collective-permute-start = (bf16[32,512]{1,0:T(8,128)(2,1)S(1)}, bf16[32,512]{1,0:T(8,128)(2,1)S(1)}, u32[]{:S(2)}, u32[]{:S(2)}) collective-permute-start(bf16[32,512]{1,0:T(8,128)(2,1)S(1)} %get-tuple-element.69), channel_id=1, source_target_pairs={{0,1},{1,0},{2,3},{3,2},{4,5},{5,4},{6,7},{7,6},{8,9},{9,8},{10,11... | collective-permute-start | bytes 98312 | tf_op jit(solution)/shard_map/ppermute | solution.py:406
  2.4 11.7 %collective-permute-start.1 = (bf16[32,512]{1,0:T(8,128)(2,1)S(1)}, bf16[32,512]{1,0:T(8,128)(2,1)S(1)}, u32[]{:S(2)}, u32[]{:S(2)}) collective-permute-start(bf16[32,512]{1,0:T(8,128)(2,1)S(1)} %get-tuple-element.70), channel_id=1, source_target_pairs={{0,15},{1,2},{2,1},{3,4},{4,3},{5,6},{6,5},{7,8},{8,7},{9,10},{10,... | collective-permute-start | bytes 98312 | tf_op jit(solution)/shard_map/ppermute | solution.py:409
  8.1 2.5 %copy-start = (bf16[1,16,16,256]{3,2,1,0:T(8,128)(2,1)S(1)}, bf16[1,16,16,256]{3,2,1,0:T(8,128)(2,1)}, u32[]{:S(2)}) copy-start(bf16[1,16,16,256]{3,2,1,0:T(8,128)(2,1)} %param.13) | copy-start | bytes 393220
  10.6 8.3 %collective-permute-start.6 = (bf16[256,256]{1,0:T(8,128)(2,1)S(1)}, bf16[256,256]{1,0:T(8,128)(2,1)S(1)}, u32[]{:S(2)}, u32[]{:S(2)}) collective-permute-start(bf16[256,256]{1,0:T(8,128)(2,1)S(1)} %bitcast.14), channel_id=1, source_target_pairs={{0,2},{1,3},{2,0},{3,1},{4,6},{5,7},{6,4},{7,5},{8,10},{9,11},{10,... | collective-permute-start | bytes 393224 | tf_op jit(solution)/shard_map/ppermute | solution.py:406
  10.7 8.2 %collective-permute-start.7 = (bf16[256,256]{1,0:T(8,128)(2,1)S(1)}, bf16[256,256]{1,0:T(8,128)(2,1)S(1)}, u32[]{:S(2)}, u32[]{:S(2)}) collective-permute-start(bf16[256,256]{1,0:T(8,128)(2,1)S(1)} %bitcast.15), channel_id=1, source_target_pairs={{0,4},{1,5},{2,6},{3,7},{4,0},{5,1},{6,2},{7,3},{8,12},{9,13},{10,... | collective-permute-start | bytes 393224 | tf_op jit(solution)/shard_map/ppermute | solution.py:406
  10.7 8.1 %collective-permute-start.8 = (bf16[256,256]{1,0:T(8,128)(2,1)S(1)}, bf16[256,256]{1,0:T(8,128)(2,1)S(1)}, u32[]{:S(2)}, u32[]{:S(2)}) collective-permute-start(bf16[256,256]{1,0:T(8,128)(2,1)S(1)} %bitcast.16), channel_id=1, source_target_pairs={{0,6},{1,7},{2,4},{3,5},{4,2},{5,3},{6,0},{7,1},{8,14},{9,15},{10,... | collective-permute-start | bytes 393224 | tf_op jit(solution)/shard_map/ppermute | solution.py:406
  16.0 6.4 %collective-permute-start.2 = (bf16[32,256]{1,0:T(8,128)(2,1)S(1)}, bf16[32,256]{1,0:T(8,128)(2,1)S(1)}, u32[]{:S(2)}, u32[]{:S(2)}) collective-permute-start(bf16[32,256]{1,0:T(8,128)(2,1)S(1)} %get-tuple-element.83), channel_id=1, source_target_pairs={{0,1},{1,0},{2,3},{3,2},{4,5},{5,4},{6,7},{7,6},{8,9},{9,8},{10,11... | collective-permute-start | bytes 49160 | tf_op jit(solution)/shard_map/ppermute | solution.py:406
  16.0 6.4 %collective-permute-start.3 = (bf16[32,256]{1,0:T(8,128)(2,1)S(1)}, bf16[32,256]{1,0:T(8,128)(2,1)S(1)}, u32[]{:S(2)}, u32[]{:S(2)}) collective-permute-start(bf16[32,256]{1,0:T(8,128)(2,1)S(1)} %get-tuple-element.84), channel_id=1, source_target_pairs={{0,15},{1,2},{2,1},{3,4},{4,3},{5,6},{6,5},{7,8},{8,7},{9,10},{10,... | collective-permute-start | bytes 49160 | tf_op jit(solution)/shard_map/ppermute | solution.py:409
  18.9 14.3 %collective-permute-start.9 = (bf16[384,256]{1,0:T(8,128)(2,1)S(1)}, bf16[384,256]{1,0:T(8,128)(2,1)S(1)}, u32[]{:S(2)}, u32[]{:S(2)}) collective-permute-start(bf16[384,256]{1,0:T(8,128)(2,1)S(1)} %get-tuple-element.100.refs_4_), channel_id=1, source_target_pairs={{0,2},{1,3},{2,0},{3,1},{4,6},{5,7},{6,4},{7,5},{8,10},{9,11},{10,... | collective-permute-start | bytes 589832 | tf_op jit(solution)/shard_map/ppermute | solution.py:406
  20.4 12.7 %collective-permute-start.10 = (bf16[384,256]{1,0:T(8,128)(2,1)S(1)}, bf16[384,256]{1,0:T(8,128)(2,1)S(1)}, u32[]{:S(2)}, u32[]{:S(2)}) collective-permute-start(bf16[384,256]{1,0:T(8,128)(2,1)S(1)} %get-tuple-element.100.refs_4_), channel_id=1, source_target_pairs={{0,4},{1,5},{2,6},{3,7},{4,0},{5,1},{6,2},{7,3},{8,12},{9,13},{10,... | collective-permute-start | bytes 589832 | tf_op jit(solution)/shard_map/ppermute | solution.py:406
  20.7 12.5 %collective-permute-start.11 = (bf16[384,256]{1,0:T(8,128)(2,1)S(1)}, bf16[384,256]{1,0:T(8,128)(2,1)S(1)}, u32[]{:S(2)}, u32[]{:S(2)}) collective-permute-start(bf16[384,256]{1,0:T(8,128)(2,1)S(1)} %get-tuple-element.100.refs_4_), channel_id=1, source_target_pairs={{0,6},{1,7},{2,4},{3,5},{4,2},{5,3},{6,0},{7,1},{8,14},{9,15},{10,... | collective-permute-start | bytes 589832 | tf_op jit(solution)/shard_map/ppermute | solution.py:406
  25.1 5.6 %collective-permute-start.4 = (bf16[32,256]{1,0:T(8,128)(2,1)S(1)}, bf16[32,256]{1,0:T(8,128)(2,1)S(1)}, u32[]{:S(2)}, u32[]{:S(2)}) collective-permute-start(bf16[32,256]{1,0:T(8,128)(2,1)S(1)} %get-tuple-element.94), channel_id=1, source_target_pairs={{0,1},{1,0},{2,3},{3,2},{4,5},{5,4},{6,7},{7,6},{8,9},{9,8},{10,11... | collective-permute-start | bytes 49160 | tf_op jit(solution)/shard_map/ppermute | solution.py:406
  25.1 7.8 %collective-permute-start.5 = (bf16[32,256]{1,0:T(8,128)(2,1)S(1)}, bf16[32,256]{1,0:T(8,128)(2,1)S(1)}, u32[]{:S(2)}, u32[]{:S(2)}) collective-permute-start(bf16[32,256]{1,0:T(8,128)(2,1)S(1)} %get-tuple-element.95), channel_id=1, source_target_pairs={{0,15},{1,2},{2,1},{3,4},{4,3},{5,6},{6,5},{7,8},{8,7},{9,10},{10,... | collective-permute-start | bytes 49160 | tf_op jit(solution)/shard_map/ppermute | solution.py:409
  33.1 13.3 %collective-permute-start.12 = (bf16[832,256]{1,0:T(8,128)(2,1)S(1)}, bf16[832,256]{1,0:T(8,128)(2,1)S(1)}, u32[]{:S(2)}, u32[]{:S(2)}) collective-permute-start(bf16[832,256]{1,0:T(8,128)(2,1)S(1)} %get-tuple-element.106.d.d0.refs_10_), channel_id=1, source_target_pairs={{0,2},{1,3},{2,0},{3,1},{4,6},{5,7},{6,4},{7,5},{8,10},{9,11},{10,... | collective-permute-start | bytes 1277960 | tf_op jit(solution)/shard_map/ppermute | solution.py:406
  33.2 13.2 %collective-permute-start.13 = (bf16[832,256]{1,0:T(8,128)(2,1)S(1)}, bf16[832,256]{1,0:T(8,128)(2,1)S(1)}, u32[]{:S(2)}, u32[]{:S(2)}) collective-permute-start(bf16[832,256]{1,0:T(8,128)(2,1)S(1)} %get-tuple-element.106.d.d0.refs_10_), channel_id=1, source_target_pairs={{0,4},{1,5},{2,6},{3,7},{4,0},{5,1},{6,2},{7,3},{8,12},{9,13},{10,... | collective-permute-start | bytes 1277960 | tf_op jit(solution)/shard_map/ppermute | solution.py:406
  33.3 20.3 %collective-permute-start.14 = (bf16[832,256]{1,0:T(8,128)(2,1)S(1)}, bf16[832,256]{1,0:T(8,128)(2,1)S(1)}, u32[]{:S(2)}, u32[]{:S(2)}) collective-permute-start(bf16[832,256]{1,0:T(8,128)(2,1)S(1)} %get-tuple-element.106.d.d0.refs_10_), channel_id=1, source_target_pairs={{0,6},{1,7},{2,4},{3,5},{4,2},{5,3},{6,0},{7,1},{8,14},{9,15},{10,... | collective-permute-start | bytes 1277960 | tf_op jit(solution)/shard_map/ppermute | solution.py:406
  45.0 11.2 %collective-permute-start.15 = (bf16[32,512]{1,0:T(8,128)(2,1)S(1)}, bf16[32,512]{1,0:T(8,128)(2,1)S(1)}, u32[]{:S(2)}, u32[]{:S(2)}) collective-permute-start(bf16[32,512]{1,0:T(8,128)(2,1)S(1)} %get-tuple-element.109), channel_id=1, source_target_pairs={{0,1},{1,0},{2,3},{3,2},{4,5},{5,4},{6,7},{7,6},{8,9},{9,8},{10,11... | collective-permute-start | bytes 98312 | tf_op jit(solution)/shard_map/ppermute | solution.py:406
  45.0 11.2 %collective-permute-start.16 = (bf16[32,512]{1,0:T(8,128)(2,1)S(1)}, bf16[32,512]{1,0:T(8,128)(2,1)S(1)}, u32[]{:S(2)}, u32[]{:S(2)}) collective-permute-start(bf16[32,512]{1,0:T(8,128)(2,1)S(1)} %get-tuple-element.110), channel_id=1, source_target_pairs={{0,15},{1,2},{2,1},{3,4},{4,3},{5,6},{6,5},{7,8},{8,7},{9,10},{10,... | collective-permute-start | bytes 98312 | tf_op jit(solution)/shard_map/ppermute | solution.py:409
  55.5 1.8 %collective-permute-start.17 = (bf16[2,288,256]{2,1,0:T(8,128)(2,1)S(1)}, bf16[2,288,256]{2,1,0:T(8,128)(2,1)S(1)}, u32[]{:S(2)}, u32[]{:S(2)}) collective-permute-start(bf16[2,288,256]{2,1,0:T(8,128)(2,1)S(1)} %get-tuple-element.114), channel_id=1, source_target_pairs={{0,1},{1,0},{2,3},{3,2},{4,5},{5,4},{6,7},{7,6},{8,9},{9,8},{10,11... | collective-permute-start | bytes 884744 | tf_op jit(solution)/shard_map/ppermute | solution.py:406
  55.7 2.0 %collective-permute-start.18 = (bf16[2,288,256]{2,1,0:T(8,128)(2,1)S(1)}, bf16[2,288,256]{2,1,0:T(8,128)(2,1)S(1)}, u32[]{:S(2)}, u32[]{:S(2)}) collective-permute-start(bf16[2,288,256]{2,1,0:T(8,128)(2,1)S(1)} %get-tuple-element.115), channel_id=1, source_target_pairs={{0,1},{1,0},{2,3},{3,2},{4,5},{5,4},{6,7},{7,6},{8,9},{9,8},{10,11... | collective-permute-start | bytes 884744 | tf_op jit(solution)/shard_map/ppermute | solution.py:406
  57.8 20.3 %collective-permute-start.21 = (bf16[288,512]{1,0:T(8,128)(2,1)S(1)}, bf16[288,512]{1,0:T(8,128)(2,1)S(1)}, u32[]{:S(2)}, u32[]{:S(2)}) collective-permute-start(bf16[288,512]{1,0:T(8,128)(2,1)S(1)} %bitcast.20), channel_id=1, source_target_pairs={{0,8},{1,9},{2,10},{3,11},{4,12},{5,13},{6,14},{7,15},{8,0},{9,1},... | collective-permute-start | bytes 884744 | tf_op jit(solution)/shard_map/ppermute | solution.py:406
  64.1 1.4 %collective-permute-start.19 = (bf16[2,288,128]{2,1,0:T(8,128)(2,1)S(1)}, bf16[2,288,128]{2,1,0:T(8,128)(2,1)S(1)}, u32[]{:S(2)}, u32[]{:S(2)}) collective-permute-start(bf16[2,288,128]{2,1,0:T(8,128)(2,1)S(1)} %get-tuple-element.119), channel_id=1, source_target_pairs={{0,1},{1,0},{2,3},{3,2},{4,5},{5,4},{6,7},{7,6},{8,9},{9,8},{10,11... | collective-permute-start | bytes 442376 | tf_op jit(solution)/shard_map/ppermute | solution.py:406
  64.1 1.6 %collective-permute-start.20 = (bf16[2,288,128]{2,1,0:T(8,128)(2,1)S(1)}, bf16[2,288,128]{2,1,0:T(8,128)(2,1)S(1)}, u32[]{:S(2)}, u32[]{:S(2)}) collective-permute-start(bf16[2,288,128]{2,1,0:T(8,128)(2,1)S(1)} %get-tuple-element.120), channel_id=1, source_target_pairs={{0,1},{1,0},{2,3},{3,2},{4,5},{5,4},{6,7},{7,6},{8,9},{9,8},{10,11... | collective-permute-start | bytes 442376 | tf_op jit(solution)/shard_map/ppermute | solution.py:406
  65.8 15.0 %collective-permute-start.22 = (bf16[288,256]{1,0:T(8,128)(2,1)S(1)}, bf16[288,256]{1,0:T(8,128)(2,1)S(1)}, u32[]{:S(2)}, u32[]{:S(2)}) collective-permute-start(bf16[288,256]{1,0:T(8,128)(2,1)S(1)} %bitcast.21), channel_id=1, source_target_pairs={{0,8},{1,9},{2,10},{3,11},{4,12},{5,13},{6,14},{7,15},{8,0},{9,1},... | collective-permute-start | bytes 442376 | tf_op jit(solution)/shard_map/ppermute | solution.py:406

commit v4 on v3

--- a/solution.py
+++ b/solution.py
@@ -24,7 +24,7 @@
     return lax.dot_general(a, b, (((0,), (0,)), ((), ())), preferred_element_type=F32)
 
 
-def call(body, outs, *args, mib=24, scratch=(), hbm=(), pin=True, cost=0):
+def call(body, outs, *args, mib=24, scratch=(), hbm=(), pin=True, cost=0, aliases=None):
     vmem = pl.BlockSpec(memory_space=pltpu.VMEM)
     far = pl.BlockSpec(memory_space=pltpu.HBM)
     in_specs = [far if i in hbm else vmem for i in range(len(args))]
@@ -35,6 +35,7 @@
         in_specs=in_specs,
         out_specs=[vmem] * len(outs),
         scratch_shapes=list(scratch),
+        input_output_aliases=aliases or {},
         compiler_params=pltpu.CompilerParams(vmem_limit_bytes=mib * 2**20),
         cost_estimate=pl.CostEstimate(flops=cost * 10**9, bytes_accessed=0, transcendentals=0),
     )(*args)
@@ -160,7 +161,17 @@
     return dot(jnp.concatenate(cols, axis=1), jnp.concatenate(rows, axis=0))
 
 
-def gate_kernel(side, xh, rp, rn, turn, m0, m2, w, bias, sel, gate, rh, pack, s_next, s_prev, f):
+def start_loads(pairs, sems):
+    copies = [pltpu.make_async_copy(a, b, sems.at[k]) for k, (a, b) in enumerate(pairs)]
+    for copy in copies:
+        copy.start()
+    return copies
+
+
+def gate_kernel(
+    side, xh, rp, rn, turn, m0, m2, w, bias, sel, wc_in, bc_in, g_in, gate, rh, pack, s_next, s_prev, f, wc, bc, g, sems
+):
+    copies = start_loads([(wc_in, wc), (bc_in, bc), (g_in, g)], sems)
     c = xh.shape[1] // 2
     cells, rim = side * side, 4 * side
     strips = dot(turn[...], jnp.concatenate([rp[...], rn[...]], axis=0)).astype(BF)
@@ -175,14 +186,12 @@
     picked = dot(sel[...], reset_h).astype(BF)
     s_next[...] = picked[: rim // 2]
     s_prev[...] = picked[rim // 2 :]
+    for copy in copies:
+        copy.wait()
 
 
 def load_kernel(n, *refs):
-    sems = refs[-1]
-    copies = [pltpu.make_async_copy(refs[k], refs[n + k], sems.at[k]) for k in range(n)]
-    for copy in copies:
-        copy.start()
-    for copy in copies:
+    for copy in start_loads([(refs[k], refs[n + k]) for k in range(n)], refs[-1]):
         copy.wait()
 
 
@@ -254,14 +263,11 @@
             acc[b, rows, c:] += dot_nt(d[cells : 2 * cells], wg[t, c:, :c])
 
 
-def reset_kernel(side, inner, rp, rn, place, gate, h, g, d_cu, d, direct):
+def reset_kernel(side, inner, rp, rn, place, gate, h, g, d, direct):
     c = g.shape[1]
     d_rh = inner[...] + dot(place[...], jnp.concatenate([rp[...], rn[...]], axis=0))
     update, reset = gate[:, :c], gate[:, c:]
-    cells = side * side
-    d[: 2 * cells] = d_cu[: 2 * cells]
-    d[3 * cells :] = d_cu[2 * cells :]
-    d[2 * cells : 3 * cells] = (d_rh * h[:, c:].astype(F32) * reset * (1.0 - reset)).astype(BF)
+    d[...] = (d_rh * h[:, c:].astype(F32) * reset * (1.0 - reset)).astype(BF)
     direct[...] = g[...].astype(F32) * (1.0 - update) + d_rh * reset
 
 
@@ -269,8 +275,7 @@
     c = d.shape[1]
     rim = 4 * side
     acc[...] = early[...]
-    cells = side * side
-    spread(side, acc, d[2 * cells : 3 * cells], w, 0, 2 * c, c, 2 * c, False)
+    spread(side, acc, d[...], w, 0, 2 * c, c, 2 * c, False)
     own, edge = gather_frame(side, acc)
     inner[:, :c] = own[:, :c]
     inner[:, c:] = own[:, c:] + direct[...]
@@ -287,21 +292,29 @@
 
 
 def near_reset_kernel(side, *refs):
-    x, packs, (m0, m2, w, bias, out, f) = refs[1:4], refs[5:8], refs[8:]
+    x, packs, (m0, m2, w, bias, taps_in, out, taps, f, sems) = refs[1:4], refs[5:8], refs[8:]
+    (copy,) = start_loads([(taps_in, taps)], sems)
     cells, rim, c = side * side, 4 * side, out.shape[2]
     for n in range(3):
-        h = packs[n][:cells]
-        tile = jnp.concatenate([x[n][...], h], axis=1)
+        tile = jnp.concatenate([x[n][...], packs[n][:cells]], axis=1)
         strips = jnp.concatenate([packs[n][cells : cells + rim], packs[n][cells + rim :]], axis=1)
-        frames(side, tile, strips, m0, m2, f)
-        reset = jax.nn.sigmoid(conv(side, f, w, 0, 2 * c, c, 2 * c) + bias[:, c:])
-        out[n] = (reset * h.astype(F32)).astype(BF)
+        frames(side, tile, strips, m0, m2, f.at[n])
+    cols = [
+        jnp.concatenate([f[n, b, a * side : a * side + cells, :] for n in range(3)], axis=0)
+        for a in range(3)
+        for b in range(3)
+    ]
+    rows = [w[t, :, c:] for t in range(9)]
+    reset = jax.nn.sigmoid(dot(jnp.concatenate(cols, axis=1), jnp.concatenate(rows, axis=0)) + bias[:, c:])
+    for n in range(3):
+        out[n] = (reset[n * cells : (n + 1) * cells] * packs[n][:cells].astype(F32)).astype(BF)
+    copy.wait()
 
 
 def lhs_kernel(side, rows, tiles, cand, *refs):
-    x, packs, more = refs[:4], refs[4:8], refs[8:-3]
+    x, packs, more = refs[:4], refs[4:8], refs[8:-4]
     me = lax.axis_index("tile")
-    taps, out, src = refs[-3:]
+    taps, out, src, turned = refs[-4:]
     cells, rim = side * side, 4 * side
     c = packs[0].shape[1]
     per_tap = 2 * c // 128
@@ -316,53 +329,69 @@
             elif cand:
                 rh, rh_near, ds = more[0], more[1], more[2:]
                 src[k, :cells, lanes] = rh[:, col] if n == 0 else rh_near[n - 1, :, col]
-                src[k, cells:, lanes] = ds[n][3 * cells :, col]
+                src[k, cells:, lanes] = ds[n][2 * cells :, col]
             else:
                 src[k, :cells, lanes] = packs[n][:cells, col]
                 src[k, cells:, lanes] = packs[n][cells + rim :, col]
+    for k in range(per_tap):
+        turned[k] = src[k].T
     for t in range(out.shape[0]):
         target = me ^ (8 * (t // 2) + t % 2)
         for n in range(out.shape[1] // 128):
             block = jnp.minimum(target * rows // 128 + n, 9 * per_tap - 1)
-            part = dot_tn(src[block % per_tap], taps[block // per_tap]).astype(BF)
+            part = dot(turned[block % per_tap], taps[block // per_tap]).astype(BF)
             for k in range(4):
                 out[t, n * 128 : (n + 1) * 128, k * cells : (k + 1) * cells] = part[k * 128 : (k + 1) * 128]
 
 
-def weight_kernel(side, rows, parts, lhs, d0, d1, d2, d3, keep, *refs):
-    sends, acc = refs[:-1], refs[-1]
-    cells = side * side
+def weight_kernel(side, rows, parts, *refs):
+    n = len(parts)
+    lhs, ds, keep, sends, acc = refs[:n], refs[n : n + 4], refs[n + 4], refs[n + 5 : -1], refs[-1]
+    cells = side * side
+    c, width = ds[0].shape[1], sends[0].shape[2]
     me = lax.axis_index("tile")
-    width = sends[0].shape[2]
-    right = [jnp.concatenate([d[k * cells : (k + 1) * cells] for k in parts], axis=1) for d in (d0, d1, d2, d3)]
-    right = jnp.concatenate(right, axis=0)
-    for t in range(lhs.shape[0]):
+    right = [jnp.concatenate([d[k * cells : (k + 1) * cells] for d in ds], axis=0) for k in parts]
+    for t in range(lhs[0].shape[0]):
         target = me ^ (8 * (t // 2) + t % 2)
         first = pl.multiple_of(target * rows % 128, 8)
-        acc[t % 2] = dot(lhs[t], right)
-        part = acc[t % 2, pl.ds(first, rows), :]
-        if t % 2 == 0:
-            keep[t // 2] = part
-        else:
-            for k, send in enumerate(sends):
-                send[t // 2] = part[:, k * width : (k + 1) * width].astype(BF)
+        for k in range(n):
+            acc[k, t % 2] = dot(lhs[k][t], right[k])
+            part = acc[k, t % 2, pl.ds(first, rows), :]
+            if t % 2 == 0:
+                keep[t // 2, :, k * c : (k + 1) * c] = part
+            else:
+                for j in range(c // width):
+                    sends[k * (c // width) + j][t // 2] = part[:, j * width : (j + 1) * width].astype(BF)
 
 
 def pair_kernel(keep, *refs):
-    got, (own, far) = refs[:-2], refs[-2:]
-    width = got[0].shape[2]
-    for k, part in enumerate(got):
-        at = slice(k * width, (k + 1) * width)
-        own[:, at] = keep[0, :, at] + part[0].astype(F32)
+    gots, (own, far) = refs[:-2], refs[-2:]
+    c = gots[0].shape[2]
+    for k, got in enumerate(gots):
+        at = slice(k * c, (k + 1) * c)
+        own[:, at] = keep[0, :, at] + got[0].astype(F32)
         for m in range(1, keep.shape[0]):
-            far[m - 1, :, at] = (keep[m, :, at] + part[m].astype(F32)).astype(BF)
-
-
-def sum_kernel(own, *refs):
-    total = own[...]
-    for r in refs[:-1]:
+            far[m - 1, :, at] = (keep[m, :, at] + got[m].astype(F32)).astype(BF)
+
+
+def sum_kernel(*refs):
+    parts, (cand, update) = refs[:-2], refs[-2:]
+    c = cand.shape[1]
+    total = parts[0][...]
+    for r in parts[1:]:
         total += r[...].astype(F32)
-    refs[-1][...] = total
+    cand[...] = total[:, :c]
+    update[...] = total[:, c:]
+
+
+def sum_reset_kernel(update, *refs):
+    parts, gate = refs[:-1], refs[-1]
+    c = update.shape[1]
+    total = parts[0][...]
+    for r in parts[1:]:
+        total += r[...].astype(F32)
+    gate[:, :c] = update[...]
+    gate[:, c:] = total
 
 
 def shards(
@@ -411,27 +440,34 @@
     def near(u):
         return [u] + [swap(u, k) for k in (2, 4, 6)]
 
-    def lhs_of(name, cand, *args):
+    def lhs_of(name, cand, *args, cost=0):
         return run(
             name, functools.partial(lhs_kernel, side, rows, tiles, cand),
             [((2 * groups, blocks, 4 * cells), BF)],
             *args, taps_v,
-            scratch=[pltpu.VMEM((2 * c // 128, cells + rim, 512), BF)],
+            scratch=[
+                pltpu.VMEM((2 * c // 128, cells + rim, 512), BF),
+                pltpu.VMEM((2 * c // 128, 512, cells + rim), BF),
+            ],
+            cost=cost,
         )[0]
 
-    def products(name, parts, lhs, ds):
+    def products(name, parts, lhs, ds, cuts=1, cost=0):
         n = len(parts)
         keep, *sends = run(
             name, functools.partial(weight_kernel, side, rows, parts),
-            [((groups, rows, n * c), F32)] + [((groups, rows, n * c // 2), BF)] * 2,
-            lhs, *ds,
-            scratch=[pltpu.VMEM((2, blocks, n * c), F32)],
+            [((groups, rows, n * c), F32)] + [((groups, rows, c // cuts), BF)] * (n * cuts),
+            *lhs, *ds,
+            scratch=[pltpu.VMEM((n, 2, blocks, c), F32)],
+            cost=cost,
         )
         return keep, [swap(u, 1) for u in sends]
 
-    def pair(name, keep, got):
+    def pair(name, keep, gots, cost=0):
         n = keep.shape[2]
-        own, far = run(name, pair_kernel, [((rows, n), F32), ((groups - 1, rows, n), BF)], keep, *got)
+        own, far = run(
+            name, pair_kernel, [((rows, n), F32), ((groups - 1, rows, n), BF)], keep, *gots, cost=cost
+        )
         return [own] + [swap(far[k - 1], 8 * k) for k in range(1, groups)]
 
     xh, s1n, s1p, sel, place, turn, rim_sel = run(
@@ -455,9 +491,9 @@
         ],
     )
     r1p, r1n = exchange(s1n, s1p)
+    x_near = near(x)
     wg_v, m0, m2, bg_v = load("load_gate", wg, m0, m2, bg)
-    x_near = near(after(x, bg_v))
-    gate, rh, pack, s2n, s2p, f = run(
+    gate, rh, pack, s2n, s2p, f, wc_v, bc_v, g_v = run(
         "gate", functools.partial(gate_kernel, side),
         [
             ((cells, 2 * c), F32),
@@ -466,11 +502,14 @@
             ((half, c), BF),
             ((half, c), BF),
             ((3, band, 2 * c), BF),
+            (wc.shape, BF),
+            (bc.shape, F32),
+            (g.shape, BF),
         ],
-        xh, r1p, r1n, turn, m0, m2, wg_v, bg_v, sel, cost=5,
+        after(xh, *x_near), r1p, r1n, turn, m0, m2, wg_v, bg_v, sel, wc, bc, g,
+        hbm=(9, 10, 11), scratch=[pltpu.SemaphoreType.DMA((3,))], cost=5,
     )
     r2p, r2n = exchange(s2n, s2p)
-    wc_v, bc_v, g_v = load("load_cand", wc, bc, g)
     pack_near = near(after(pack, *x_near))
     (acc_x,) = run("cand_x", functools.partial(cand_x_kernel, side), [((cells, c), F32)], f, wc_v, bc_v)
     d_cu, _ = run(
@@ -484,38 +523,41 @@
         d_cu, wc_v, rim_sel,
     )
     r3p, r3n = exchange(s3n, s3p)
+    d_near = near(after(d_cu, s3n, *pack_near))
+    rh_near, taps_v = run(
+        "near_reset", functools.partial(near_reset_kernel, side), [((3, cells, c), BF), (taps.shape, BF)],
+        *x_near, *pack_near, m0, m2, wg_v, bg_v, taps,
+        hbm=(12,),
+        scratch=[pltpu.VMEM((3, 3, band, 2 * c), BF), pltpu.SemaphoreType.DMA((1,))],
+    )
+    lhs_gate = lhs_of("lhs_gate", False, *x_near, *pack_near, cost=5)
+    d_r, direct = run(
+        "reset", functools.partial(reset_kernel, side),
+        [((cells, c), BF), ((cells, c), F32)],
+        inner_rh, r3p, r3n, place, gate, xh, g_v,
+    )
+    r_near = near(d_r)
+    lhs_cand = lhs_of("lhs_cand", True, *x_near, *pack_near, rh, rh_near, *d_near)
+    keep_f, gots_f = products("weights_first", (0, 1), [lhs_cand, lhs_gate], d_near, cost=0)
+    keep, gots = products("weights_reset", (0,), [lhs_gate], r_near, cuts=2, cost=4)
+    parts = pair("pair_first", keep_f, gots_f, cost=0)
+    parts_r = pair("pair_reset", keep, gots, cost=0)
     (early,) = run(
         "back_early", functools.partial(back_early_kernel, side), [((3, band, 2 * c), F32)], d_cu, wc_v, wg_v
-    )
-    (taps_v,) = load("load_taps", taps)
-    d, direct = run(
-        "reset", functools.partial(reset_kernel, side),
-        [((3 * cells + rim, c), BF), ((cells, c), F32)],
-        inner_rh, r3p, r3n, place, gate, xh, g_v, d_cu,
-    )
-    d_near = near(after(d, *pack_near))
-    lhs_gate = lhs_of("lhs_gate", False, *x_near, *pack_near)
-    (rh_near,) = run(
-        "near_reset", functools.partial(near_reset_kernel, side), [((3, cells, c), BF)],
-        *x_near, *pack_near, m0, m2, wg_v, bg_v,
-        scratch=[pltpu.VMEM((3, band, 2 * c), BF)],
     )
     inner, s4n, s4p, _ = run(
         "back_gate", functools.partial(back_gate_kernel, side),
         [((cells, 2 * c), F32), ((half, 2 * c), BF), ((half, 2 * c), BF), ((3, band, 2 * c), F32)],
-        early, d, wg_v, direct, rim_sel,
+        early, d_r, wg_v, direct, rim_sel, cost=0,
     )
     r4p, r4n = exchange(s4n, s4p)
-    keep_g, got_g = products("weights_gate", (1, 2), lhs_gate, d_near)
+    grad_w_cand, sum_u = run(
+        "sum_first", sum_kernel, [((rows, c), F32), ((rows, c), F32)], *parts, pin=False, cost=2
+    )
     gx, gh = run(
-        "final", final_kernel, [((cells, c), BF), ((cells, c), BF)], inner, r4p, r4n, place, pin=False, cost=5
-    )
-    parts_g = pair("pair_gate", keep_g, got_g)
-    lhs_cand = lhs_of("lhs_cand", True, *x_near, *pack_near, rh, rh_near, *d_near)
-    keep_c, got_c = products("weights_cand", (0,), lhs_cand, d_near)
-    parts_c = pair("pair_cand", keep_c, got_c)
-    (grad_w_gate,) = run("sum_gate", sum_kernel, [((rows, 2 * c), F32)], *parts_g, pin=False, cost=2)
-    (grad_w_cand,) = run("sum_cand", sum_kernel, [((rows, c), F32)], *parts_c, pin=False)
+        "final", final_kernel, [((cells, c), BF), ((cells, c), BF)], inner, r4p, r4n, place, pin=False, cost=0
+    )
+    (grad_w_gate,) = run("sum_reset", sum_reset_kernel, [((rows, 2 * c), F32)], sum_u, *parts_r, pin=False)
     shape = (1, side, side, c)
     return gx.reshape(shape), gh.reshape(shape), grad_w_gate, grad_w_cand
 

time: 81.7 us -> 76.5 us (0.936)
  waiting for transfers between devices: 25.2 us -> 15.9 us
  starting transfers between devices: 26.3 us -> 33.8 us
  Pallas kernels: 29.2 us -> 25.8 us
    ppermute x19 -> x22, waiting for transfers between devices: 23 us -> 15.9 us  [swap(): return lax.ppermute(u, 'tile', [(i, i ^ k) for i in range(tiles)])]
    ppermute x19 -> x22, starting transfers between devices: 15.6 us -> 21.3 us  [swap(): return lax.ppermute(u, 'tile', [(i, i ^ k) for i in range(tiles)])]
    pallas_call x21 -> x19, Pallas kernels: 29.2 us -> 25.8 us  [call(): pl.pallas_call(body, out_shape=[pltpu.VMEM(s, d) if pin else jax.ShapeDty...]
    ppermute x4, waiting for transfers between devices: 2.19 us -> 0.01 us  [exchange(): return (swap(s_first, 1), lax.ppermute(s_second, 'tile', cross))]
    ppermute x4, starting transfers between devices: 10.7 us -> 12.5 us  [exchange(): return (swap(s_first, 1), lax.ppermute(s_second, 'tile', cross))]
  transfers between devices with their start and end apart: 23 -> 26, of which waited for: 8 -> 9; matrix products, arithmetic and copies ran while one was open for 0% -> 0% of each run, Pallas kernels for 33% -> 30%
where the time goes in v4:
time: 76.5 us; the launch traced here: 76.3 us
  starting transfers between devices  33.8 us (44%)
  Pallas kernels  25.8 us (34%)
  waiting for transfers between devices  15.9 us (21%)
  between operations  0.85 us (1%)
    pallas_call x19, Pallas kernels, call(): pl.pallas_call(body, out_shape=[pltpu.VMEM(s, d) if pin else jax.ShapeDty...  25.8 us
    ppermute x22, starting transfers between devices, swap(): return lax.ppermute(u, 'tile', [(i, i ^ k) for i in range(tiles)])  21.3 us
    ppermute x22, waiting for transfers between devices, swap(): return lax.ppermute(u, 'tile', [(i, i ^ k) for i in range(tiles)])  15.9 us
    ppermute x4, starting transfers between devices, exchange(): return (swap(s_first, 1), lax.ppermute(s_second, 'tile', cross))  12.5 us
  transfers between devices with their start and end apart: 26, of which 9 were waited for; matrix products, arithmetic and copies ran while one was open for 0% of the time, Pallas kernels for 30%

profile of v4, /device:TPU:0, one launch (start us, length us, event | category | flops | bytes accessed | tf_op | source)
XLA Modules:
  0.0 76.3 jit_solution(17367074957661395902)
XLA Ops:
  0.6 4.0 %collective-permute-start.2 = (bf16[256,256]{1,0:T(8,128)(2,1)}, bf16[256,256]{1,0:T(8,128)(2,1)S(1)}, u32[]{:S(2)}, u32[]{:S(2)}) collective-permute-start(bf16[256,256]{1,0:T(8,128)(2,1)} %bitcast.13), channel_id=1, source_target_pairs={{0,6},{1,7},{2,4},{3,5},{4,2},{5,3},{6,0},{7,1},{8,14},{9,15},{10,... | collective-permute-start | bytes 393224 | tf_op jit(solution)/shard_map/ppermute | solution.py:435
  5.3 1.2 %route.1 = (bf16[256,512]{1,0:T(8,128)(2,1)S(1)}, bf16[32,512]{1,0:T(8,128)(2,1)S(1)}, bf16[32,512]{1,0:T(8,128)(2,1)S(1)}, bf16[64,256]{1,0:T(8,128)(2,1)S(1)},...) custom-call(s32[4,16]{1,0:T(4,128)} %bitcast.24, s32[4,16]{1,0:T(4,128)} %bitcast.25, ...), custom_call_target="tpu_custom_call" | custom-call | tf_op jit(solution)/shard_map/route/pallas_call | solution.py:32
  6.6 5.0 %collective-permute-start.4 = (bf16[32,512]{1,0:T(8,128)(2,1)S(1)}, bf16[32,512]{1,0:T(8,128)(2,1)S(1)}, u32[]{:S(2)}, u32[]{:S(2)}) collective-permute-start(bf16[32,512]{1,0:T(8,128)(2,1)S(1)} %get-tuple-element.73), channel_id=1, source_target_pairs={{0,15},{1,2},{2,1},{3,4},{4,3},{5,6},{6,5},{7,8},{8,7},{9,10},{10,... | collective-permute-start | bytes 98312 | tf_op jit(solution)/shard_map/ppermute | solution.py:438
  11.6 2.5 %load_gate.1 = (bf16[9,512,512]{2,1,0:T(8,128)(2,1)S(1)}, bf16[288,320]{1,0:T(8,128)(2,1)S(1)}, bf16[288,320]{1,0:T(8,128)(2,1)S(1)}, f32[1,512]{1,0:T(1,128)S(1)}) custom-call(bf16[9,512,512]{2,1,0:T(8,128)(2,1)} %bitcast.22, bf16[288,320]{1,0:T(8,128)(2,1)} %constant.6.clone.refs_1_, bf16[288,320]{1,0:T(8,128)(2,1)} %constant.7.clone.refs_2_, ...), custom_call_target="tpu_custom_call" | custom-call | tf_op jit(solution)/shard_map/load_gate/pallas_call | solution.py:32
  14.1 1.9 %gate.1 = (f32[256,512]{1,0:T(8,128)S(1)}, bf16[256,256]{1,0:T(8,128)(2,1)S(1)}, bf16[384,256]{1,0:T(8,128)(2,1)S(1)}, bf16[32,256]{1,0:T(8,128)(2,1)S(1)}, bf16...) custom-call(bf16[256,512]{1,0:T(8,128)(2,1)S(1)} %get-tuple-element., ...), custom_call_target="tpu_custom_call" | custom-call | flops 5000000000 | tf_op jit(solution)/shard_map/gate/pallas_call | solution.py:32
  16.2 3.6 %collective-permute-start.6 = (bf16[32,256]{1,0:T(8,128)(2,1)S(1)}, bf16[32,256]{1,0:T(8,128)(2,1)S(1)}, u32[]{:S(2)}, u32[]{:S(2)}) collective-permute-start(bf16[32,256]{1,0:T(8,128)(2,1)S(1)} %get-tuple-element.86), channel_id=1, source_target_pairs={{0,15},{1,2},{2,1},{3,4},{4,3},{5,6},{6,5},{7,8},{8,7},{9,10},{10,... | collective-permute-start | bytes 49160 | tf_op jit(solution)/shard_map/ppermute | solution.py:438
  19.7 3.5 %collective-permute-start.7 = (bf16[384,256]{1,0:T(8,128)(2,1)S(1)}, bf16[384,256]{1,0:T(8,128)(2,1)S(1)}, u32[]{:S(2)}, u32[]{:S(2)}) collective-permute-start(bf16[384,256]{1,0:T(8,128)(2,1)S(1)} %get-tuple-element.94.refs_4_), channel_id=1, source_target_pairs={{0,2},{1,3},{2,0},{3,1},{4,6},{5,7},{6,4},{7,5},{8,10},{9,11},{10,... | collective-permute-start | bytes 589832 | tf_op jit(solution)/shard_map/ppermute | solution.py:435
  23.7 1.2 %cand.1 = (bf16[576,256]{1,0:T(8,128)(2,1)S(1)}, bf16[3,288,256]{2,1,0:T(8,128)(2,1)}) custom-call(f32[256,256]{1,0:T(8,128)S(1)} %cand_x.1.acc, bf16[256,256]{1,0:T(8,128)(2,1)S(1)} %get-tuple-element.84.rh.refs_8_, bf16[32,256]{1,0:T(8,128)(2,1)S(1)} %collective-permute-done.5.rp, bf16[32,256]{1,0:T(8,128)(2,1)S(1)} %collective-permute-done.6.rn, ...), custom_call_target="tpu_custom_call" | custom-call | flops 3000000000 | tf_op jit(solution)/shard_map/cand/pallas_call | solution.py:32
  24.9 1.5 %back_rh.1 = (f32[256,256]{1,0:T(8,128)S(1)}, bf16[32,256]{1,0:T(8,128)(2,1)S(1)}, bf16[32,256]{1,0:T(8,128)(2,1)S(1)}, f32[3,288,256]{2,1,0:T(8,128)}) custom-call(bf16[576,256]{1,0:T(8,128)(2,1)S(1)} %get-tuple-element.116.d.refs_10_.refs_2_, bf16[9,512,256]{2,1,0:T(8,128)(2,1)S(1)} %get-tuple-element.82.w.wc, bf16[64,544]{1,0:T(8,128)(2,1)S(1)} %get-tuple-element.90.rim_sel), custom_call_target="tpu_custom_call" | custom-call | tf_op jit(solution)/shard_map/back_rh/pallas_call | solution.py:32
  26.4 2.2 %collective-permute-start.11 = (bf16[32,256]{1,0:T(8,128)(2,1)S(1)}, bf16[32,256]{1,0:T(8,128)(2,1)S(1)}, u32[]{:S(2)}, u32[]{:S(2)}) collective-permute-start(bf16[32,256]{1,0:T(8,128)(2,1)S(1)} %get-tuple-element.100), channel_id=1, source_target_pairs={{0,15},{1,2},{2,1},{3,4},{4,3},{5,6},{6,5},{7,8},{8,7},{9,10},{10,... | collective-permute-start | bytes 49160 | tf_op jit(solution)/shard_map/ppermute | solution.py:438
  28.8 1.5 %collective-permute-start.14 = (bf16[576,256]{1,0:T(8,128)(2,1)S(1)}, bf16[576,256]{1,0:T(8,128)(2,1)S(1)}, u32[]{:S(2)}, u32[]{:S(2)}) collective-permute-start(bf16[576,256]{1,0:T(8,128)(2,1)S(1)} %get-tuple-element.116.d.refs_10_.refs_2_), channel_id=1, source_target_pairs={{0,6},{1,7},{2,4},{3,5},{4,2},{5,3},{6,0},{7,1},{8,14},{9,15},{10,... | collective-permute-start | bytes 884744 | tf_op jit(solution)/shard_map/ppermute | solution.py:435
  30.9 1.4 %collective-permute-start.12 = (bf16[576,256]{1,0:T(8,128)(2,1)S(1)}, bf16[576,256]{1,0:T(8,128)(2,1)S(1)}, u32[]{:S(2)}, u32[]{:S(2)}) collective-permute-start(bf16[576,256]{1,0:T(8,128)(2,1)S(1)} %get-tuple-element.116.d.refs_10_.refs_2_), channel_id=1, source_target_pairs={{0,2},{1,3},{2,0},{3,1},{4,6},{5,7},{6,4},{7,5},{8,10},{9,11},{10,... | collective-permute-start | bytes 884744 | tf_op jit(solution)/shard_map/ppermute | solution.py:435
  32.2 2.9 %near_reset.1 = (bf16[3,256,256]{2,1,0:T(8,128)(2,1)S(1)}, bf16[9,320,256]{2,1,0:T(8,128)(2,1)S(1)}) custom-call(bf16[256,256]{1,0:T(8,128)(2,1)S(1)} %bitcast.17, bf16[256,256]{1,0:T(8,128)(2,1)S(1)} %collective-permute-done.refs_1_, bf16[256,256]{1,0:T(8,128)(2,1)S(1)} %collective-permute-done.1.refs_2_, ...), custom_call_target="tpu_custom_call" | custom-call | tf_op jit(solution)/shard_map/near_reset/pallas_call | solution.py:32
  35.2 2.3 %lhs_gate.1.refs_1_.refs_0_ = bf16[4,384,1024]{2,1,0:T(8,128)(2,1)S(1)} custom-call(bf16[256,256]{1,0:T(8,128)(2,1)S(1)} %bitcast.18, bf16[256,256]{1,0:T(8,128)(2,1)S(1)} %collective-permute-done.refs_1_, bf16[256,256]{1,0:T(8,128)(2,1)S(1)} %collective-permute-done.1.refs_2_, bf16[256,256]{1,0:T(8,128)(2,1)S(1)} %collective-permute-done.2.refs_3_, ...), custom_call_target="tpu_custom_call" | custom-call | flops 5000000000 | tf_op jit(solution)/shard_map/lhs_gate/pallas_call | solution.py:32
  37.7 1.6 %collective-permute-start.17 = (bf16[256,256]{1,0:T(8,128)(2,1)S(1)}, bf16[256,256]{1,0:T(8,128)(2,1)S(1)}, u32[]{:S(2)}, u32[]{:S(2)}) collective-permute-start(bf16[256,256]{1,0:T(8,128)(2,1)S(1)} %get-tuple-element.102.refs_1_.d), channel_id=1, source_target_pairs={{0,6},{1,7},{2,4},{3,5},{4,2},{5,3},{6,0},{7,1},{8,14},{9,15},{10,... | collective-permute-start | bytes 393224 | tf_op jit(solution)/shard_map/ppermute | solution.py:435
  39.9 1.4 %collective-permute-start.15 = (bf16[256,256]{1,0:T(8,128)(2,1)S(1)}, bf16[256,256]{1,0:T(8,128)(2,1)S(1)}, u32[]{:S(2)}, u32[]{:S(2)}) collective-permute-start(bf16[256,256]{1,0:T(8,128)(2,1)S(1)} %get-tuple-element.102.refs_1_.d), channel_id=1, source_target_pairs={{0,2},{1,3},{2,0},{3,1},{4,6},{5,7},{6,4},{7,5},{8,10},{9,11},{10,... | collective-permute-start | bytes 393224 | tf_op jit(solution)/shard_map/ppermute | solution.py:435
  41.3 3.8 %collective-permute-done.13.refs_12_.refs_4_ = bf16[576,256]{1,0:T(8,128)(2,1)S(1)} collective-permute-done((bf16[576,256]{1,0:T(8,128)(2,1)S(1)}, bf16[576,256]{1,0:T(8,128)(2,1)S(1)}, u32[]{:S(2)}, u32[]{:S(2)}) %collective-permute-start.13) | collective-permute-done | bytes 294944 | tf_op jit(solution)/shard_map/ppermute | solution.py:435
  45.1 0.8 %collective-permute-done.12.refs_11_.refs_3_ = bf16[576,256]{1,0:T(8,128)(2,1)S(1)} collective-permute-done((bf16[576,256]{1,0:T(8,128)(2,1)S(1)}, bf16[576,256]{1,0:T(8,128)(2,1)S(1)}, u32[]{:S(2)}, u32[]{:S(2)}) %collective-permute-start.12) | collective-permute-done | bytes 294944 | tf_op jit(solution)/shard_map/ppermute | solution.py:435
  45.9 2.3 %lhs_cand.1.refs_0_ = bf16[4,384,1024]{2,1,0:T(8,128)(2,1)S(1)} custom-call(bf16[256,256]{1,0:T(8,128)(2,1)S(1)} %bitcast.19, bf16[256,256]{1,0:T(8,128)(2,1)S(1)} %collective-permute-done.refs_1_, bf16[256,256]{1,0:T(8,128)(2,1)S(1)} %collective-permute-done.1.refs_2_, bf16[256,256]{1,0:T(8,128)(2,1)S(1)} %collective-permute-done.2.refs_3_, ...), custom_call_target="tpu_custom_call" | custom-call | tf_op jit(solution)/shard_map/lhs_cand/pallas_call | solution.py:32
  48.2 2.1 %weights_first.1 = (f32[2,288,512]{2,1,0:T(8,128)S(1)}, bf16[2,288,256]{2,1,0:T(8,128)(2,1)S(1)}, bf16[2,288,256]{2,1,0:T(8,128)(2,1)S(1)}) custom-call(bf16[4,384,1024]{2,1,0:T(8,128)(2,1)S(1)} %lhs_cand.1.refs_0_, bf16[4,384,1024]{2,1,0:T(8,128)(2,1)S(1)} %lhs_gate.1.refs_1_.refs_0_, bf16[576,256]{1,0:T(8,128)(2,1)S(1)} %get-tuple-element.116.d.refs_10_.refs_2_, ...), custom_call_target="tpu_custom_call" | custom-call | tf_op jit(solution)/shard_map/weights_first/pallas_call | solution.py:32
  50.9 1.3 %weights_reset.1 = (f32[2,288,256]{2,1,0:T(8,128)S(1)}, bf16[2,288,128]{2,1,0:T(8,128)(2,1)S(1)}, bf16[2,288,128]{2,1,0:T(8,128)(2,1)S(1)}) custom-call(bf16[4,384,1024]{2,1,0:T(8,128)(2,1)S(1)} %lhs_gate.1.refs_1_.refs_0_, bf16[256,256]{1,0:T(8,128)(2,1)S(1)} %get-tuple-element.102.refs_1_.d, bf16[256,256]{1,0:T(8,128)(2,1)S(1)} %collective-permute-done.15.refs_2_, ...), custom_call_target="tpu_custom_call" | custom-call | flops 4000000000 | tf_op jit(solution)/shard_map/weights_reset/pallas_call | solution.py:32
  52.4 2.6 %collective-permute-start.22 = (bf16[288,512]{1,0:T(8,128)(2,1)S(1)}, bf16[288,512]{1,0:T(8,128)(2,1)S(1)}, u32[]{:S(2)}, u32[]{:S(2)}) collective-permute-start(bf16[288,512]{1,0:T(8,128)(2,1)S(1)} %bitcast.20), channel_id=1, source_target_pairs={{0,8},{1,9},{2,10},{3,11},{4,12},{5,13},{6,14},{7,15},{8,0},{9,1},... | collective-permute-start | bytes 884744 | tf_op jit(solution)/shard_map/ppermute | solution.py:435
  55.5 0.9 %collective-permute-done.20.refs_0_ = bf16[2,288,128]{2,1,0:T(8,128)(2,1)S(1)} collective-permute-done((bf16[2,288,128]{2,1,0:T(8,128)(2,1)S(1)}, bf16[2,288,128]{2,1,0:T(8,128)(2,1)S(1)}, u32[]{:S(2)}, u32[]{:S(2)}) %collective-permute-start.20) | collective-permute-done | bytes 147488 | tf_op jit(solution)/shard_map/ppermute | solution.py:435
  56.7 1.2 %back_early.1.early = f32[3,288,512]{2,1,0:T(8,128)S(1)} custom-call(bf16[576,256]{1,0:T(8,128)(2,1)S(1)} %get-tuple-element.116.d.refs_10_.refs_2_, bf16[9,512,256]{2,1,0:T(8,128)(2,1)S(1)} %get-tuple-element.82.w.wc, bf16[9,512,512]{2,1,0:T(8,128)(2,1)S(1)} %get-tuple-element.70.w.refs_10_.wg), custom_call_target="tpu_custom_call" | custom-call | tf_op jit(solution)/shard_map/back_early/pallas_call | solution.py:32
  57.8 2.1 %back_gate.1 = (f32[256,512]{1,0:T(8,128)S(1)}, bf16[32,512]{1,0:T(8,128)(2,1)S(1)}, bf16[32,512]{1,0:T(8,128)(2,1)S(1)}, f32[3,288,512]{2,1,0:T(8,128)}) custom-call(f32[3,288,512]{2,1,0:T(8,128)S(1)} %back_early.1.early, bf16[256,256]{1,0:T(8,128)(2,1)S(1)} %get-tuple-element.102.refs_1_.d, bf16[9,512,512]{2,1,0:T(8,128)(2,1)S(1)} %get-tuple-element.70.w.refs_10_.wg, ...), custom_call_target="tpu_custom_call" | custom-call | tf_op jit(solution)/shard_map/back_gate/pallas_call | solution.py:32
  60.3 1.8 %collective-permute-start.24 = (bf16[32,512]{1,0:T(8,128)(2,1)S(1)}, bf16[32,512]{1,0:T(8,128)(2,1)S(1)}, u32[]{:S(2)}, u32[]{:S(2)}) collective-permute-start(bf16[32,512]{1,0:T(8,128)(2,1)S(1)} %get-tuple-element.124), channel_id=1, source_target_pairs={{0,15},{1,2},{2,1},{3,4},{4,3},{5,6},{6,5},{7,8},{8,7},{9,10},{10,... | collective-permute-start | bytes 98312 | tf_op jit(solution)/shard_map/ppermute | solution.py:438
  62.0 2.0 %collective-permute-start.25 = (bf16[288,256]{1,0:T(8,128)(2,1)S(1)}, bf16[288,256]{1,0:T(8,128)(2,1)S(1)}, u32[]{:S(2)}, u32[]{:S(2)}) collective-permute-start(bf16[288,256]{1,0:T(8,128)(2,1)S(1)} %bitcast.21), channel_id=1, source_target_pairs={{0,8},{1,9},{2,10},{3,11},{4,12},{5,13},{6,14},{7,15},{8,0},{9,1},... | collective-permute-start | bytes 442376 | tf_op jit(solution)/shard_map/ppermute | solution.py:435
  64.0 8.8 %collective-permute-done.22.refs_1_ = bf16[288,512]{1,0:T(8,128)(2,1)S(1)} collective-permute-done((bf16[288,512]{1,0:T(8,128)(2,1)S(1)}, bf16[288,512]{1,0:T(8,128)(2,1)S(1)}, u32[]{:S(2)}, u32[]{:S(2)}) %collective-permute-start.22) | collective-permute-done | bytes 294944 | tf_op jit(solution)/shard_map/ppermute | solution.py:435
  72.8 0.8 %sum_first.1 = (f32[288,256]{1,0:T(8,128)}, f32[288,256]{1,0:T(8,128)S(1)}) custom-call(f32[288,512]{1,0:T(8,128)S(1)} %get-tuple-element.119.refs_0_, bf16[288,512]{1,0:T(8,128)(2,1)S(1)} %collective-permute-done.22.refs_1_), custom_call_target="tpu_custom_call" | custom-call | flops 2000000000 | tf_op jit(solution)/shard_map/sum_first/pallas_call | solution.py:32
  73.5 0.9 %final.1 = (bf16[256,256]{1,0:T(8,128)(2,1)}, bf16[256,256]{1,0:T(8,128)(2,1)}) custom-call(f32[256,512]{1,0:T(8,128)S(1)} %get-tuple-element.122.inner, bf16[32,512]{1,0:T(8,128)(2,1)S(1)} %collective-permute-done.23.rp, bf16[32,512]{1,0:T(8,128)(2,1)S(1)} %collective-permute-done.24.rn, bf16[256,64]{1,0:T(8,128)(2,1)S(1)} %get-tuple-element.101.place), custom_call_target="tpu_custom_call" | custom-call | tf_op jit(solution)/shard_map/final/pallas_call | solution.py:32
  74.4 1.0 %collective-permute-done.25.refs_1_ = bf16[288,256]{1,0:T(8,128)(2,1)S(1)} collective-permute-done((bf16[288,256]{1,0:T(8,128)(2,1)S(1)}, bf16[288,256]{1,0:T(8,128)(2,1)S(1)}, u32[]{:S(2)}, u32[]{:S(2)}) %collective-permute-start.25) | collective-permute-done | bytes 147488 | tf_op jit(solution)/shard_map/ppermute | solution.py:435
  75.5 0.9 %sum_reset.1 = f32[288,512]{1,0:T(8,128)} custom-call(f32[288,256]{1,0:T(8,128)S(1)} %get-tuple-element.128.update, f32[288,256]{1,0:T(8,128)S(1)} %get-tuple-element.115.refs_0_, bf16[288,256]{1,0:T(8,128)(2,1)S(1)} %collective-permute-done.25.refs_1_), custom_call_target="tpu_custom_call" | custom-call | tf_op jit(solution)/shard_map/sum_reset/pallas_call | solution.py:32
  (41 shorter events, 4.8 us)
Async XLA Ops:
  0.6 13.4 %collective-permute-start.2 = (bf16[256,256]{1,0:T(8,128)(2,1)}, bf16[256,256]{1,0:T(8,128)(2,1)S(1)}, u32[]{:S(2)}, u32[]{:S(2)}) collective-permute-start(bf16[256,256]{1,0:T(8,128)(2,1)} %bitcast.13), channel_id=1, source_target_pairs={{0,6},{1,7},{2,4},{3,5},{4,2},{5,3},{6,0},{7,1},{8,14},{9,15},{10,... | collective-permute-start | bytes 393224 | tf_op jit(solution)/shard_map/ppermute | solution.py:435
  4.7 9.4 %collective-permute-start.1 = (bf16[256,256]{1,0:T(8,128)(2,1)}, bf16[256,256]{1,0:T(8,128)(2,1)S(1)}, u32[]{:S(2)}, u32[]{:S(2)}) collective-permute-start(bf16[256,256]{1,0:T(8,128)(2,1)} %bitcast.14), channel_id=1, source_target_pairs={{0,4},{1,5},{2,6},{3,7},{4,0},{5,1},{6,2},{7,3},{8,12},{9,13},{10,... | collective-permute-start | bytes 393224 | tf_op jit(solution)/shard_map/ppermute | solution.py:435
  5.1 9.0 %collective-permute-start = (bf16[256,256]{1,0:T(8,128)(2,1)}, bf16[256,256]{1,0:T(8,128)(2,1)S(1)}, u32[]{:S(2)}, u32[]{:S(2)}) collective-permute-start(bf16[256,256]{1,0:T(8,128)(2,1)} %bitcast.15), channel_id=1, source_target_pairs={{0,2},{1,3},{2,0},{3,1},{4,6},{5,7},{6,4},{7,5},{8,10},{9,11},{10,... | collective-permute-start | bytes 393224 | tf_op jit(solution)/shard_map/ppermute | solution.py:435
  6.6 7.6 %collective-permute-start.3 = (bf16[32,512]{1,0:T(8,128)(2,1)S(1)}, bf16[32,512]{1,0:T(8,128)(2,1)S(1)}, u32[]{:S(2)}, u32[]{:S(2)}) collective-permute-start(bf16[32,512]{1,0:T(8,128)(2,1)S(1)} %get-tuple-element.72), channel_id=1, source_target_pairs={{0,1},{1,0},{2,3},{3,2},{4,5},{5,4},{6,7},{7,6},{8,9},{9,8},{10,11... | collective-permute-start | bytes 98312 | tf_op jit(solution)/shard_map/ppermute | solution.py:435
  6.6 7.5 %collective-permute-start.4 = (bf16[32,512]{1,0:T(8,128)(2,1)S(1)}, bf16[32,512]{1,0:T(8,128)(2,1)S(1)}, u32[]{:S(2)}, u32[]{:S(2)}) collective-permute-start(bf16[32,512]{1,0:T(8,128)(2,1)S(1)} %get-tuple-element.73), channel_id=1, source_target_pairs={{0,15},{1,2},{2,1},{3,4},{4,3},{5,6},{6,5},{7,8},{8,7},{9,10},{10,... | collective-permute-start | bytes 98312 | tf_op jit(solution)/shard_map/ppermute | solution.py:438
  16.1 7.6 %collective-permute-start.5 = (bf16[32,256]{1,0:T(8,128)(2,1)S(1)}, bf16[32,256]{1,0:T(8,128)(2,1)S(1)}, u32[]{:S(2)}, u32[]{:S(2)}) collective-permute-start(bf16[32,256]{1,0:T(8,128)(2,1)S(1)} %get-tuple-element.85), channel_id=1, source_target_pairs={{0,1},{1,0},{2,3},{3,2},{4,5},{5,4},{6,7},{7,6},{8,9},{9,8},{10,11... | collective-permute-start | bytes 49160 | tf_op jit(solution)/shard_map/ppermute | solution.py:435
  16.2 7.6 %collective-permute-start.6 = (bf16[32,256]{1,0:T(8,128)(2,1)S(1)}, bf16[32,256]{1,0:T(8,128)(2,1)S(1)}, u32[]{:S(2)}, u32[]{:S(2)}) collective-permute-start(bf16[32,256]{1,0:T(8,128)(2,1)S(1)} %get-tuple-element.86), channel_id=1, source_target_pairs={{0,15},{1,2},{2,1},{3,4},{4,3},{5,6},{6,5},{7,8},{8,7},{9,10},{10,... | collective-permute-start | bytes 49160 | tf_op jit(solution)/shard_map/ppermute | solution.py:438
  19.7 8.9 %collective-permute-start.9 = (bf16[384,256]{1,0:T(8,128)(2,1)S(1)}, bf16[384,256]{1,0:T(8,128)(2,1)S(1)}, u32[]{:S(2)}, u32[]{:S(2)}) collective-permute-start(bf16[384,256]{1,0:T(8,128)(2,1)S(1)} %get-tuple-element.94.refs_4_), channel_id=1, source_target_pairs={{0,6},{1,7},{2,4},{3,5},{4,2},{5,3},{6,0},{7,1},{8,14},{9,15},{10,... | collective-permute-start | bytes 589832 | tf_op jit(solution)/shard_map/ppermute | solution.py:435
  19.7 8.9 %collective-permute-start.8 = (bf16[384,256]{1,0:T(8,128)(2,1)S(1)}, bf16[384,256]{1,0:T(8,128)(2,1)S(1)}, u32[]{:S(2)}, u32[]{:S(2)}) collective-permute-start(bf16[384,256]{1,0:T(8,128)(2,1)S(1)} %get-tuple-element.94.refs_4_), channel_id=1, source_target_pairs={{0,4},{1,5},{2,6},{3,7},{4,0},{5,1},{6,2},{7,3},{8,12},{9,13},{10,... | collective-permute-start | bytes 589832 | tf_op jit(solution)/shard_map/ppermute | solution.py:435
  19.7 9.0 %collective-permute-start.7 = (bf16[384,256]{1,0:T(8,128)(2,1)S(1)}, bf16[384,256]{1,0:T(8,128)(2,1)S(1)}, u32[]{:S(2)}, u32[]{:S(2)}) collective-permute-start(bf16[384,256]{1,0:T(8,128)(2,1)S(1)} %get-tuple-element.94.refs_4_), channel_id=1, source_target_pairs={{0,2},{1,3},{2,0},{3,1},{4,6},{5,7},{6,4},{7,5},{8,10},{9,11},{10,... | collective-permute-start | bytes 589832 | tf_op jit(solution)/shard_map/ppermute | solution.py:435
  24.9 7.3 %copy-start = (bf16[1,16,16,256]{3,2,1,0:T(8,128)(2,1)S(1)}, bf16[1,16,16,256]{3,2,1,0:T(8,128)(2,1)}, u32[]{:S(2)}) copy-start(bf16[1,16,16,256]{3,2,1,0:T(8,128)(2,1)} %param.13) | copy-start | bytes 393220
  26.4 11.1 %collective-permute-start.11 = (bf16[32,256]{1,0:T(8,128)(2,1)S(1)}, bf16[32,256]{1,0:T(8,128)(2,1)S(1)}, u32[]{:S(2)}, u32[]{:S(2)}) collective-permute-start(bf16[32,256]{1,0:T(8,128)(2,1)S(1)} %get-tuple-element.100), channel_id=1, source_target_pairs={{0,15},{1,2},{2,1},{3,4},{4,3},{5,6},{6,5},{7,8},{8,7},{9,10},{10,... | collective-permute-start | bytes 49160 | tf_op jit(solution)/shard_map/ppermute | solution.py:438
  28.6 8.9 %collective-permute-start.10 = (bf16[32,256]{1,0:T(8,128)(2,1)S(1)}, bf16[32,256]{1,0:T(8,128)(2,1)S(1)}, u32[]{:S(2)}, u32[]{:S(2)}) collective-permute-start(bf16[32,256]{1,0:T(8,128)(2,1)S(1)} %get-tuple-element.99), channel_id=1, source_target_pairs={{0,1},{1,0},{2,3},{3,2},{4,5},{5,4},{6,7},{7,6},{8,9},{9,8},{10,11... | collective-permute-start | bytes 49160 | tf_op jit(solution)/shard_map/ppermute | solution.py:435
  28.8 11.2 %collective-permute-start.14 = (bf16[576,256]{1,0:T(8,128)(2,1)S(1)}, bf16[576,256]{1,0:T(8,128)(2,1)S(1)}, u32[]{:S(2)}, u32[]{:S(2)}) collective-permute-start(bf16[576,256]{1,0:T(8,128)(2,1)S(1)} %get-tuple-element.116.d.refs_10_.refs_2_), channel_id=1, source_target_pairs={{0,6},{1,7},{2,4},{3,5},{4,2},{5,3},{6,0},{7,1},{8,14},{9,15},{10,... | collective-permute-start | bytes 884744 | tf_op jit(solution)/shard_map/ppermute | solution.py:435
  30.3 14.8 %collective-permute-start.13 = (bf16[576,256]{1,0:T(8,128)(2,1)S(1)}, bf16[576,256]{1,0:T(8,128)(2,1)S(1)}, u32[]{:S(2)}, u32[]{:S(2)}) collective-permute-start(bf16[576,256]{1,0:T(8,128)(2,1)S(1)} %get-tuple-element.116.d.refs_10_.refs_2_), channel_id=1, source_target_pairs={{0,4},{1,5},{2,6},{3,7},{4,0},{5,1},{6,2},{7,3},{8,12},{9,13},{10,... | collective-permute-start | bytes 884744 | tf_op jit(solution)/shard_map/ppermute | solution.py:435
  30.9 15.0 %collective-permute-start.12 = (bf16[576,256]{1,0:T(8,128)(2,1)S(1)}, bf16[576,256]{1,0:T(8,128)(2,1)S(1)}, u32[]{:S(2)}, u32[]{:S(2)}) collective-permute-start(bf16[576,256]{1,0:T(8,128)(2,1)S(1)} %get-tuple-element.116.d.refs_10_.refs_2_), channel_id=1, source_target_pairs={{0,2},{1,3},{2,0},{3,1},{4,6},{5,7},{6,4},{7,5},{8,10},{9,11},{10,... | collective-permute-start | bytes 884744 | tf_op jit(solution)/shard_map/ppermute | solution.py:435
  37.7 13.1 %collective-permute-start.17 = (bf16[256,256]{1,0:T(8,128)(2,1)S(1)}, bf16[256,256]{1,0:T(8,128)(2,1)S(1)}, u32[]{:S(2)}, u32[]{:S(2)}) collective-permute-start(bf16[256,256]{1,0:T(8,128)(2,1)S(1)} %get-tuple-element.102.refs_1_.d), channel_id=1, source_target_pairs={{0,6},{1,7},{2,4},{3,5},{4,2},{5,3},{6,0},{7,1},{8,14},{9,15},{10,... | collective-permute-start | bytes 393224 | tf_op jit(solution)/shard_map/ppermute | solution.py:435
  39.3 11.5 %collective-permute-start.16 = (bf16[256,256]{1,0:T(8,128)(2,1)S(1)}, bf16[256,256]{1,0:T(8,128)(2,1)S(1)}, u32[]{:S(2)}, u32[]{:S(2)}) collective-permute-start(bf16[256,256]{1,0:T(8,128)(2,1)S(1)} %get-tuple-element.102.refs_1_.d), channel_id=1, source_target_pairs={{0,4},{1,5},{2,6},{3,7},{4,0},{5,1},{6,2},{7,3},{8,12},{9,13},{10,... | collective-permute-start | bytes 393224 | tf_op jit(solution)/shard_map/ppermute | solution.py:435
  39.9 11.0 %collective-permute-start.15 = (bf16[256,256]{1,0:T(8,128)(2,1)S(1)}, bf16[256,256]{1,0:T(8,128)(2,1)S(1)}, u32[]{:S(2)}, u32[]{:S(2)}) collective-permute-start(bf16[256,256]{1,0:T(8,128)(2,1)S(1)} %get-tuple-element.102.refs_1_.d), channel_id=1, source_target_pairs={{0,2},{1,3},{2,0},{3,1},{4,6},{5,7},{6,4},{7,5},{8,10},{9,11},{10,... | collective-permute-start | bytes 393224 | tf_op jit(solution)/shard_map/ppermute | solution.py:435
  50.3 2.0 %collective-permute-start.18 = (bf16[2,288,256]{2,1,0:T(8,128)(2,1)S(1)}, bf16[2,288,256]{2,1,0:T(8,128)(2,1)S(1)}, u32[]{:S(2)}, u32[]{:S(2)}) collective-permute-start(bf16[2,288,256]{2,1,0:T(8,128)(2,1)S(1)} %get-tuple-element.109), channel_id=1, source_target_pairs={{0,1},{1,0},{2,3},{3,2},{4,5},{5,4},{6,7},{7,6},{8,9},{9,8},{10,11... | collective-permute-start | bytes 884744 | tf_op jit(solution)/shard_map/ppermute | solution.py:435
  50.3 2.0 %collective-permute-start.19 = (bf16[2,288,256]{2,1,0:T(8,128)(2,1)S(1)}, bf16[2,288,256]{2,1,0:T(8,128)(2,1)S(1)}, u32[]{:S(2)}, u32[]{:S(2)}) collective-permute-start(bf16[2,288,256]{2,1,0:T(8,128)(2,1)S(1)} %get-tuple-element.110), channel_id=1, source_target_pairs={{0,1},{1,0},{2,3},{3,2},{4,5},{5,4},{6,7},{7,6},{8,9},{9,8},{10,11... | collective-permute-start | bytes 884744 | tf_op jit(solution)/shard_map/ppermute | solution.py:435
  52.4 20.3 %collective-permute-start.22 = (bf16[288,512]{1,0:T(8,128)(2,1)S(1)}, bf16[288,512]{1,0:T(8,128)(2,1)S(1)}, u32[]{:S(2)}, u32[]{:S(2)}) collective-permute-start(bf16[288,512]{1,0:T(8,128)(2,1)S(1)} %bitcast.20), channel_id=1, source_target_pairs={{0,8},{1,9},{2,10},{3,11},{4,12},{5,13},{6,14},{7,15},{8,0},{9,1},... | collective-permute-start | bytes 884744 | tf_op jit(solution)/shard_map/ppermute | solution.py:435
  55.0 1.4 %collective-permute-start.20 = (bf16[2,288,128]{2,1,0:T(8,128)(2,1)S(1)}, bf16[2,288,128]{2,1,0:T(8,128)(2,1)S(1)}, u32[]{:S(2)}, u32[]{:S(2)}) collective-permute-start(bf16[2,288,128]{2,1,0:T(8,128)(2,1)S(1)} %get-tuple-element.113), channel_id=1, source_target_pairs={{0,1},{1,0},{2,3},{3,2},{4,5},{5,4},{6,7},{7,6},{8,9},{9,8},{10,11... | collective-permute-start | bytes 442376 | tf_op jit(solution)/shard_map/ppermute | solution.py:435
  55.0 1.6 %collective-permute-start.21 = (bf16[2,288,128]{2,1,0:T(8,128)(2,1)S(1)}, bf16[2,288,128]{2,1,0:T(8,128)(2,1)S(1)}, u32[]{:S(2)}, u32[]{:S(2)}) collective-permute-start(bf16[2,288,128]{2,1,0:T(8,128)(2,1)S(1)} %get-tuple-element.114), channel_id=1, source_target_pairs={{0,1},{1,0},{2,3},{3,2},{4,5},{5,4},{6,7},{7,6},{8,9},{9,8},{10,11... | collective-permute-start | bytes 442376 | tf_op jit(solution)/shard_map/ppermute | solution.py:435
  60.0 13.6 %collective-permute-start.23 = (bf16[32,512]{1,0:T(8,128)(2,1)S(1)}, bf16[32,512]{1,0:T(8,128)(2,1)S(1)}, u32[]{:S(2)}, u32[]{:S(2)}) collective-permute-start(bf16[32,512]{1,0:T(8,128)(2,1)S(1)} %get-tuple-element.123), channel_id=1, source_target_pairs={{0,1},{1,0},{2,3},{3,2},{4,5},{5,4},{6,7},{7,6},{8,9},{9,8},{10,11... | collective-permute-start | bytes 98312 | tf_op jit(solution)/shard_map/ppermute | solution.py:435
  60.3 13.3 %collective-permute-start.24 = (bf16[32,512]{1,0:T(8,128)(2,1)S(1)}, bf16[32,512]{1,0:T(8,128)(2,1)S(1)}, u32[]{:S(2)}, u32[]{:S(2)}) collective-permute-start(bf16[32,512]{1,0:T(8,128)(2,1)S(1)} %get-tuple-element.124), channel_id=1, source_target_pairs={{0,15},{1,2},{2,1},{3,4},{4,3},{5,6},{6,5},{7,8},{8,7},{9,10},{10,... | collective-permute-start | bytes 98312 | tf_op jit(solution)/shard_map/ppermute | solution.py:438
  62.0 13.4 %collective-permute-start.25 = (bf16[288,256]{1,0:T(8,128)(2,1)S(1)}, bf16[288,256]{1,0:T(8,128)(2,1)S(1)}, u32[]{:S(2)}, u32[]{:S(2)}) collective-permute-start(bf16[288,256]{1,0:T(8,128)(2,1)S(1)} %bitcast.21), channel_id=1, source_target_pairs={{0,8},{1,9},{2,10},{3,11},{4,12},{5,13},{6,14},{7,15},{8,0},{9,1},... | collective-permute-start | bytes 442376 | tf_op jit(solution)/shard_map/ppermute | solution.py:435

commit v5 on v4

--- a/solution.py
+++ b/solution.py
@@ -203,17 +203,17 @@
     out[...] = dot(jnp.concatenate(cols, axis=1), jnp.concatenate(rows, axis=0)) + bias[...]
 
 
-def cand_kernel(side, acc, rh, rp, rn, turn, m0, m2, w, gate, h, g, d, f):
+def cand_kernel(side, acc, rh, rp, rn, turn, m0, m2, w, gate, h, g, d, d_u, f):
     c = g.shape[1]
     cells = side * side
     strips = dot(turn[...], jnp.concatenate([rp[...], rn[...]], axis=0)).astype(BF)
     frames(side, rh[...], strips, m0, m2, f)
-    d[2 * cells :] = strips
+    d_u[cells:] = strips
     candidate = jnp.tanh(acc[...] + conv(side, f, w, c, 2 * c))
     update = gate[:, :c]
     grad = g[...].astype(F32)
-    d[:cells] = (grad * update * (1.0 - candidate * candidate)).astype(BF)
-    d[cells : 2 * cells] = (grad * (candidate - h[:, c:].astype(F32)) * update * (1.0 - update)).astype(BF)
+    d[...] = (grad * update * (1.0 - candidate * candidate)).astype(BF)
+    d_u[:cells] = (grad * (candidate - h[:, c:].astype(F32)) * update * (1.0 - update)).astype(BF)
 
 
 def spread(side, acc, d, w, lo, hi, col_lo, col_hi, fresh):
@@ -251,7 +251,7 @@
     s_prev[...] = picked[rim // 2 :]
 
 
-def back_early_kernel(side, d, wc, wg, acc):
+def back_early_kernel(side, d, d_u, wc, wg, acc):
     c = wc.shape[2]
     cells = side * side
     acc[...] = jnp.zeros_like(acc)
@@ -259,15 +259,17 @@
         for b in range(3):
             rows = slice(a * side, a * side + cells)
             t = a * 3 + b
-            acc[b, rows, :c] += dot_nt(d[:cells], wc[t, :c, :]) + dot_nt(d[cells : 2 * cells], wg[t, :c, :c])
-            acc[b, rows, c:] += dot_nt(d[cells : 2 * cells], wg[t, c:, :c])
-
-
-def reset_kernel(side, inner, rp, rn, place, gate, h, g, d, direct):
+            acc[b, rows, :c] += dot_nt(d[:cells], wc[t, :c, :]) + dot_nt(d_u[:cells], wg[t, :c, :c])
+            acc[b, rows, c:] += dot_nt(d_u[:cells], wg[t, c:, :c])
+
+
+def reset_kernel(side, inner, rp, rn, place, gate, h, g, d_c, d, direct):
     c = g.shape[1]
     d_rh = inner[...] + dot(place[...], jnp.concatenate([rp[...], rn[...]], axis=0))
     update, reset = gate[:, :c], gate[:, c:]
-    d[...] = (d_rh * h[:, c:].astype(F32) * reset * (1.0 - reset)).astype(BF)
+    cells = side * side
+    d[:cells] = d_c[...]
+    d[cells:] = (d_rh * h[:, c:].astype(F32) * reset * (1.0 - reset)).astype(BF)
     direct[...] = g[...].astype(F32) * (1.0 - update) + d_rh * reset
 
 
@@ -275,7 +277,8 @@
     c = d.shape[1]
     rim = 4 * side
     acc[...] = early[...]
-    spread(side, acc, d[...], w, 0, 2 * c, c, 2 * c, False)
+    cells = side * side
+    spread(side, acc, d[cells:], w, 0, 2 * c, c, 2 * c, False)
     own, edge = gather_frame(side, acc)
     inner[:, :c] = own[:, :c]
     inner[:, c:] = own[:, c:] + direct[...]
@@ -329,7 +332,7 @@
             elif cand:
                 rh, rh_near, ds = more[0], more[1], more[2:]
                 src[k, :cells, lanes] = rh[:, col] if n == 0 else rh_near[n - 1, :, col]
-                src[k, cells:, lanes] = ds[n][2 * cells :, col]
+                src[k, cells:, lanes] = ds[n][cells:, col]
             else:
                 src[k, :cells, lanes] = packs[n][:cells, col]
                 src[k, cells:, lanes] = packs[n][cells + rim :, col]
@@ -364,27 +367,29 @@
                     sends[k * (c // width) + j][t // 2] = part[:, j * width : (j + 1) * width].astype(BF)
 
 
-def pair_kernel(keep, *refs):
-    gots, (own, far) = refs[:-2], refs[-2:]
-    c = gots[0].shape[2]
-    for k, got in enumerate(gots):
-        at = slice(k * c, (k + 1) * c)
-        own[:, at] = keep[0, :, at] + got[0].astype(F32)
+def pair_kernel(*refs):
+    own, far = refs[-2:]
+    keep, first, at = None, 0, 0
+    for r in refs[:-2]:
+        if r.dtype == F32:
+            keep, at = r, 0
+            continue
+        c = r.shape[2]
+        cols = slice(first, first + c)
+        own[:, cols] = keep[0, :, at : at + c] + r[0].astype(F32)
         for m in range(1, keep.shape[0]):
-            far[m - 1, :, at] = (keep[m, :, at] + got[m].astype(F32)).astype(BF)
+            far[m - 1, :, cols] = (keep[m, :, at : at + c] + r[m].astype(F32)).astype(BF)
+        at, first = at + c, first + c
 
 
 def sum_kernel(*refs):
-    parts, (cand, update) = refs[:-2], refs[-2:]
-    c = cand.shape[1]
-    total = parts[0][...]
-    for r in parts[1:]:
+    total = refs[0][...]
+    for r in refs[1:-1]:
         total += r[...].astype(F32)
-    cand[...] = total[:, :c]
-    update[...] = total[:, c:]
-
-
-def sum_reset_kernel(update, *refs):
+    refs[-1][...] = total
+
+
+def sum_gate_kernel(update, *refs):
     parts, gate = refs[:-1], refs[-1]
     c = update.shape[1]
     total = parts[0][...]
@@ -461,12 +466,12 @@
             scratch=[pltpu.VMEM((n, 2, blocks, c), F32)],
             cost=cost,
         )
-        return keep, [swap(u, 1) for u in sends]
-
-    def pair(name, keep, gots, cost=0):
-        n = keep.shape[2]
+        return [keep] + [swap(u, 1) for u in sends]
+
+    def pair(name, *sums, cost=0):
+        n = sum(u.shape[2] for u in sums if u.dtype == F32)
         own, far = run(
-            name, pair_kernel, [((rows, n), F32), ((groups - 1, rows, n), BF)], keep, *gots, cost=cost
+            name, pair_kernel, [((rows, n), F32), ((groups - 1, rows, n), BF)], *sums, cost=cost
         )
         return [own] + [swap(far[k - 1], 8 * k) for k in range(1, groups)]
 
@@ -512,52 +517,55 @@
     r2p, r2n = exchange(s2n, s2p)
     pack_near = near(after(pack, *x_near))
     (acc_x,) = run("cand_x", functools.partial(cand_x_kernel, side), [((cells, c), F32)], f, wc_v, bc_v)
-    d_cu, _ = run(
+    d_c, d_u, _ = run(
         "cand", functools.partial(cand_kernel, side),
-        [((2 * cells + rim, c), BF), ((3, band, c), BF)],
+        [((cells, c), BF), ((cells + rim, c), BF), ((3, band, c), BF)],
         acc_x, rh, r2p, r2n, turn, m0, m2, wc_v, gate, xh, g_v, cost=3,
     )
     inner_rh, s3n, s3p, _ = run(
         "back_rh", functools.partial(back_rh_kernel, side),
         [((cells, c), F32), ((half, c), BF), ((half, c), BF), ((3, band, c), F32)],
-        d_cu, wc_v, rim_sel,
+        d_c, wc_v, rim_sel,
     )
     r3p, r3n = exchange(s3n, s3p)
-    d_near = near(after(d_cu, s3n, *pack_near))
+    u_near = near(after(d_u, s3n, *pack_near))
     rh_near, taps_v = run(
         "near_reset", functools.partial(near_reset_kernel, side), [((3, cells, c), BF), (taps.shape, BF)],
         *x_near, *pack_near, m0, m2, wg_v, bg_v, taps,
         hbm=(12,),
-        scratch=[pltpu.VMEM((3, 3, band, 2 * c), BF), pltpu.SemaphoreType.DMA((1,))],
-    )
-    lhs_gate = lhs_of("lhs_gate", False, *x_near, *pack_near, cost=5)
-    d_r, direct = run(
+        scratch=[pltpu.VMEM((3, 3, band, 2 * c), BF), pltpu.SemaphoreType.DMA((1,))], cost=0,
+    )
+    d_cr, direct = run(
         "reset", functools.partial(reset_kernel, side),
-        [((cells, c), BF), ((cells, c), F32)],
-        inner_rh, r3p, r3n, place, gate, xh, g_v,
-    )
-    r_near = near(d_r)
-    lhs_cand = lhs_of("lhs_cand", True, *x_near, *pack_near, rh, rh_near, *d_near)
-    keep_f, gots_f = products("weights_first", (0, 1), [lhs_cand, lhs_gate], d_near, cost=0)
-    keep, gots = products("weights_reset", (0,), [lhs_gate], r_near, cuts=2, cost=4)
-    parts = pair("pair_first", keep_f, gots_f, cost=0)
-    parts_r = pair("pair_reset", keep, gots, cost=0)
+        [((2 * cells, c), BF), ((cells, c), F32)],
+        inner_rh, r3p, r3n, place, gate, xh, g_v, d_c, cost=5,
+    )
+    d_near = near(d_cr)
+    lhs_gate = lhs_of("lhs_gate", False, *x_near, *pack_near, cost=0)
+    sums_u = products("weights_update", (0,), [lhs_gate], u_near, cuts=2, cost=0)
+    lhs_cand = lhs_of("lhs_cand", True, *x_near, *pack_near, rh, rh_near, *u_near, cost=0)
+    parts_u = pair("pair_update", *sums_u)
     (early,) = run(
-        "back_early", functools.partial(back_early_kernel, side), [((3, band, 2 * c), F32)], d_cu, wc_v, wg_v
+        "back_early", functools.partial(back_early_kernel, side), [((3, band, 2 * c), F32)], d_c, d_u, wc_v, wg_v
     )
     inner, s4n, s4p, _ = run(
         "back_gate", functools.partial(back_gate_kernel, side),
         [((cells, 2 * c), F32), ((half, 2 * c), BF), ((half, 2 * c), BF), ((3, band, 2 * c), F32)],
-        early, d_r, wg_v, direct, rim_sel, cost=0,
+        early, d_cr, wg_v, direct, rim_sel,
     )
     r4p, r4n = exchange(s4n, s4p)
-    grad_w_cand, sum_u = run(
-        "sum_first", sum_kernel, [((rows, c), F32), ((rows, c), F32)], *parts, pin=False, cost=2
+    sums_r = products("weights_reset", (1,), [lhs_gate], d_near, cuts=1, cost=0)
+    sums_c = products("weights_cand", (0,), [lhs_cand], d_near, cuts=2, cost=0)
+    (sum_u,) = run("sum_update", sum_kernel, [((rows, c), F32)], *parts_u, cost=2)
+    parts_r = pair("pair_reset", *sums_r)
+    parts_c = pair("pair_cand", *sums_c)
+    (grad_w_gate,) = run(
+        "sum_gate", sum_gate_kernel, [((rows, 2 * c), F32)], sum_u, *parts_r, pin=False, cost=0
     )
     gx, gh = run(
-        "final", final_kernel, [((cells, c), BF), ((cells, c), BF)], inner, r4p, r4n, place, pin=False, cost=0
-    )
-    (grad_w_gate,) = run("sum_reset", sum_reset_kernel, [((rows, 2 * c), F32)], sum_u, *parts_r, pin=False)
+        "final", final_kernel, [((cells, c), BF), ((cells, c), BF)], inner, r4p, r4n, place, pin=False, cost=3
+    )
+    (grad_w_cand,) = run("sum_cand", sum_kernel, [((rows, c), F32)], *parts_c, pin=False)
     shape = (1, side, side, c)
     return gx.reshape(shape), gh.reshape(shape), grad_w_gate, grad_w_cand
 

time: 76.5 us -> 73.5 us (0.961)
  waiting for transfers between devices: 15.9 us -> 9.17 us
  starting transfers between devices: 33.8 us -> 37.1 us
    ppermute x22 -> x24, waiting for transfers between devices: 15.9 us -> 9.16 us  [swap(): return lax.ppermute(u, 'tile', [(i, i ^ k) for i in range(tiles)])]
    ppermute x22 -> x24, starting transfers between devices: 21.3 us -> 24.9 us  [swap(): return lax.ppermute(u, 'tile', [(i, i ^ k) for i in range(tiles)])]
    pallas_call x19 -> x22, Pallas kernels: 25.8 us -> 26.2 us  [call(): pl.pallas_call(body, out_shape=[pltpu.VMEM(s, d) if pin else jax.ShapeDty...]
  transfers between devices with their start and end apart: 26 -> 28, of which waited for: 9 -> 3; matrix products, arithmetic and copies ran while one was open for 0% -> 0% of each run, Pallas kernels for 30% -> 32%
where the time goes in v5:
time: 73.5 us; the launch traced here: 73.3 us
  starting transfers between devices  37.1 us (50%)
  Pallas kernels  26.2 us (36%)
  waiting for transfers between devices  9.17 us (12%)
  between operations  0.91 us (1%)
    pallas_call x22, Pallas kernels, call(): pl.pallas_call(body, out_shape=[pltpu.VMEM(s, d) if pin else jax.ShapeDty...  26.2 us
    ppermute x24, starting transfers between devices, swap(): return lax.ppermute(u, 'tile', [(i, i ^ k) for i in range(tiles)])  24.9 us
    ppermute x4, starting transfers between devices, exchange(): return (swap(s_first, 1), lax.ppermute(s_second, 'tile', cross))  12.2 us
    ppermute x24, waiting for transfers between devices, swap(): return lax.ppermute(u, 'tile', [(i, i ^ k) for i in range(tiles)])  9.16 us
  transfers between devices with their start and end apart: 28, of which 3 were waited for; matrix products, arithmetic and copies ran while one was open for 0% of the time, Pallas kernels for 32%

profile of v5, /device:TPU:0, one launch (start us, length us, event | category | flops | bytes accessed | tf_op | source)
XLA Modules:
  0.0 73.3 jit_solution(4711235566461727411)
XLA Ops:
  0.6 3.0 %collective-permute-start = (bf16[256,256]{1,0:T(8,128)(2,1)}, bf16[256,256]{1,0:T(8,128)(2,1)S(1)}, u32[]{:S(2)}, u32[]{:S(2)}) collective-permute-start(bf16[256,256]{1,0:T(8,128)(2,1)} %bitcast.14), channel_id=1, source_target_pairs={{0,2},{1,3},{2,0},{3,1},{4,6},{5,7},{6,4},{7,5},{8,10},{9,11},{10,... | collective-permute-start | bytes 393224 | tf_op jit(solution)/shard_map/ppermute | solution.py:440
  3.7 1.6 %collective-permute-start.1 = (bf16[256,256]{1,0:T(8,128)(2,1)}, bf16[256,256]{1,0:T(8,128)(2,1)S(1)}, u32[]{:S(2)}, u32[]{:S(2)}) collective-permute-start(bf16[256,256]{1,0:T(8,128)(2,1)} %bitcast.15), channel_id=1, source_target_pairs={{0,4},{1,5},{2,6},{3,7},{4,0},{5,1},{6,2},{7,3},{8,12},{9,13},{10,... | collective-permute-start | bytes 393224 | tf_op jit(solution)/shard_map/ppermute | solution.py:440
  5.2 1.2 %route.1 = (bf16[256,512]{1,0:T(8,128)(2,1)S(1)}, bf16[32,512]{1,0:T(8,128)(2,1)S(1)}, bf16[32,512]{1,0:T(8,128)(2,1)S(1)}, bf16[64,256]{1,0:T(8,128)(2,1)S(1)},...) custom-call(s32[4,16]{1,0:T(4,128)} %bitcast.26, s32[4,16]{1,0:T(4,128)} %bitcast.27, ...), custom_call_target="tpu_custom_call" | custom-call | tf_op jit(solution)/shard_map/route/pallas_call | solution.py:32
  6.6 5.0 %collective-permute-start.4 = (bf16[32,512]{1,0:T(8,128)(2,1)S(1)}, bf16[32,512]{1,0:T(8,128)(2,1)S(1)}, u32[]{:S(2)}, u32[]{:S(2)}) collective-permute-start(bf16[32,512]{1,0:T(8,128)(2,1)S(1)} %get-tuple-element.80), channel_id=1, source_target_pairs={{0,15},{1,2},{2,1},{3,4},{4,3},{5,6},{6,5},{7,8},{8,7},{9,10},{10,... | collective-permute-start | bytes 98312 | tf_op jit(solution)/shard_map/ppermute | solution.py:443
  11.6 2.5 %load_gate.1 = (bf16[9,512,512]{2,1,0:T(8,128)(2,1)S(1)}, bf16[288,320]{1,0:T(8,128)(2,1)S(1)}, bf16[288,320]{1,0:T(8,128)(2,1)S(1)}, f32[1,512]{1,0:T(1,128)S(1)}) custom-call(bf16[9,512,512]{2,1,0:T(8,128)(2,1)} %bitcast.24, bf16[288,320]{1,0:T(8,128)(2,1)} %constant.6.clone.refs_1_, bf16[288,320]{1,0:T(8,128)(2,1)} %constant.7.clone.refs_2_, ...), custom_call_target="tpu_custom_call" | custom-call | tf_op jit(solution)/shard_map/load_gate/pallas_call | solution.py:32
  14.1 1.9 %gate.1 = (f32[256,512]{1,0:T(8,128)S(1)}, bf16[256,256]{1,0:T(8,128)(2,1)S(1)}, bf16[384,256]{1,0:T(8,128)(2,1)S(1)}, bf16[32,256]{1,0:T(8,128)(2,1)S(1)}, bf16...) custom-call(bf16[256,512]{1,0:T(8,128)(2,1)S(1)} %get-tuple-element., ...), custom_call_target="tpu_custom_call" | custom-call | flops 5000000000 | tf_op jit(solution)/shard_map/gate/pallas_call | solution.py:32
  16.1 3.6 %collective-permute-start.6 = (bf16[32,256]{1,0:T(8,128)(2,1)S(1)}, bf16[32,256]{1,0:T(8,128)(2,1)S(1)}, u32[]{:S(2)}, u32[]{:S(2)}) collective-permute-start(bf16[32,256]{1,0:T(8,128)(2,1)S(1)} %get-tuple-element.93), channel_id=1, source_target_pairs={{0,15},{1,2},{2,1},{3,4},{4,3},{5,6},{6,5},{7,8},{8,7},{9,10},{10,... | collective-permute-start | bytes 49160 | tf_op jit(solution)/shard_map/ppermute | solution.py:443
  19.7 3.5 %collective-permute-start.9 = (bf16[384,256]{1,0:T(8,128)(2,1)S(1)}, bf16[384,256]{1,0:T(8,128)(2,1)S(1)}, u32[]{:S(2)}, u32[]{:S(2)}) collective-permute-start(bf16[384,256]{1,0:T(8,128)(2,1)S(1)} %get-tuple-element.101.refs_4_), channel_id=1, source_target_pairs={{0,6},{1,7},{2,4},{3,5},{4,2},{5,3},{6,0},{7,1},{8,14},{9,15},{10,... | collective-permute-start | bytes 589832 | tf_op jit(solution)/shard_map/ppermute | solution.py:440
  23.7 1.3 %cand.1 = (bf16[256,256]{1,0:T(8,128)(2,1)S(1)}, bf16[320,256]{1,0:T(8,128)(2,1)S(1)}, bf16[3,288,256]{2,1,0:T(8,128)(2,1)}) custom-call(f32[256,256]{1,0:T(8,128)S(1)} %cand_x.1.acc, bf16[256,256]{1,0:T(8,128)(2,1)S(1)} %get-tuple-element.91.rh.refs_8_, bf16[32,256]{1,0:T(8,128)(2,1)S(1)} %collective-permute-done.5.rp, ...), custom_call_target="tpu_custom_call" | custom-call | flops 3000000000 | tf_op jit(solution)/shard_map/cand/pallas_call | solution.py:32
  25.1 1.5 %back_rh.1 = (f32[256,256]{1,0:T(8,128)S(1)}, bf16[32,256]{1,0:T(8,128)(2,1)S(1)}, bf16[32,256]{1,0:T(8,128)(2,1)S(1)}, f32[3,288,256]{2,1,0:T(8,128)}) custom-call(bf16[256,256]{1,0:T(8,128)(2,1)S(1)} %get-tuple-element.119.d.d_c, bf16[9,512,256]{2,1,0:T(8,128)(2,1)S(1)} %get-tuple-element.89.w.wc, bf16[64,544]{1,0:T(8,128)(2,1)S(1)} %get-tuple-element.97.rim_sel), custom_call_target="tpu_custom_call" | custom-call | tf_op jit(solution)/shard_map/back_rh/pallas_call | solution.py:32
  26.6 2.1 %collective-permute-start.11 = (bf16[32,256]{1,0:T(8,128)(2,1)S(1)}, bf16[32,256]{1,0:T(8,128)(2,1)S(1)}, u32[]{:S(2)}, u32[]{:S(2)}) collective-permute-start(bf16[32,256]{1,0:T(8,128)(2,1)S(1)} %get-tuple-element.105), channel_id=1, source_target_pairs={{0,15},{1,2},{2,1},{3,4},{4,3},{5,6},{6,5},{7,8},{8,7},{9,10},{10,... | collective-permute-start | bytes 49160 | tf_op jit(solution)/shard_map/ppermute | solution.py:443
  29.5 1.8 %collective-permute-start.13 = (bf16[320,256]{1,0:T(8,128)(2,1)S(1)}, bf16[320,256]{1,0:T(8,128)(2,1)S(1)}, u32[]{:S(2)}, u32[]{:S(2)}) collective-permute-start(bf16[320,256]{1,0:T(8,128)(2,1)S(1)} %get-tuple-element.112.refs_1_.refs_10_.d_u), channel_id=1, source_target_pairs={{0,4},{1,5},{2,6},{3,7},{4,0},{5,1},{6,2},{7,3},{8,12},{9,13},{10,... | collective-permute-start | bytes 491528 | tf_op jit(solution)/shard_map/ppermute | solution.py:440
  31.3 1.2 %collective-permute-start.14 = (bf16[320,256]{1,0:T(8,128)(2,1)S(1)}, bf16[320,256]{1,0:T(8,128)(2,1)S(1)}, u32[]{:S(2)}, u32[]{:S(2)}) collective-permute-start(bf16[320,256]{1,0:T(8,128)(2,1)S(1)} %get-tuple-element.112.refs_1_.refs_10_.d_u), channel_id=1, source_target_pairs={{0,6},{1,7},{2,4},{3,5},{4,2},{5,3},{6,0},{7,1},{8,14},{9,15},{10,... | collective-permute-start | bytes 491528 | tf_op jit(solution)/shard_map/ppermute | solution.py:440
  32.5 2.9 %near_reset.1 = (bf16[3,256,256]{2,1,0:T(8,128)(2,1)S(1)}, bf16[9,320,256]{2,1,0:T(8,128)(2,1)S(1)}) custom-call(bf16[256,256]{1,0:T(8,128)(2,1)S(1)} %bitcast.18, bf16[256,256]{1,0:T(8,128)(2,1)S(1)} %collective-permute-done.refs_1_, bf16[256,256]{1,0:T(8,128)(2,1)S(1)} %collective-permute-done.1.refs_2_, ...), custom_call_target="tpu_custom_call" | custom-call | tf_op jit(solution)/shard_map/near_reset/pallas_call | solution.py:32
  36.2 1.8 %collective-permute-start.18 = (bf16[512,256]{1,0:T(8,128)(2,1)S(1)}, bf16[512,256]{1,0:T(8,128)(2,1)S(1)}, u32[]{:S(2)}, u32[]{:S(2)}) collective-permute-start(bf16[512,256]{1,0:T(8,128)(2,1)S(1)} %get-tuple-element.107.d.refs_1_), channel_id=1, source_target_pairs={{0,4},{1,5},{2,6},{3,7},{4,0},{5,1},{6,2},{7,3},{8,12},{9,13},{10,... | collective-permute-start | bytes 786440 | tf_op jit(solution)/shard_map/ppermute | solution.py:440
  38.0 1.2 %collective-permute-start.19 = (bf16[512,256]{1,0:T(8,128)(2,1)S(1)}, bf16[512,256]{1,0:T(8,128)(2,1)S(1)}, u32[]{:S(2)}, u32[]{:S(2)}) collective-permute-start(bf16[512,256]{1,0:T(8,128)(2,1)S(1)} %get-tuple-element.107.d.refs_1_), channel_id=1, source_target_pairs={{0,6},{1,7},{2,4},{3,5},{4,2},{5,3},{6,0},{7,1},{8,14},{9,15},{10,... | collective-permute-start | bytes 786440 | tf_op jit(solution)/shard_map/ppermute | solution.py:440
  39.3 2.3 %lhs_gate.1.refs_0_ = bf16[4,384,1024]{2,1,0:T(8,128)(2,1)S(1)} custom-call(bf16[256,256]{1,0:T(8,128)(2,1)S(1)} %bitcast.19, bf16[256,256]{1,0:T(8,128)(2,1)S(1)} %collective-permute-done.refs_1_, bf16[256,256]{1,0:T(8,128)(2,1)S(1)} %collective-permute-done.1.refs_2_, bf16[256,256]{1,0:T(8,128)(2,1)S(1)} %collective-permute-done.2.refs_3_, ...), custom_call_target="tpu_custom_call" | custom-call | tf_op jit(solution)/shard_map/lhs_gate/pallas_call | solution.py:32
  41.6 1.1 %weights_update.1 = (f32[2,288,256]{2,1,0:T(8,128)S(1)}, bf16[2,288,128]{2,1,0:T(8,128)(2,1)S(1)}, bf16[2,288,128]{2,1,0:T(8,128)(2,1)S(1)}) custom-call(bf16[4,384,1024]{2,1,0:T(8,128)(2,1)S(1)} %lhs_gate.1.refs_0_, bf16[320,256]{1,0:T(8,128)(2,1)S(1)} %get-tuple-element.112.refs_1_.refs_10_.d_u, ...), custom_call_target="tpu_custom_call" | custom-call | tf_op jit(solution)/shard_map/weights_update/pallas_call | solution.py:32
  43.3 2.3 %lhs_cand.1.refs_0_ = bf16[4,384,1024]{2,1,0:T(8,128)(2,1)S(1)} custom-call(bf16[256,256]{1,0:T(8,128)(2,1)S(1)} %bitcast.20, bf16[256,256]{1,0:T(8,128)(2,1)S(1)} %collective-permute-done.refs_1_, bf16[256,256]{1,0:T(8,128)(2,1)S(1)} %collective-permute-done.1.refs_2_, bf16[256,256]{1,0:T(8,128)(2,1)S(1)} %collective-permute-done.2.refs_3_, ...), custom_call_target="tpu_custom_call" | custom-call | tf_op jit(solution)/shard_map/lhs_cand/pallas_call | solution.py:32
  45.7 3.0 %collective-permute-start.20 = (bf16[288,256]{1,0:T(8,128)(2,1)S(1)}, bf16[288,256]{1,0:T(8,128)(2,1)S(1)}, u32[]{:S(2)}, u32[]{:S(2)}) collective-permute-start(bf16[288,256]{1,0:T(8,128)(2,1)S(1)} %bitcast.21), channel_id=1, source_target_pairs={{0,8},{1,9},{2,10},{3,11},{4,12},{5,13},{6,14},{7,15},{8,0},{9,1},... | collective-permute-start | bytes 442376 | tf_op jit(solution)/shard_map/ppermute | solution.py:440
  48.6 1.2 %back_early.1.early = f32[3,288,512]{2,1,0:T(8,128)S(1)} custom-call(bf16[256,256]{1,0:T(8,128)(2,1)S(1)} %get-tuple-element.119.d.d_c, bf16[320,256]{1,0:T(8,128)(2,1)S(1)} %get-tuple-element.112.refs_1_.refs_10_.d_u, bf16[9,512,256]{2,1,0:T(8,128)(2,1)S(1)} %get-tuple-element.89.w.wc, bf16[9,512,512]{2,1,0:T(8,128)(2,1)S(1)} %get-tuple-element.77.w.refs_10_.wg), custom_call_target="tpu_custom_call" | custom-call | tf_op jit(solution)/shard_map/back_early/pallas_call | solution.py:32
  49.8 2.3 %back_gate.1 = (f32[256,512]{1,0:T(8,128)S(1)}, bf16[32,512]{1,0:T(8,128)(2,1)S(1)}, bf16[32,512]{1,0:T(8,128)(2,1)S(1)}, f32[3,288,512]{2,1,0:T(8,128)}) custom-call(f32[3,288,512]{2,1,0:T(8,128)S(1)} %back_early.1.early, bf16[512,256]{1,0:T(8,128)(2,1)S(1)} %get-tuple-element.107.d.refs_1_, bf16[9,512,512]{2,1,0:T(8,128)(2,1)S(1)} %get-tuple-element.77.w.refs_10_.wg, ...), custom_call_target="tpu_custom_call" | custom-call | tf_op jit(solution)/shard_map/back_gate/pallas_call | solution.py:32
  52.1 1.1 %weights_reset.1 = (f32[2,288,256]{2,1,0:T(8,128)S(1)}, bf16[2,288,256]{2,1,0:T(8,128)(2,1)S(1)}) custom-call(bf16[4,384,1024]{2,1,0:T(8,128)(2,1)S(1)} %lhs_gate.1.refs_0_, bf16[512,256]{1,0:T(8,128)(2,1)S(1)} %get-tuple-element.107.d.refs_1_, bf16[512,256]{1,0:T(8,128)(2,1)S(1)} %collective-permute-done.17.refs_2_, ...), custom_call_target="tpu_custom_call" | custom-call | tf_op jit(solution)/shard_map/weights_reset/pallas_call | solution.py:32
  53.3 1.1 %weights_cand.1 = (f32[2,288,256]{2,1,0:T(8,128)S(1)}, bf16[2,288,128]{2,1,0:T(8,128)(2,1)S(1)}, bf16[2,288,128]{2,1,0:T(8,128)(2,1)S(1)}) custom-call(bf16[4,384,1024]{2,1,0:T(8,128)(2,1)S(1)} %lhs_cand.1.refs_0_, bf16[512,256]{1,0:T(8,128)(2,1)S(1)} %get-tuple-element.107.d.refs_1_, bf16[512,256]{1,0:T(8,128)(2,1)S(1)} %collective-permute-done.17.refs_2_, ...), custom_call_target="tpu_custom_call" | custom-call | tf_op jit(solution)/shard_map/weights_cand/pallas_call | solution.py:32
  55.2 3.1 %collective-permute-start.24 = (bf16[288,256]{1,0:T(8,128)(2,1)S(1)}, bf16[288,256]{1,0:T(8,128)(2,1)S(1)}, u32[]{:S(2)}, u32[]{:S(2)}) collective-permute-start(bf16[288,256]{1,0:T(8,128)(2,1)S(1)} %bitcast.22), channel_id=1, source_target_pairs={{0,8},{1,9},{2,10},{3,11},{4,12},{5,13},{6,14},{7,15},{8,0},{9,1},... | collective-permute-start | bytes 442376 | tf_op jit(solution)/shard_map/ppermute | solution.py:440
  58.5 1.5 %collective-permute-start.26 = (bf16[32,512]{1,0:T(8,128)(2,1)S(1)}, bf16[32,512]{1,0:T(8,128)(2,1)S(1)}, u32[]{:S(2)}, u32[]{:S(2)}) collective-permute-start(bf16[32,512]{1,0:T(8,128)(2,1)S(1)} %get-tuple-element.139), channel_id=1, source_target_pairs={{0,15},{1,2},{2,1},{3,4},{4,3},{5,6},{6,5},{7,8},{8,7},{9,10},{10,... | collective-permute-start | bytes 98312 | tf_op jit(solution)/shard_map/ppermute | solution.py:443
  60.1 2.0 %collective-permute-start.27 = (bf16[288,256]{1,0:T(8,128)(2,1)S(1)}, bf16[288,256]{1,0:T(8,128)(2,1)S(1)}, u32[]{:S(2)}, u32[]{:S(2)}) collective-permute-start(bf16[288,256]{1,0:T(8,128)(2,1)S(1)} %bitcast.23), channel_id=1, source_target_pairs={{0,8},{1,9},{2,10},{3,11},{4,12},{5,13},{6,14},{7,15},{8,0},{9,1},... | collective-permute-start | bytes 442376 | tf_op jit(solution)/shard_map/ppermute | solution.py:440
  62.1 7.3 %collective-permute-done.24.refs_1_ = bf16[288,256]{1,0:T(8,128)(2,1)S(1)} collective-permute-done((bf16[288,256]{1,0:T(8,128)(2,1)S(1)}, bf16[288,256]{1,0:T(8,128)(2,1)S(1)}, u32[]{:S(2)}, u32[]{:S(2)}) %collective-permute-start.24) | collective-permute-done | bytes 147488 | tf_op jit(solution)/shard_map/ppermute | solution.py:440
  69.3 0.9 %sum_gate.1 = f32[288,512]{1,0:T(8,128)} custom-call(f32[288,256]{1,0:T(8,128)S(1)} %sum_update.1.update, f32[288,256]{1,0:T(8,128)S(1)} %get-tuple-element.130.refs_0_, bf16[288,256]{1,0:T(8,128)(2,1)S(1)} %collective-permute-done.24.refs_1_), custom_call_target="tpu_custom_call" | custom-call | tf_op jit(solution)/shard_map/sum_gate/pallas_call | solution.py:32
  70.2 0.9 %final.1 = (bf16[256,256]{1,0:T(8,128)(2,1)}, bf16[256,256]{1,0:T(8,128)(2,1)}) custom-call(f32[256,512]{1,0:T(8,128)S(1)} %get-tuple-element.137.inner, bf16[32,512]{1,0:T(8,128)(2,1)S(1)} %collective-permute-done.25.rp, bf16[32,512]{1,0:T(8,128)(2,1)S(1)} %collective-permute-done.26.rn, bf16[256,64]{1,0:T(8,128)(2,1)S(1)} %get-tuple-element.106.place), custom_call_target="tpu_custom_call" | custom-call | flops 3000000000 | tf_op jit(solution)/shard_map/final/pallas_call | solution.py:32
  71.1 1.5 %collective-permute-done.27.refs_1_ = bf16[288,256]{1,0:T(8,128)(2,1)S(1)} collective-permute-done((bf16[288,256]{1,0:T(8,128)(2,1)S(1)}, bf16[288,256]{1,0:T(8,128)(2,1)S(1)}, u32[]{:S(2)}, u32[]{:S(2)}) %collective-permute-start.27) | collective-permute-done | bytes 147488 | tf_op jit(solution)/shard_map/ppermute | solution.py:440
  72.6 0.7 %sum_cand.1 = f32[288,256]{1,0:T(8,128)} custom-call(f32[288,256]{1,0:T(8,128)S(1)} %get-tuple-element.142.refs_0_, bf16[288,256]{1,0:T(8,128)(2,1)S(1)} %collective-permute-done.27.refs_1_), custom_call_target="tpu_custom_call" | custom-call | tf_op jit(solution)/shard_map/sum_cand/pallas_call | solution.py:32
  (48 shorter events, 3.8 us)
Async XLA Ops:
  0.6 13.4 %collective-permute-start = (bf16[256,256]{1,0:T(8,128)(2,1)}, bf16[256,256]{1,0:T(8,128)(2,1)S(1)}, u32[]{:S(2)}, u32[]{:S(2)}) collective-permute-start(bf16[256,256]{1,0:T(8,128)(2,1)} %bitcast.14), channel_id=1, source_target_pairs={{0,2},{1,3},{2,0},{3,1},{4,6},{5,7},{6,4},{7,5},{8,10},{9,11},{10,... | collective-permute-start | bytes 393224 | tf_op jit(solution)/shard_map/ppermute | solution.py:440
  3.7 10.4 %collective-permute-start.1 = (bf16[256,256]{1,0:T(8,128)(2,1)}, bf16[256,256]{1,0:T(8,128)(2,1)S(1)}, u32[]{:S(2)}, u32[]{:S(2)}) collective-permute-start(bf16[256,256]{1,0:T(8,128)(2,1)} %bitcast.15), channel_id=1, source_target_pairs={{0,4},{1,5},{2,6},{3,7},{4,0},{5,1},{6,2},{7,3},{8,12},{9,13},{10,... | collective-permute-start | bytes 393224 | tf_op jit(solution)/shard_map/ppermute | solution.py:440
  5.2 8.9 %collective-permute-start.2 = (bf16[256,256]{1,0:T(8,128)(2,1)}, bf16[256,256]{1,0:T(8,128)(2,1)S(1)}, u32[]{:S(2)}, u32[]{:S(2)}) collective-permute-start(bf16[256,256]{1,0:T(8,128)(2,1)} %bitcast.16), channel_id=1, source_target_pairs={{0,6},{1,7},{2,4},{3,5},{4,2},{5,3},{6,0},{7,1},{8,14},{9,15},{10,... | collective-permute-start | bytes 393224 | tf_op jit(solution)/shard_map/ppermute | solution.py:440
  6.5 7.6 %collective-permute-start.3 = (bf16[32,512]{1,0:T(8,128)(2,1)S(1)}, bf16[32,512]{1,0:T(8,128)(2,1)S(1)}, u32[]{:S(2)}, u32[]{:S(2)}) collective-permute-start(bf16[32,512]{1,0:T(8,128)(2,1)S(1)} %get-tuple-element.79), channel_id=1, source_target_pairs={{0,1},{1,0},{2,3},{3,2},{4,5},{5,4},{6,7},{7,6},{8,9},{9,8},{10,11... | collective-permute-start | bytes 98312 | tf_op jit(solution)/shard_map/ppermute | solution.py:440
  6.6 7.6 %collective-permute-start.4 = (bf16[32,512]{1,0:T(8,128)(2,1)S(1)}, bf16[32,512]{1,0:T(8,128)(2,1)S(1)}, u32[]{:S(2)}, u32[]{:S(2)}) collective-permute-start(bf16[32,512]{1,0:T(8,128)(2,1)S(1)} %get-tuple-element.80), channel_id=1, source_target_pairs={{0,15},{1,2},{2,1},{3,4},{4,3},{5,6},{6,5},{7,8},{8,7},{9,10},{10,... | collective-permute-start | bytes 98312 | tf_op jit(solution)/shard_map/ppermute | solution.py:443
  16.1 7.6 %collective-permute-start.5 = (bf16[32,256]{1,0:T(8,128)(2,1)S(1)}, bf16[32,256]{1,0:T(8,128)(2,1)S(1)}, u32[]{:S(2)}, u32[]{:S(2)}) collective-permute-start(bf16[32,256]{1,0:T(8,128)(2,1)S(1)} %get-tuple-element.92), channel_id=1, source_target_pairs={{0,1},{1,0},{2,3},{3,2},{4,5},{5,4},{6,7},{7,6},{8,9},{9,8},{10,11... | collective-permute-start | bytes 49160 | tf_op jit(solution)/shard_map/ppermute | solution.py:440
  16.1 7.6 %collective-permute-start.6 = (bf16[32,256]{1,0:T(8,128)(2,1)S(1)}, bf16[32,256]{1,0:T(8,128)(2,1)S(1)}, u32[]{:S(2)}, u32[]{:S(2)}) collective-permute-start(bf16[32,256]{1,0:T(8,128)(2,1)S(1)} %get-tuple-element.93), channel_id=1, source_target_pairs={{0,15},{1,2},{2,1},{3,4},{4,3},{5,6},{6,5},{7,8},{8,7},{9,10},{10,... | collective-permute-start | bytes 49160 | tf_op jit(solution)/shard_map/ppermute | solution.py:443
  19.7 9.0 %collective-permute-start.7 = (bf16[384,256]{1,0:T(8,128)(2,1)S(1)}, bf16[384,256]{1,0:T(8,128)(2,1)S(1)}, u32[]{:S(2)}, u32[]{:S(2)}) collective-permute-start(bf16[384,256]{1,0:T(8,128)(2,1)S(1)} %get-tuple-element.101.refs_4_), channel_id=1, source_target_pairs={{0,2},{1,3},{2,0},{3,1},{4,6},{5,7},{6,4},{7,5},{8,10},{9,11},{10,... | collective-permute-start | bytes 589832 | tf_op jit(solution)/shard_map/ppermute | solution.py:440
  19.7 9.0 %collective-permute-start.8 = (bf16[384,256]{1,0:T(8,128)(2,1)S(1)}, bf16[384,256]{1,0:T(8,128)(2,1)S(1)}, u32[]{:S(2)}, u32[]{:S(2)}) collective-permute-start(bf16[384,256]{1,0:T(8,128)(2,1)S(1)} %get-tuple-element.101.refs_4_), channel_id=1, source_target_pairs={{0,4},{1,5},{2,6},{3,7},{4,0},{5,1},{6,2},{7,3},{8,12},{9,13},{10,... | collective-permute-start | bytes 589832 | tf_op jit(solution)/shard_map/ppermute | solution.py:440
  19.7 9.3 %collective-permute-start.9 = (bf16[384,256]{1,0:T(8,128)(2,1)S(1)}, bf16[384,256]{1,0:T(8,128)(2,1)S(1)}, u32[]{:S(2)}, u32[]{:S(2)}) collective-permute-start(bf16[384,256]{1,0:T(8,128)(2,1)S(1)} %get-tuple-element.101.refs_4_), channel_id=1, source_target_pairs={{0,6},{1,7},{2,4},{3,5},{4,2},{5,3},{6,0},{7,1},{8,14},{9,15},{10,... | collective-permute-start | bytes 589832 | tf_op jit(solution)/shard_map/ppermute | solution.py:440
  25.1 7.5 %copy-start = (bf16[1,16,16,256]{3,2,1,0:T(8,128)(2,1)S(1)}, bf16[1,16,16,256]{3,2,1,0:T(8,128)(2,1)}, u32[]{:S(2)}) copy-start(bf16[1,16,16,256]{3,2,1,0:T(8,128)(2,1)} %param.13) | copy-start | bytes 393220
  26.6 8.9 %collective-permute-start.10 = (bf16[32,256]{1,0:T(8,128)(2,1)S(1)}, bf16[32,256]{1,0:T(8,128)(2,1)S(1)}, u32[]{:S(2)}, u32[]{:S(2)}) collective-permute-start(bf16[32,256]{1,0:T(8,128)(2,1)S(1)} %get-tuple-element.104), channel_id=1, source_target_pairs={{0,1},{1,0},{2,3},{3,2},{4,5},{5,4},{6,7},{7,6},{8,9},{9,8},{10,11... | collective-permute-start | bytes 49160 | tf_op jit(solution)/shard_map/ppermute | solution.py:440
  26.6 8.9 %collective-permute-start.11 = (bf16[32,256]{1,0:T(8,128)(2,1)S(1)}, bf16[32,256]{1,0:T(8,128)(2,1)S(1)}, u32[]{:S(2)}, u32[]{:S(2)}) collective-permute-start(bf16[32,256]{1,0:T(8,128)(2,1)S(1)} %get-tuple-element.105), channel_id=1, source_target_pairs={{0,15},{1,2},{2,1},{3,4},{4,3},{5,6},{6,5},{7,8},{8,7},{9,10},{10,... | collective-permute-start | bytes 49160 | tf_op jit(solution)/shard_map/ppermute | solution.py:443
  29.1 9.0 %collective-permute-start.12 = (bf16[320,256]{1,0:T(8,128)(2,1)S(1)}, bf16[320,256]{1,0:T(8,128)(2,1)S(1)}, u32[]{:S(2)}, u32[]{:S(2)}) collective-permute-start(bf16[320,256]{1,0:T(8,128)(2,1)S(1)} %get-tuple-element.112.refs_1_.refs_10_.d_u), channel_id=1, source_target_pairs={{0,2},{1,3},{2,0},{3,1},{4,6},{5,7},{6,4},{7,5},{8,10},{9,11},{10,... | collective-permute-start | bytes 491528 | tf_op jit(solution)/shard_map/ppermute | solution.py:440
  29.5 12.1 %collective-permute-start.13 = (bf16[320,256]{1,0:T(8,128)(2,1)S(1)}, bf16[320,256]{1,0:T(8,128)(2,1)S(1)}, u32[]{:S(2)}, u32[]{:S(2)}) collective-permute-start(bf16[320,256]{1,0:T(8,128)(2,1)S(1)} %get-tuple-element.112.refs_1_.refs_10_.d_u), channel_id=1, source_target_pairs={{0,4},{1,5},{2,6},{3,7},{4,0},{5,1},{6,2},{7,3},{8,12},{9,13},{10,... | collective-permute-start | bytes 491528 | tf_op jit(solution)/shard_map/ppermute | solution.py:440
  31.3 10.3 %collective-permute-start.14 = (bf16[320,256]{1,0:T(8,128)(2,1)S(1)}, bf16[320,256]{1,0:T(8,128)(2,1)S(1)}, u32[]{:S(2)}, u32[]{:S(2)}) collective-permute-start(bf16[320,256]{1,0:T(8,128)(2,1)S(1)} %get-tuple-element.112.refs_1_.refs_10_.d_u), channel_id=1, source_target_pairs={{0,6},{1,7},{2,4},{3,5},{4,2},{5,3},{6,0},{7,1},{8,14},{9,15},{10,... | collective-permute-start | bytes 491528 | tf_op jit(solution)/shard_map/ppermute | solution.py:440
  35.7 16.4 %collective-permute-start.17 = (bf16[512,256]{1,0:T(8,128)(2,1)S(1)}, bf16[512,256]{1,0:T(8,128)(2,1)S(1)}, u32[]{:S(2)}, u32[]{:S(2)}) collective-permute-start(bf16[512,256]{1,0:T(8,128)(2,1)S(1)} %get-tuple-element.107.d.refs_1_), channel_id=1, source_target_pairs={{0,2},{1,3},{2,0},{3,1},{4,6},{5,7},{6,4},{7,5},{8,10},{9,11},{10,... | collective-permute-start | bytes 786440 | tf_op jit(solution)/shard_map/ppermute | solution.py:440
  36.2 15.9 %collective-permute-start.18 = (bf16[512,256]{1,0:T(8,128)(2,1)S(1)}, bf16[512,256]{1,0:T(8,128)(2,1)S(1)}, u32[]{:S(2)}, u32[]{:S(2)}) collective-permute-start(bf16[512,256]{1,0:T(8,128)(2,1)S(1)} %get-tuple-element.107.d.refs_1_), channel_id=1, source_target_pairs={{0,4},{1,5},{2,6},{3,7},{4,0},{5,1},{6,2},{7,3},{8,12},{9,13},{10,... | collective-permute-start | bytes 786440 | tf_op jit(solution)/shard_map/ppermute | solution.py:440
  38.0 14.1 %collective-permute-start.19 = (bf16[512,256]{1,0:T(8,128)(2,1)S(1)}, bf16[512,256]{1,0:T(8,128)(2,1)S(1)}, u32[]{:S(2)}, u32[]{:S(2)}) collective-permute-start(bf16[512,256]{1,0:T(8,128)(2,1)S(1)} %get-tuple-element.107.d.refs_1_), channel_id=1, source_target_pairs={{0,6},{1,7},{2,4},{3,5},{4,2},{5,3},{6,0},{7,1},{8,14},{9,15},{10,... | collective-permute-start | bytes 786440 | tf_op jit(solution)/shard_map/ppermute | solution.py:440
  42.7 2.9 %collective-permute-start.15 = (bf16[2,288,128]{2,1,0:T(8,128)(2,1)S(1)}, bf16[2,288,128]{2,1,0:T(8,128)(2,1)S(1)}, u32[]{:S(2)}, u32[]{:S(2)}) collective-permute-start(bf16[2,288,128]{2,1,0:T(8,128)(2,1)S(1)} %get-tuple-element.116), channel_id=1, source_target_pairs={{0,1},{1,0},{2,3},{3,2},{4,5},{5,4},{6,7},{7,6},{8,9},{9,8},{10,11... | collective-permute-start | bytes 442376 | tf_op jit(solution)/shard_map/ppermute | solution.py:440
  42.8 2.8 %collective-permute-start.16 = (bf16[2,288,128]{2,1,0:T(8,128)(2,1)S(1)}, bf16[2,288,128]{2,1,0:T(8,128)(2,1)S(1)}, u32[]{:S(2)}, u32[]{:S(2)}) collective-permute-start(bf16[2,288,128]{2,1,0:T(8,128)(2,1)S(1)} %get-tuple-element.117), channel_id=1, source_target_pairs={{0,1},{1,0},{2,3},{3,2},{4,5},{5,4},{6,7},{7,6},{8,9},{9,8},{10,11... | collective-permute-start | bytes 442376 | tf_op jit(solution)/shard_map/ppermute | solution.py:440
  45.7 9.4 %collective-permute-start.20 = (bf16[288,256]{1,0:T(8,128)(2,1)S(1)}, bf16[288,256]{1,0:T(8,128)(2,1)S(1)}, u32[]{:S(2)}, u32[]{:S(2)}) collective-permute-start(bf16[288,256]{1,0:T(8,128)(2,1)S(1)} %bitcast.21), channel_id=1, source_target_pairs={{0,8},{1,9},{2,10},{3,11},{4,12},{5,13},{6,14},{7,15},{8,0},{9,1},... | collective-permute-start | bytes 442376 | tf_op jit(solution)/shard_map/ppermute | solution.py:440
  53.2 1.9 %collective-permute-start.21 = (bf16[2,288,256]{2,1,0:T(8,128)(2,1)S(1)}, bf16[2,288,256]{2,1,0:T(8,128)(2,1)S(1)}, u32[]{:S(2)}, u32[]{:S(2)}) collective-permute-start(bf16[2,288,256]{2,1,0:T(8,128)(2,1)S(1)} %get-tuple-element.129), channel_id=1, source_target_pairs={{0,1},{1,0},{2,3},{3,2},{4,5},{5,4},{6,7},{7,6},{8,9},{9,8},{10,11... | collective-permute-start | bytes 884744 | tf_op jit(solution)/shard_map/ppermute | solution.py:440
  54.4 5.6 %collective-permute-start.22 = (bf16[2,288,128]{2,1,0:T(8,128)(2,1)S(1)}, bf16[2,288,128]{2,1,0:T(8,128)(2,1)S(1)}, u32[]{:S(2)}, u32[]{:S(2)}) collective-permute-start(bf16[2,288,128]{2,1,0:T(8,128)(2,1)S(1)} %get-tuple-element.132), channel_id=1, source_target_pairs={{0,1},{1,0},{2,3},{3,2},{4,5},{5,4},{6,7},{7,6},{8,9},{9,8},{10,11... | collective-permute-start | bytes 442376 | tf_op jit(solution)/shard_map/ppermute | solution.py:440
  55.0 5.0 %collective-permute-start.23 = (bf16[2,288,128]{2,1,0:T(8,128)(2,1)S(1)}, bf16[2,288,128]{2,1,0:T(8,128)(2,1)S(1)}, u32[]{:S(2)}, u32[]{:S(2)}) collective-permute-start(bf16[2,288,128]{2,1,0:T(8,128)(2,1)S(1)} %get-tuple-element.133), channel_id=1, source_target_pairs={{0,1},{1,0},{2,3},{3,2},{4,5},{5,4},{6,7},{7,6},{8,9},{9,8},{10,11... | collective-permute-start | bytes 442376 | tf_op jit(solution)/shard_map/ppermute | solution.py:440
  55.2 14.2 %collective-permute-start.24 = (bf16[288,256]{1,0:T(8,128)(2,1)S(1)}, bf16[288,256]{1,0:T(8,128)(2,1)S(1)}, u32[]{:S(2)}, u32[]{:S(2)}) collective-permute-start(bf16[288,256]{1,0:T(8,128)(2,1)S(1)} %bitcast.22), channel_id=1, source_target_pairs={{0,8},{1,9},{2,10},{3,11},{4,12},{5,13},{6,14},{7,15},{8,0},{9,1},... | collective-permute-start | bytes 442376 | tf_op jit(solution)/shard_map/ppermute | solution.py:440
  58.3 11.9 %collective-permute-start.25 = (bf16[32,512]{1,0:T(8,128)(2,1)S(1)}, bf16[32,512]{1,0:T(8,128)(2,1)S(1)}, u32[]{:S(2)}, u32[]{:S(2)}) collective-permute-start(bf16[32,512]{1,0:T(8,128)(2,1)S(1)} %get-tuple-element.138), channel_id=1, source_target_pairs={{0,1},{1,0},{2,3},{3,2},{4,5},{5,4},{6,7},{7,6},{8,9},{9,8},{10,11... | collective-permute-start | bytes 98312 | tf_op jit(solution)/shard_map/ppermute | solution.py:440
  58.5 11.7 %collective-permute-start.26 = (bf16[32,512]{1,0:T(8,128)(2,1)S(1)}, bf16[32,512]{1,0:T(8,128)(2,1)S(1)}, u32[]{:S(2)}, u32[]{:S(2)}) collective-permute-start(bf16[32,512]{1,0:T(8,128)(2,1)S(1)} %get-tuple-element.139), channel_id=1, source_target_pairs={{0,15},{1,2},{2,1},{3,4},{4,3},{5,6},{6,5},{7,8},{8,7},{9,10},{10,... | collective-permute-start | bytes 98312 | tf_op jit(solution)/shard_map/ppermute | solution.py:443
  60.1 12.5 %collective-permute-start.27 = (bf16[288,256]{1,0:T(8,128)(2,1)S(1)}, bf16[288,256]{1,0:T(8,128)(2,1)S(1)}, u32[]{:S(2)}, u32[]{:S(2)}) collective-permute-start(bf16[288,256]{1,0:T(8,128)(2,1)S(1)} %bitcast.23), channel_id=1, source_target_pairs={{0,8},{1,9},{2,10},{3,11},{4,12},{5,13},{6,14},{7,15},{8,0},{9,1},... | collective-permute-start | bytes 442376 | tf_op jit(solution)/shard_map/ppermute | solution.py:440

commit v6 on v5

--- a/solution.py
+++ b/solution.py
@@ -511,12 +511,12 @@
             (bc.shape, F32),
             (g.shape, BF),
         ],
-        after(xh, *x_near), r1p, r1n, turn, m0, m2, wg_v, bg_v, sel, wc, bc, g,
+        xh, r1p, r1n, turn, m0, m2, wg_v, bg_v, sel, wc, bc, g,
         hbm=(9, 10, 11), scratch=[pltpu.SemaphoreType.DMA((3,))], cost=5,
     )
     r2p, r2n = exchange(s2n, s2p)
     pack_near = near(after(pack, *x_near))
-    (acc_x,) = run("cand_x", functools.partial(cand_x_kernel, side), [((cells, c), F32)], f, wc_v, bc_v)
+    (acc_x,) = run("cand_x", functools.partial(cand_x_kernel, side), [((cells, c), F32)], after(f, *x_near), wc_v, bc_v)
     d_c, d_u, _ = run(
         "cand", functools.partial(cand_kernel, side),
         [((cells, c), BF), ((cells + rim, c), BF), ((3, band, c), BF)],
@@ -528,7 +528,7 @@
         d_c, wc_v, rim_sel,
     )
     r3p, r3n = exchange(s3n, s3p)
-    u_near = near(after(d_u, s3n, *pack_near))
+    u_near = near(d_u)
     rh_near, taps_v = run(
         "near_reset", functools.partial(near_reset_kernel, side), [((3, cells, c), BF), (taps.shape, BF)],
         *x_near, *pack_near, m0, m2, wg_v, bg_v, taps,

time: 73.5 us -> 69.5 us (0.946)
  starting transfers between devices: 37.1 us -> 29.1 us
  waiting for transfers between devices: 9.17 us -> 13.1 us
    ppermute x24, starting transfers between devices: 24.9 us -> 18.5 us  [swap(): return lax.ppermute(u, 'tile', [(i, i ^ k) for i in range(tiles)])]
    ppermute x24, waiting for transfers between devices: 9.16 us -> 11.7 us  [swap(): return lax.ppermute(u, 'tile', [(i, i ^ k) for i in range(tiles)])]
    ppermute x4, starting transfers between devices: 12.2 us -> 10.6 us  [exchange(): return (swap(s_first, 1), lax.ppermute(s_second, 'tile', cross))]
    ppermute x4, waiting for transfers between devices: 0.01 us -> 1.38 us  [exchange(): return (swap(s_first, 1), lax.ppermute(s_second, 'tile', cross))]
  transfers between devices with their start and end apart: 28 -> 28, of which waited for: 3 -> 6; matrix products, arithmetic and copies ran while one was open for 0% -> 0% of each run, Pallas kernels for 32% -> 35%
where the time goes in v6:
time: 69.5 us; the launch traced here: 69.3 us
  starting transfers between devices  29.1 us (42%)
  Pallas kernels  26.2 us (38%)
  waiting for transfers between devices  13.1 us (19%)
  between operations  0.87 us (1%)
    pallas_call x22, Pallas kernels, call(): pl.pallas_call(body, out_shape=[pltpu.VMEM(s, d) if pin else jax.ShapeDty...  26.2 us
    ppermute x24, starting transfers between devices, swap(): return lax.ppermute(u, 'tile', [(i, i ^ k) for i in range(tiles)])  18.5 us
    ppermute x24, waiting for transfers between devices, swap(): return lax.ppermute(u, 'tile', [(i, i ^ k) for i in range(tiles)])  11.7 us
    ppermute x4, starting transfers between devices, exchange(): return (swap(s_first, 1), lax.ppermute(s_second, 'tile', cross))  10.6 us
  transfers between devices with their start and end apart: 28, of which 6 were waited for; matrix products, arithmetic and copies ran while one was open for 0% of the time, Pallas kernels for 35%

profile of v6, /device:TPU:0, one launch (start us, length us, event | category | flops | bytes accessed | tf_op | source)
XLA Modules:
  0.0 69.3 jit_solution(15714355081885124183)
XLA Ops:
  0.6 1.2 %route.1 = (bf16[256,512]{1,0:T(8,128)(2,1)S(1)}, bf16[32,512]{1,0:T(8,128)(2,1)S(1)}, bf16[32,512]{1,0:T(8,128)(2,1)S(1)}, bf16[64,256]{1,0:T(8,128)(2,1)S(1)},...) custom-call(s32[4,16]{1,0:T(4,128)} %bitcast.26, s32[4,16]{1,0:T(4,128)} %bitcast.27, ...), custom_call_target="tpu_custom_call" | custom-call | tf_op jit(solution)/shard_map/route/pallas_call | solution.py:32
  2.4 5.7 %collective-permute-start.1 = (bf16[32,512]{1,0:T(8,128)(2,1)S(1)}, bf16[32,512]{1,0:T(8,128)(2,1)S(1)}, u32[]{:S(2)}, u32[]{:S(2)}) collective-permute-start(bf16[32,512]{1,0:T(8,128)(2,1)S(1)} %get-tuple-element.78), channel_id=1, source_target_pairs={{0,15},{1,2},{2,1},{3,4},{4,3},{5,6},{6,5},{7,8},{8,7},{9,10},{10,... | collective-permute-start | bytes 98312 | tf_op jit(solution)/shard_map/ppermute | solution.py:443
  8.1 3.5 %collective-permute-start.4 = (bf16[256,256]{1,0:T(8,128)(2,1)}, bf16[256,256]{1,0:T(8,128)(2,1)S(1)}, u32[]{:S(2)}, u32[]{:S(2)}) collective-permute-start(bf16[256,256]{1,0:T(8,128)(2,1)} %bitcast.17), channel_id=1, source_target_pairs={{0,6},{1,7},{2,4},{3,5},{4,2},{5,3},{6,0},{7,1},{8,14},{9,15},{10,... | collective-permute-start | bytes 393224 | tf_op jit(solution)/shard_map/ppermute | solution.py:440
  11.5 2.5 %load_gate.1 = (bf16[9,512,512]{2,1,0:T(8,128)(2,1)S(1)}, bf16[288,320]{1,0:T(8,128)(2,1)S(1)}, bf16[288,320]{1,0:T(8,128)(2,1)S(1)}, f32[1,512]{1,0:T(1,128)S(1)}) custom-call(bf16[9,512,512]{2,1,0:T(8,128)(2,1)} %bitcast.24, bf16[288,320]{1,0:T(8,128)(2,1)} %constant.6.clone.refs_1_, bf16[288,320]{1,0:T(8,128)(2,1)} %constant.7.clone.refs_2_, ...), custom_call_target="tpu_custom_call" | custom-call | tf_op jit(solution)/shard_map/load_gate/pallas_call | solution.py:32
  14.0 1.9 %gate.1 = (f32[256,512]{1,0:T(8,128)S(1)}, bf16[256,256]{1,0:T(8,128)(2,1)S(1)}, bf16[384,256]{1,0:T(8,128)(2,1)S(1)}, bf16[32,256]{1,0:T(8,128)(2,1)S(1)}, bf16...) custom-call(bf16[256,512]{1,0:T(8,128)(2,1)S(1)} %get-tuple-element., ...), custom_call_target="tpu_custom_call" | custom-call | flops 5000000000 | tf_op jit(solution)/shard_map/gate/pallas_call | solution.py:32
  16.7 1.6 %collective-permute-start.7 = (bf16[384,256]{1,0:T(8,128)(2,1)S(1)}, bf16[384,256]{1,0:T(8,128)(2,1)S(1)}, u32[]{:S(2)}, u32[]{:S(2)}) collective-permute-start(bf16[384,256]{1,0:T(8,128)(2,1)S(1)} %get-tuple-element.100.refs_4_), channel_id=1, source_target_pairs={{0,2},{1,3},{2,0},{3,1},{4,6},{5,7},{6,4},{7,5},{8,10},{9,11},{10,... | collective-permute-start | bytes 589832 | tf_op jit(solution)/shard_map/ppermute | solution.py:440
  18.3 2.0 %collective-permute-start.9 = (bf16[384,256]{1,0:T(8,128)(2,1)S(1)}, bf16[384,256]{1,0:T(8,128)(2,1)S(1)}, u32[]{:S(2)}, u32[]{:S(2)}) collective-permute-start(bf16[384,256]{1,0:T(8,128)(2,1)S(1)} %get-tuple-element.100.refs_4_), channel_id=1, source_target_pairs={{0,6},{1,7},{2,4},{3,5},{4,2},{5,3},{6,0},{7,1},{8,14},{9,15},{10,... | collective-permute-start | bytes 589832 | tf_op jit(solution)/shard_map/ppermute | solution.py:440
  20.7 1.4 %collective-permute-done.6.rn = bf16[32,256]{1,0:T(8,128)(2,1)S(1)} collective-permute-done((bf16[32,256]{1,0:T(8,128)(2,1)S(1)}, bf16[32,256]{1,0:T(8,128)(2,1)S(1)}, u32[]{:S(2)}, u32[]{:S(2)}) %collective-permute-start.6) | collective-permute-done | bytes 16416 | tf_op jit(solution)/shard_map/ppermute | solution.py:443
  22.1 1.3 %cand.1 = (bf16[256,256]{1,0:T(8,128)(2,1)S(1)}, bf16[320,256]{1,0:T(8,128)(2,1)S(1)}, bf16[3,288,256]{2,1,0:T(8,128)(2,1)}) custom-call(f32[256,256]{1,0:T(8,128)S(1)} %cand_x.1.acc, bf16[256,256]{1,0:T(8,128)(2,1)S(1)} %get-tuple-element.90.rh.refs_8_, bf16[32,256]{1,0:T(8,128)(2,1)S(1)} %collective-permute-done.5.rp, ...), custom_call_target="tpu_custom_call" | custom-call | flops 3000000000 | tf_op jit(solution)/shard_map/cand/pallas_call | solution.py:32
  23.4 1.5 %back_rh.1 = (f32[256,256]{1,0:T(8,128)S(1)}, bf16[32,256]{1,0:T(8,128)(2,1)S(1)}, bf16[32,256]{1,0:T(8,128)(2,1)S(1)}, f32[3,288,256]{2,1,0:T(8,128)}) custom-call(bf16[256,256]{1,0:T(8,128)(2,1)S(1)} %get-tuple-element.117.d.d_c, bf16[9,512,256]{2,1,0:T(8,128)(2,1)S(1)} %get-tuple-element.88.w.wc, bf16[64,544]{1,0:T(8,128)(2,1)S(1)} %get-tuple-element.96.rim_sel), custom_call_target="tpu_custom_call" | custom-call | tf_op jit(solution)/shard_map/back_rh/pallas_call | solution.py:32
  25.0 1.7 %collective-permute-start.11 = (bf16[32,256]{1,0:T(8,128)(2,1)S(1)}, bf16[32,256]{1,0:T(8,128)(2,1)S(1)}, u32[]{:S(2)}, u32[]{:S(2)}) collective-permute-start(bf16[32,256]{1,0:T(8,128)(2,1)S(1)} %get-tuple-element.104), channel_id=1, source_target_pairs={{0,15},{1,2},{2,1},{3,4},{4,3},{5,6},{6,5},{7,8},{8,7},{9,10},{10,... | collective-permute-start | bytes 49160 | tf_op jit(solution)/shard_map/ppermute | solution.py:443
  27.1 2.0 %collective-permute-done.9.refs_7_ = bf16[384,256]{1,0:T(8,128)(2,1)S(1)} collective-permute-done((bf16[384,256]{1,0:T(8,128)(2,1)S(1)}, bf16[384,256]{1,0:T(8,128)(2,1)S(1)}, u32[]{:S(2)}, u32[]{:S(2)}) %collective-permute-start.9) | collective-permute-done | bytes 196640 | tf_op jit(solution)/shard_map/ppermute | solution.py:440
  29.1 1.0 %collective-permute-start.14 = (bf16[320,256]{1,0:T(8,128)(2,1)S(1)}, bf16[320,256]{1,0:T(8,128)(2,1)S(1)}, u32[]{:S(2)}, u32[]{:S(2)}) collective-permute-start(bf16[320,256]{1,0:T(8,128)(2,1)S(1)} %get-tuple-element.110.refs_1_.refs_10_.d_u), channel_id=1, source_target_pairs={{0,6},{1,7},{2,4},{3,5},{4,2},{5,3},{6,0},{7,1},{8,14},{9,15},{10,... | collective-permute-start | bytes 491528 | tf_op jit(solution)/shard_map/ppermute | solution.py:440
  30.2 2.9 %near_reset.1 = (bf16[3,256,256]{2,1,0:T(8,128)(2,1)S(1)}, bf16[9,320,256]{2,1,0:T(8,128)(2,1)S(1)}) custom-call(bf16[256,256]{1,0:T(8,128)(2,1)S(1)} %bitcast.18, bf16[256,256]{1,0:T(8,128)(2,1)S(1)} %collective-permute-done.2.refs_1_, bf16[256,256]{1,0:T(8,128)(2,1)S(1)} %collective-permute-done.3.refs_2_, ...), custom_call_target="tpu_custom_call" | custom-call | tf_op jit(solution)/shard_map/near_reset/pallas_call | solution.py:32
  33.3 0.8 %collective-permute-start.17 = (bf16[512,256]{1,0:T(8,128)(2,1)S(1)}, bf16[512,256]{1,0:T(8,128)(2,1)S(1)}, u32[]{:S(2)}, u32[]{:S(2)}) collective-permute-start(bf16[512,256]{1,0:T(8,128)(2,1)S(1)} %get-tuple-element.106.d.refs_1_), channel_id=1, source_target_pairs={{0,2},{1,3},{2,0},{3,1},{4,6},{5,7},{6,4},{7,5},{8,10},{9,11},{10,... | collective-permute-start | bytes 786440 | tf_op jit(solution)/shard_map/ppermute | solution.py:440
  34.1 1.7 %collective-permute-start.18 = (bf16[512,256]{1,0:T(8,128)(2,1)S(1)}, bf16[512,256]{1,0:T(8,128)(2,1)S(1)}, u32[]{:S(2)}, u32[]{:S(2)}) collective-permute-start(bf16[512,256]{1,0:T(8,128)(2,1)S(1)} %get-tuple-element.106.d.refs_1_), channel_id=1, source_target_pairs={{0,4},{1,5},{2,6},{3,7},{4,0},{5,1},{6,2},{7,3},{8,12},{9,13},{10,... | collective-permute-start | bytes 786440 | tf_op jit(solution)/shard_map/ppermute | solution.py:440
  36.0 0.9 %collective-permute-start.19 = (bf16[512,256]{1,0:T(8,128)(2,1)S(1)}, bf16[512,256]{1,0:T(8,128)(2,1)S(1)}, u32[]{:S(2)}, u32[]{:S(2)}) collective-permute-start(bf16[512,256]{1,0:T(8,128)(2,1)S(1)} %get-tuple-element.106.d.refs_1_), channel_id=1, source_target_pairs={{0,6},{1,7},{2,4},{3,5},{4,2},{5,3},{6,0},{7,1},{8,14},{9,15},{10,... | collective-permute-start | bytes 786440 | tf_op jit(solution)/shard_map/ppermute | solution.py:440
  36.9 2.3 %lhs_gate.1.refs_0_ = bf16[4,384,1024]{2,1,0:T(8,128)(2,1)S(1)} custom-call(bf16[256,256]{1,0:T(8,128)(2,1)S(1)} %bitcast.19, bf16[256,256]{1,0:T(8,128)(2,1)S(1)} %collective-permute-done.2.refs_1_, bf16[256,256]{1,0:T(8,128)(2,1)S(1)} %collective-permute-done.3.refs_2_, bf16[256,256]{1,0:T(8,128)(2,1)S(1)} %collective-permute-done.4.refs_3_, ...), custom_call_target="tpu_custom_call" | custom-call | tf_op jit(solution)/shard_map/lhs_gate/pallas_call | solution.py:32
  39.2 1.1 %weights_update.1 = (f32[2,288,256]{2,1,0:T(8,128)S(1)}, bf16[2,288,128]{2,1,0:T(8,128)(2,1)S(1)}, bf16[2,288,128]{2,1,0:T(8,128)(2,1)S(1)}) custom-call(bf16[4,384,1024]{2,1,0:T(8,128)(2,1)S(1)} %lhs_gate.1.refs_0_, bf16[320,256]{1,0:T(8,128)(2,1)S(1)} %get-tuple-element.110.refs_1_.refs_10_.d_u, ...), custom_call_target="tpu_custom_call" | custom-call | tf_op jit(solution)/shard_map/weights_update/pallas_call | solution.py:32
  40.9 2.3 %lhs_cand.1.refs_0_ = bf16[4,384,1024]{2,1,0:T(8,128)(2,1)S(1)} custom-call(bf16[256,256]{1,0:T(8,128)(2,1)S(1)} %bitcast.20, bf16[256,256]{1,0:T(8,128)(2,1)S(1)} %collective-permute-done.2.refs_1_, bf16[256,256]{1,0:T(8,128)(2,1)S(1)} %collective-permute-done.3.refs_2_, bf16[256,256]{1,0:T(8,128)(2,1)S(1)} %collective-permute-done.4.refs_3_, ...), custom_call_target="tpu_custom_call" | custom-call | tf_op jit(solution)/shard_map/lhs_cand/pallas_call | solution.py:32
  43.3 1.6 %collective-permute-start.20 = (bf16[288,256]{1,0:T(8,128)(2,1)S(1)}, bf16[288,256]{1,0:T(8,128)(2,1)S(1)}, u32[]{:S(2)}, u32[]{:S(2)}) collective-permute-start(bf16[288,256]{1,0:T(8,128)(2,1)S(1)} %bitcast.21), channel_id=1, source_target_pairs={{0,8},{1,9},{2,10},{3,11},{4,12},{5,13},{6,14},{7,15},{8,0},{9,1},... | collective-permute-start | bytes 442376 | tf_op jit(solution)/shard_map/ppermute | solution.py:440
  44.9 1.2 %back_early.1.early = f32[3,288,512]{2,1,0:T(8,128)S(1)} custom-call(bf16[256,256]{1,0:T(8,128)(2,1)S(1)} %get-tuple-element.117.d.d_c, bf16[320,256]{1,0:T(8,128)(2,1)S(1)} %get-tuple-element.110.refs_1_.refs_10_.d_u, bf16[9,512,256]{2,1,0:T(8,128)(2,1)S(1)} %get-tuple-element.88.w.wc, bf16[9,512,512]{2,1,0:T(8,128)(2,1)S(1)} %get-tuple-element.75.w.refs_10_.wg), custom_call_target="tpu_custom_call" | custom-call | tf_op jit(solution)/shard_map/back_early/pallas_call | solution.py:32
  46.0 2.3 %back_gate.1 = (f32[256,512]{1,0:T(8,128)S(1)}, bf16[32,512]{1,0:T(8,128)(2,1)S(1)}, bf16[32,512]{1,0:T(8,128)(2,1)S(1)}, f32[3,288,512]{2,1,0:T(8,128)}) custom-call(f32[3,288,512]{2,1,0:T(8,128)S(1)} %back_early.1.early, bf16[512,256]{1,0:T(8,128)(2,1)S(1)} %get-tuple-element.106.d.refs_1_, bf16[9,512,512]{2,1,0:T(8,128)(2,1)S(1)} %get-tuple-element.75.w.refs_10_.wg, ...), custom_call_target="tpu_custom_call" | custom-call | tf_op jit(solution)/shard_map/back_gate/pallas_call | solution.py:32
  48.3 1.1 %weights_reset.1 = (f32[2,288,256]{2,1,0:T(8,128)S(1)}, bf16[2,288,256]{2,1,0:T(8,128)(2,1)S(1)}) custom-call(bf16[4,384,1024]{2,1,0:T(8,128)(2,1)S(1)} %lhs_gate.1.refs_0_, bf16[512,256]{1,0:T(8,128)(2,1)S(1)} %get-tuple-element.106.d.refs_1_, bf16[512,256]{1,0:T(8,128)(2,1)S(1)} %collective-permute-done.17.refs_2_, ...), custom_call_target="tpu_custom_call" | custom-call | tf_op jit(solution)/shard_map/weights_reset/pallas_call | solution.py:32
  49.5 1.1 %weights_cand.1 = (f32[2,288,256]{2,1,0:T(8,128)S(1)}, bf16[2,288,128]{2,1,0:T(8,128)(2,1)S(1)}, bf16[2,288,128]{2,1,0:T(8,128)(2,1)S(1)}) custom-call(bf16[4,384,1024]{2,1,0:T(8,128)(2,1)S(1)} %lhs_cand.1.refs_0_, bf16[512,256]{1,0:T(8,128)(2,1)S(1)} %get-tuple-element.106.d.refs_1_, bf16[512,256]{1,0:T(8,128)(2,1)S(1)} %collective-permute-done.17.refs_2_, ...), custom_call_target="tpu_custom_call" | custom-call | tf_op jit(solution)/shard_map/weights_cand/pallas_call | solution.py:32
  51.3 2.0 %collective-permute-done.20.refs_1_ = bf16[288,256]{1,0:T(8,128)(2,1)S(1)} collective-permute-done((bf16[288,256]{1,0:T(8,128)(2,1)S(1)}, bf16[288,256]{1,0:T(8,128)(2,1)S(1)}, u32[]{:S(2)}, u32[]{:S(2)}) %collective-permute-start.20) | collective-permute-done | bytes 147488 | tf_op jit(solution)/shard_map/ppermute | solution.py:440
  53.4 0.9 %collective-permute-start.24 = (bf16[288,256]{1,0:T(8,128)(2,1)S(1)}, bf16[288,256]{1,0:T(8,128)(2,1)S(1)}, u32[]{:S(2)}, u32[]{:S(2)}) collective-permute-start(bf16[288,256]{1,0:T(8,128)(2,1)S(1)} %bitcast.22), channel_id=1, source_target_pairs={{0,8},{1,9},{2,10},{3,11},{4,12},{5,13},{6,14},{7,15},{8,0},{9,1},... | collective-permute-start | bytes 442376 | tf_op jit(solution)/shard_map/ppermute | solution.py:440
  54.4 2.7 %collective-permute-start.26 = (bf16[32,512]{1,0:T(8,128)(2,1)S(1)}, bf16[32,512]{1,0:T(8,128)(2,1)S(1)}, u32[]{:S(2)}, u32[]{:S(2)}) collective-permute-start(bf16[32,512]{1,0:T(8,128)(2,1)S(1)} %get-tuple-element.137), channel_id=1, source_target_pairs={{0,15},{1,2},{2,1},{3,4},{4,3},{5,6},{6,5},{7,8},{8,7},{9,10},{10,... | collective-permute-start | bytes 98312 | tf_op jit(solution)/shard_map/ppermute | solution.py:443
  57.2 2.0 %collective-permute-start.27 = (bf16[288,256]{1,0:T(8,128)(2,1)S(1)}, bf16[288,256]{1,0:T(8,128)(2,1)S(1)}, u32[]{:S(2)}, u32[]{:S(2)}) collective-permute-start(bf16[288,256]{1,0:T(8,128)(2,1)S(1)} %bitcast.23), channel_id=1, source_target_pairs={{0,8},{1,9},{2,10},{3,11},{4,12},{5,13},{6,14},{7,15},{8,0},{9,1},... | collective-permute-start | bytes 442376 | tf_op jit(solution)/shard_map/ppermute | solution.py:440
  59.2 7.4 %collective-permute-done.24.refs_1_ = bf16[288,256]{1,0:T(8,128)(2,1)S(1)} collective-permute-done((bf16[288,256]{1,0:T(8,128)(2,1)S(1)}, bf16[288,256]{1,0:T(8,128)(2,1)S(1)}, u32[]{:S(2)}, u32[]{:S(2)}) %collective-permute-start.24) | collective-permute-done | bytes 147488 | tf_op jit(solution)/shard_map/ppermute | solution.py:440
  66.5 0.9 %sum_gate.1 = f32[288,512]{1,0:T(8,128)} custom-call(f32[288,256]{1,0:T(8,128)S(1)} %sum_update.1.update, f32[288,256]{1,0:T(8,128)S(1)} %get-tuple-element.128.refs_0_, bf16[288,256]{1,0:T(8,128)(2,1)S(1)} %collective-permute-done.24.refs_1_), custom_call_target="tpu_custom_call" | custom-call | tf_op jit(solution)/shard_map/sum_gate/pallas_call | solution.py:32
  67.4 0.9 %final.1 = (bf16[256,256]{1,0:T(8,128)(2,1)}, bf16[256,256]{1,0:T(8,128)(2,1)}) custom-call(f32[256,512]{1,0:T(8,128)S(1)} %get-tuple-element.135.inner, bf16[32,512]{1,0:T(8,128)(2,1)S(1)} %collective-permute-done.25.rp, bf16[32,512]{1,0:T(8,128)(2,1)S(1)} %collective-permute-done.26.rn, bf16[256,64]{1,0:T(8,128)(2,1)S(1)} %get-tuple-element.105.place), custom_call_target="tpu_custom_call" | custom-call | flops 3000000000 | tf_op jit(solution)/shard_map/final/pallas_call | solution.py:32
  (48 shorter events, 5.1 us)
Async XLA Ops:
  1.9 12.1 %collective-permute-start = (bf16[32,512]{1,0:T(8,128)(2,1)S(1)}, bf16[32,512]{1,0:T(8,128)(2,1)S(1)}, u32[]{:S(2)}, u32[]{:S(2)}) collective-permute-start(bf16[32,512]{1,0:T(8,128)(2,1)S(1)} %get-tuple-element.77), channel_id=1, source_target_pairs={{0,1},{1,0},{2,3},{3,2},{4,5},{5,4},{6,7},{7,6},{8,9},{9,8},{10,11... | collective-permute-start | bytes 98312 | tf_op jit(solution)/shard_map/ppermute | solution.py:440
  2.4 11.6 %collective-permute-start.1 = (bf16[32,512]{1,0:T(8,128)(2,1)S(1)}, bf16[32,512]{1,0:T(8,128)(2,1)S(1)}, u32[]{:S(2)}, u32[]{:S(2)}) collective-permute-start(bf16[32,512]{1,0:T(8,128)(2,1)S(1)} %get-tuple-element.78), channel_id=1, source_target_pairs={{0,15},{1,2},{2,1},{3,4},{4,3},{5,6},{6,5},{7,8},{8,7},{9,10},{10,... | collective-permute-start | bytes 98312 | tf_op jit(solution)/shard_map/ppermute | solution.py:443
  8.1 8.6 %collective-permute-start.2 = (bf16[256,256]{1,0:T(8,128)(2,1)}, bf16[256,256]{1,0:T(8,128)(2,1)S(1)}, u32[]{:S(2)}, u32[]{:S(2)}) collective-permute-start(bf16[256,256]{1,0:T(8,128)(2,1)} %bitcast.15), channel_id=1, source_target_pairs={{0,2},{1,3},{2,0},{3,1},{4,6},{5,7},{6,4},{7,5},{8,10},{9,11},{10,... | collective-permute-start | bytes 393224 | tf_op jit(solution)/shard_map/ppermute | solution.py:440
  8.1 8.6 %collective-permute-start.3 = (bf16[256,256]{1,0:T(8,128)(2,1)}, bf16[256,256]{1,0:T(8,128)(2,1)S(1)}, u32[]{:S(2)}, u32[]{:S(2)}) collective-permute-start(bf16[256,256]{1,0:T(8,128)(2,1)} %bitcast.16), channel_id=1, source_target_pairs={{0,4},{1,5},{2,6},{3,7},{4,0},{5,1},{6,2},{7,3},{8,12},{9,13},{10,... | collective-permute-start | bytes 393224 | tf_op jit(solution)/shard_map/ppermute | solution.py:440
  8.1 8.6 %collective-permute-start.4 = (bf16[256,256]{1,0:T(8,128)(2,1)}, bf16[256,256]{1,0:T(8,128)(2,1)S(1)}, u32[]{:S(2)}, u32[]{:S(2)}) collective-permute-start(bf16[256,256]{1,0:T(8,128)(2,1)} %bitcast.17), channel_id=1, source_target_pairs={{0,6},{1,7},{2,4},{3,5},{4,2},{5,3},{6,0},{7,1},{8,14},{9,15},{10,... | collective-permute-start | bytes 393224 | tf_op jit(solution)/shard_map/ppermute | solution.py:440
  16.0 4.7 %collective-permute-start.5 = (bf16[32,256]{1,0:T(8,128)(2,1)S(1)}, bf16[32,256]{1,0:T(8,128)(2,1)S(1)}, u32[]{:S(2)}, u32[]{:S(2)}) collective-permute-start(bf16[32,256]{1,0:T(8,128)(2,1)S(1)} %get-tuple-element.91), channel_id=1, source_target_pairs={{0,1},{1,0},{2,3},{3,2},{4,5},{5,4},{6,7},{7,6},{8,9},{9,8},{10,11... | collective-permute-start | bytes 49160 | tf_op jit(solution)/shard_map/ppermute | solution.py:440
  16.0 6.0 %collective-permute-start.6 = (bf16[32,256]{1,0:T(8,128)(2,1)S(1)}, bf16[32,256]{1,0:T(8,128)(2,1)S(1)}, u32[]{:S(2)}, u32[]{:S(2)}) collective-permute-start(bf16[32,256]{1,0:T(8,128)(2,1)S(1)} %get-tuple-element.92), channel_id=1, source_target_pairs={{0,15},{1,2},{2,1},{3,4},{4,3},{5,6},{6,5},{7,8},{8,7},{9,10},{10,... | collective-permute-start | bytes 49160 | tf_op jit(solution)/shard_map/ppermute | solution.py:443
  16.7 10.0 %collective-permute-start.7 = (bf16[384,256]{1,0:T(8,128)(2,1)S(1)}, bf16[384,256]{1,0:T(8,128)(2,1)S(1)}, u32[]{:S(2)}, u32[]{:S(2)}) collective-permute-start(bf16[384,256]{1,0:T(8,128)(2,1)S(1)} %get-tuple-element.100.refs_4_), channel_id=1, source_target_pairs={{0,2},{1,3},{2,0},{3,1},{4,6},{5,7},{6,4},{7,5},{8,10},{9,11},{10,... | collective-permute-start | bytes 589832 | tf_op jit(solution)/shard_map/ppermute | solution.py:440
  18.2 8.9 %collective-permute-start.8 = (bf16[384,256]{1,0:T(8,128)(2,1)S(1)}, bf16[384,256]{1,0:T(8,128)(2,1)S(1)}, u32[]{:S(2)}, u32[]{:S(2)}) collective-permute-start(bf16[384,256]{1,0:T(8,128)(2,1)S(1)} %get-tuple-element.100.refs_4_), channel_id=1, source_target_pairs={{0,4},{1,5},{2,6},{3,7},{4,0},{5,1},{6,2},{7,3},{8,12},{9,13},{10,... | collective-permute-start | bytes 589832 | tf_op jit(solution)/shard_map/ppermute | solution.py:440
  18.3 10.9 %collective-permute-start.9 = (bf16[384,256]{1,0:T(8,128)(2,1)S(1)}, bf16[384,256]{1,0:T(8,128)(2,1)S(1)}, u32[]{:S(2)}, u32[]{:S(2)}) collective-permute-start(bf16[384,256]{1,0:T(8,128)(2,1)S(1)} %get-tuple-element.100.refs_4_), channel_id=1, source_target_pairs={{0,6},{1,7},{2,4},{3,5},{4,2},{5,3},{6,0},{7,1},{8,14},{9,15},{10,... | collective-permute-start | bytes 589832 | tf_op jit(solution)/shard_map/ppermute | solution.py:440
  23.4 6.7 %copy-start = (bf16[1,16,16,256]{3,2,1,0:T(8,128)(2,1)S(1)}, bf16[1,16,16,256]{3,2,1,0:T(8,128)(2,1)}, u32[]{:S(2)}) copy-start(bf16[1,16,16,256]{3,2,1,0:T(8,128)(2,1)} %param.13) | copy-start | bytes 393220
  25.0 8.1 %collective-permute-start.10 = (bf16[32,256]{1,0:T(8,128)(2,1)S(1)}, bf16[32,256]{1,0:T(8,128)(2,1)S(1)}, u32[]{:S(2)}, u32[]{:S(2)}) collective-permute-start(bf16[32,256]{1,0:T(8,128)(2,1)S(1)} %get-tuple-element.103), channel_id=1, source_target_pairs={{0,1},{1,0},{2,3},{3,2},{4,5},{5,4},{6,7},{7,6},{8,9},{9,8},{10,11... | collective-permute-start | bytes 49160 | tf_op jit(solution)/shard_map/ppermute | solution.py:440
  25.0 8.2 %collective-permute-start.11 = (bf16[32,256]{1,0:T(8,128)(2,1)S(1)}, bf16[32,256]{1,0:T(8,128)(2,1)S(1)}, u32[]{:S(2)}, u32[]{:S(2)}) collective-permute-start(bf16[32,256]{1,0:T(8,128)(2,1)S(1)} %get-tuple-element.104), channel_id=1, source_target_pairs={{0,15},{1,2},{2,1},{3,4},{4,3},{5,6},{6,5},{7,8},{8,7},{9,10},{10,... | collective-permute-start | bytes 49160 | tf_op jit(solution)/shard_map/ppermute | solution.py:443
  26.7 9.3 %collective-permute-start.12 = (bf16[320,256]{1,0:T(8,128)(2,1)S(1)}, bf16[320,256]{1,0:T(8,128)(2,1)S(1)}, u32[]{:S(2)}, u32[]{:S(2)}) collective-permute-start(bf16[320,256]{1,0:T(8,128)(2,1)S(1)} %get-tuple-element.110.refs_1_.refs_10_.d_u), channel_id=1, source_target_pairs={{0,2},{1,3},{2,0},{3,1},{4,6},{5,7},{6,4},{7,5},{8,10},{9,11},{10,... | collective-permute-start | bytes 491528 | tf_op jit(solution)/shard_map/ppermute | solution.py:440
  27.1 12.1 %collective-permute-start.13 = (bf16[320,256]{1,0:T(8,128)(2,1)S(1)}, bf16[320,256]{1,0:T(8,128)(2,1)S(1)}, u32[]{:S(2)}, u32[]{:S(2)}) collective-permute-start(bf16[320,256]{1,0:T(8,128)(2,1)S(1)} %get-tuple-element.110.refs_1_.refs_10_.d_u), channel_id=1, source_target_pairs={{0,4},{1,5},{2,6},{3,7},{4,0},{5,1},{6,2},{7,3},{8,12},{9,13},{10,... | collective-permute-start | bytes 491528 | tf_op jit(solution)/shard_map/ppermute | solution.py:440
  29.1 10.1 %collective-permute-start.14 = (bf16[320,256]{1,0:T(8,128)(2,1)S(1)}, bf16[320,256]{1,0:T(8,128)(2,1)S(1)}, u32[]{:S(2)}, u32[]{:S(2)}) collective-permute-start(bf16[320,256]{1,0:T(8,128)(2,1)S(1)} %get-tuple-element.110.refs_1_.refs_10_.d_u), channel_id=1, source_target_pairs={{0,6},{1,7},{2,4},{3,5},{4,2},{5,3},{6,0},{7,1},{8,14},{9,15},{10,... | collective-permute-start | bytes 491528 | tf_op jit(solution)/shard_map/ppermute | solution.py:440
  33.3 15.0 %collective-permute-start.17 = (bf16[512,256]{1,0:T(8,128)(2,1)S(1)}, bf16[512,256]{1,0:T(8,128)(2,1)S(1)}, u32[]{:S(2)}, u32[]{:S(2)}) collective-permute-start(bf16[512,256]{1,0:T(8,128)(2,1)S(1)} %get-tuple-element.106.d.refs_1_), channel_id=1, source_target_pairs={{0,2},{1,3},{2,0},{3,1},{4,6},{5,7},{6,4},{7,5},{8,10},{9,11},{10,... | collective-permute-start | bytes 786440 | tf_op jit(solution)/shard_map/ppermute | solution.py:440
  34.1 14.2 %collective-permute-start.18 = (bf16[512,256]{1,0:T(8,128)(2,1)S(1)}, bf16[512,256]{1,0:T(8,128)(2,1)S(1)}, u32[]{:S(2)}, u32[]{:S(2)}) collective-permute-start(bf16[512,256]{1,0:T(8,128)(2,1)S(1)} %get-tuple-element.106.d.refs_1_), channel_id=1, source_target_pairs={{0,4},{1,5},{2,6},{3,7},{4,0},{5,1},{6,2},{7,3},{8,12},{9,13},{10,... | collective-permute-start | bytes 786440 | tf_op jit(solution)/shard_map/ppermute | solution.py:440
  36.0 12.4 %collective-permute-start.19 = (bf16[512,256]{1,0:T(8,128)(2,1)S(1)}, bf16[512,256]{1,0:T(8,128)(2,1)S(1)}, u32[]{:S(2)}, u32[]{:S(2)}) collective-permute-start(bf16[512,256]{1,0:T(8,128)(2,1)S(1)} %get-tuple-element.106.d.refs_1_), channel_id=1, source_target_pairs={{0,6},{1,7},{2,4},{3,5},{4,2},{5,3},{6,0},{7,1},{8,14},{9,15},{10,... | collective-permute-start | bytes 786440 | tf_op jit(solution)/shard_map/ppermute | solution.py:440
  40.3 2.9 %collective-permute-start.15 = (bf16[2,288,128]{2,1,0:T(8,128)(2,1)S(1)}, bf16[2,288,128]{2,1,0:T(8,128)(2,1)S(1)}, u32[]{:S(2)}, u32[]{:S(2)}) collective-permute-start(bf16[2,288,128]{2,1,0:T(8,128)(2,1)S(1)} %get-tuple-element.114), channel_id=1, source_target_pairs={{0,1},{1,0},{2,3},{3,2},{4,5},{5,4},{6,7},{7,6},{8,9},{9,8},{10,11... | collective-permute-start | bytes 442376 | tf_op jit(solution)/shard_map/ppermute | solution.py:440
  40.4 2.8 %collective-permute-start.16 = (bf16[2,288,128]{2,1,0:T(8,128)(2,1)S(1)}, bf16[2,288,128]{2,1,0:T(8,128)(2,1)S(1)}, u32[]{:S(2)}, u32[]{:S(2)}) collective-permute-start(bf16[2,288,128]{2,1,0:T(8,128)(2,1)S(1)} %get-tuple-element.115), channel_id=1, source_target_pairs={{0,1},{1,0},{2,3},{3,2},{4,5},{5,4},{6,7},{7,6},{8,9},{9,8},{10,11... | collective-permute-start | bytes 442376 | tf_op jit(solution)/shard_map/ppermute | solution.py:440
  43.3 10.0 %collective-permute-start.20 = (bf16[288,256]{1,0:T(8,128)(2,1)S(1)}, bf16[288,256]{1,0:T(8,128)(2,1)S(1)}, u32[]{:S(2)}, u32[]{:S(2)}) collective-permute-start(bf16[288,256]{1,0:T(8,128)(2,1)S(1)} %bitcast.21), channel_id=1, source_target_pairs={{0,8},{1,9},{2,10},{3,11},{4,12},{5,13},{6,14},{7,15},{8,0},{9,1},... | collective-permute-start | bytes 442376 | tf_op jit(solution)/shard_map/ppermute | solution.py:440
  49.5 3.9 %collective-permute-start.21 = (bf16[2,288,256]{2,1,0:T(8,128)(2,1)S(1)}, bf16[2,288,256]{2,1,0:T(8,128)(2,1)S(1)}, u32[]{:S(2)}, u32[]{:S(2)}) collective-permute-start(bf16[2,288,256]{2,1,0:T(8,128)(2,1)S(1)} %get-tuple-element.127), channel_id=1, source_target_pairs={{0,1},{1,0},{2,3},{3,2},{4,5},{5,4},{6,7},{7,6},{8,9},{9,8},{10,11... | collective-permute-start | bytes 884744 | tf_op jit(solution)/shard_map/ppermute | solution.py:440
  50.6 6.5 %collective-permute-start.22 = (bf16[2,288,128]{2,1,0:T(8,128)(2,1)S(1)}, bf16[2,288,128]{2,1,0:T(8,128)(2,1)S(1)}, u32[]{:S(2)}, u32[]{:S(2)}) collective-permute-start(bf16[2,288,128]{2,1,0:T(8,128)(2,1)S(1)} %get-tuple-element.130), channel_id=1, source_target_pairs={{0,1},{1,0},{2,3},{3,2},{4,5},{5,4},{6,7},{7,6},{8,9},{9,8},{10,11... | collective-permute-start | bytes 442376 | tf_op jit(solution)/shard_map/ppermute | solution.py:440
  51.2 5.9 %collective-permute-start.23 = (bf16[2,288,128]{2,1,0:T(8,128)(2,1)S(1)}, bf16[2,288,128]{2,1,0:T(8,128)(2,1)S(1)}, u32[]{:S(2)}, u32[]{:S(2)}) collective-permute-start(bf16[2,288,128]{2,1,0:T(8,128)(2,1)S(1)} %get-tuple-element.131), channel_id=1, source_target_pairs={{0,1},{1,0},{2,3},{3,2},{4,5},{5,4},{6,7},{7,6},{8,9},{9,8},{10,11... | collective-permute-start | bytes 442376 | tf_op jit(solution)/shard_map/ppermute | solution.py:440
  53.4 13.2 %collective-permute-start.24 = (bf16[288,256]{1,0:T(8,128)(2,1)S(1)}, bf16[288,256]{1,0:T(8,128)(2,1)S(1)}, u32[]{:S(2)}, u32[]{:S(2)}) collective-permute-start(bf16[288,256]{1,0:T(8,128)(2,1)S(1)} %bitcast.22), channel_id=1, source_target_pairs={{0,8},{1,9},{2,10},{3,11},{4,12},{5,13},{6,14},{7,15},{8,0},{9,1},... | collective-permute-start | bytes 442376 | tf_op jit(solution)/shard_map/ppermute | solution.py:440
  54.3 13.2 %collective-permute-start.25 = (bf16[32,512]{1,0:T(8,128)(2,1)S(1)}, bf16[32,512]{1,0:T(8,128)(2,1)S(1)}, u32[]{:S(2)}, u32[]{:S(2)}) collective-permute-start(bf16[32,512]{1,0:T(8,128)(2,1)S(1)} %get-tuple-element.136), channel_id=1, source_target_pairs={{0,1},{1,0},{2,3},{3,2},{4,5},{5,4},{6,7},{7,6},{8,9},{9,8},{10,11... | collective-permute-start | bytes 98312 | tf_op jit(solution)/shard_map/ppermute | solution.py:440
  54.4 13.0 %collective-permute-start.26 = (bf16[32,512]{1,0:T(8,128)(2,1)S(1)}, bf16[32,512]{1,0:T(8,128)(2,1)S(1)}, u32[]{:S(2)}, u32[]{:S(2)}) collective-permute-start(bf16[32,512]{1,0:T(8,128)(2,1)S(1)} %get-tuple-element.137), channel_id=1, source_target_pairs={{0,15},{1,2},{2,1},{3,4},{4,3},{5,6},{6,5},{7,8},{8,7},{9,10},{10,... | collective-permute-start | bytes 98312 | tf_op jit(solution)/shard_map/ppermute | solution.py:443
  57.2 11.4 %collective-permute-start.27 = (bf16[288,256]{1,0:T(8,128)(2,1)S(1)}, bf16[288,256]{1,0:T(8,128)(2,1)S(1)}, u32[]{:S(2)}, u32[]{:S(2)}) collective-permute-start(bf16[288,256]{1,0:T(8,128)(2,1)S(1)} %bitcast.23), channel_id=1, source_target_pairs={{0,8},{1,9},{2,10},{3,11},{4,12},{5,13},{6,14},{7,15},{8,0},{9,1},... | collective-permute-start | bytes 442376 | tf_op jit(solution)/shard_map/ppermute | solution.py:440

commit v7 on v6

--- a/solution.py
+++ b/solution.py
@@ -81,9 +81,10 @@
     )
 
 
-def route_kernel(side, tiles, p_in, f_in, s_in, x, h, xh, s_first, s_second, sel, place, turn, rim_sel, partner, flip, slot, sems):
+def route_kernel(side, tiles, p_in, f_in, s_in, x, h, xh, front, s_first, s_second, sel, place, turn, rim_sel, partner, flip, slot, sems):
     c = x.shape[1]
     loads = [(p_in, partner), (f_in, flip), (s_in, slot), (x, xh.at[:, :c]), (h, xh.at[:, c:])]
+    loads += [(x, front.at[:, :c]), (h.at[:, : c - 128], front.at[:, c:])]
     loads = [pltpu.make_async_copy(a, b, sems.at[n]) for n, (a, b) in enumerate(loads)]
     for copy in loads:
         copy.start()
@@ -180,9 +181,9 @@
     gate[...] = act
     reset_h = (act[:, c:] * xh[:, c:].astype(F32)).astype(BF)
     rh[...] = reset_h
-    pack[:cells] = xh[:, c:]
-    pack[cells : cells + rim] = strips[:, :c]
-    pack[cells + rim :] = strips[:, c:]
+    pack[:cells] = xh[:, 2 * c - 128 :]
+    for k in range(2 * c // 128):
+        pack[cells + k * rim : cells + (k + 1) * rim] = strips[:, k * 128 : (k + 1) * 128]
     picked = dot(sel[...], reset_h).astype(BF)
     s_next[...] = picked[: rim // 2]
     s_prev[...] = picked[rim // 2 :]
@@ -300,7 +301,8 @@
     cells, rim, c = side * side, 4 * side, out.shape[2]
     for n in range(3):
         tile = jnp.concatenate([x[n][...], packs[n][:cells]], axis=1)
-        strips = jnp.concatenate([packs[n][cells : cells + rim], packs[n][cells + rim :]], axis=1)
+        strips = [packs[n][cells + k * rim : cells + (k + 1) * rim] for k in range(2 * c // 128)]
+        strips = jnp.concatenate(strips, axis=1)
         frames(side, tile, strips, m0, m2, f.at[n])
     cols = [
         jnp.concatenate([f[n, b, a * side : a * side + cells, :] for n in range(3)], axis=0)
@@ -310,7 +312,7 @@
     rows = [w[t, :, c:] for t in range(9)]
     reset = jax.nn.sigmoid(dot(jnp.concatenate(cols, axis=1), jnp.concatenate(rows, axis=0)) + bias[:, c:])
     for n in range(3):
-        out[n] = (reset[n * cells : (n + 1) * cells] * packs[n][:cells].astype(F32)).astype(BF)
+        out[n] = (reset[n * cells : (n + 1) * cells] * jnp.concatenate([x[n][:, c:], packs[n][:cells]], axis=1).astype(F32)).astype(BF)
     copy.wait()
 
 
@@ -319,23 +321,20 @@
     me = lax.axis_index("tile")
     taps, out, src, turned = refs[-4:]
     cells, rim = side * side, 4 * side
-    c = packs[0].shape[1]
+    c = (x[0].shape[1] + 128) // 2
     per_tap = 2 * c // 128
     for n in range(4):
         lanes = slice(n * 128, (n + 1) * 128)
         for k in range(per_tap):
             at = slice(k * 128, (k + 1) * 128)
             col = slice(at.start % c, at.start % c + 128)
-            if at.start < c:
-                src[k, :cells, lanes] = x[n][:, col]
-                src[k, cells:, lanes] = packs[n][cells : cells + rim, col]
-            elif cand:
+            if cand and at.start >= c:
                 rh, rh_near, ds = more[0], more[1], more[2:]
                 src[k, :cells, lanes] = rh[:, col] if n == 0 else rh_near[n - 1, :, col]
                 src[k, cells:, lanes] = ds[n][cells:, col]
             else:
-                src[k, :cells, lanes] = packs[n][:cells, col]
-                src[k, cells:, lanes] = packs[n][cells + rim :, col]
+                src[k, :cells, lanes] = x[n][:, at] if k < per_tap - 1 else packs[n][:cells]
+                src[k, cells:, lanes] = packs[n][cells + k * rim : cells + (k + 1) * rim]
     for k in range(per_tap):
         turned[k] = src[k].T
     for t in range(out.shape[0]):
@@ -475,10 +474,11 @@
         )
         return [own] + [swap(far[k - 1], 8 * k) for k in range(1, groups)]
 
-    xh, s1n, s1p, sel, place, turn, rim_sel = run(
+    xh, front, s1n, s1p, sel, place, turn, rim_sel = run(
         "route", functools.partial(route_kernel, side, tiles),
         [
             ((cells, 2 * c), BF),
+            ((cells, 2 * c - 128), BF),
             ((half, 2 * c), BF),
             ((half, 2 * c), BF),
             ((rim, cells), BF),
@@ -492,18 +492,18 @@
             pltpu.SMEM((4, tiles), jnp.int32),
             pltpu.SMEM((4, tiles), jnp.int32),
             pltpu.SMEM((tiles,), jnp.int32),
-            pltpu.SemaphoreType.DMA((5,)),
+            pltpu.SemaphoreType.DMA((7,)),
         ],
     )
     r1p, r1n = exchange(s1n, s1p)
-    x_near = near(x)
+    x_near = near(front)
     wg_v, m0, m2, bg_v = load("load_gate", wg, m0, m2, bg)
     gate, rh, pack, s2n, s2p, f, wc_v, bc_v, g_v = run(
         "gate", functools.partial(gate_kernel, side),
         [
             ((cells, 2 * c), F32),
             ((cells, c), BF),
-            ((cells + 2 * rim, c), BF),
+            ((cells + 2 * c // 128 * rim, 128), BF),
             ((half, c), BF),
             ((half, c), BF),
             ((3, band, 2 * c), BF),

time: 69.5 us -> 71.6 us (1.030)
  starting transfers between devices: 29.1 us -> 30.5 us
    ppermute x24, waiting for transfers between devices: 11.7 us -> 13.2 us  [swap(): return lax.ppermute(u, 'tile', [(i, i ^ k) for i in range(tiles)])]
    ppermute x4, starting transfers between devices: 10.6 us -> 11.8 us  [exchange(): return (swap(s_first, 1), lax.ppermute(s_second, 'tile', cross))]
    ppermute x4, waiting for transfers between devices: 1.38 us -> 0.46 us  [exchange(): return (swap(s_first, 1), lax.ppermute(s_second, 'tile', cross))]
  transfers between devices with their start and end apart: 28 -> 28, of which waited for: 6 -> 7; matrix products, arithmetic and copies ran while one was open for 0% -> 0% of each run, Pallas kernels for 35% -> 34%
where the time goes in v7:
time: 71.6 us; the launch traced here: 71.4 us
  starting transfers between devices  30.5 us (43%)
  Pallas kernels  26.3 us (37%)
  waiting for transfers between devices  13.7 us (19%)
  between operations  0.89 us (1%)
    pallas_call x22, Pallas kernels, call(): pl.pallas_call(body, out_shape=[pltpu.VMEM(s, d) if pin else jax.ShapeDty...  26.3 us
    ppermute x24, starting transfers between devices, swap(): return lax.ppermute(u, 'tile', [(i, i ^ k) for i in range(tiles)])  18.7 us
    ppermute x24, waiting for transfers between devices, swap(): return lax.ppermute(u, 'tile', [(i, i ^ k) for i in range(tiles)])  13.2 us
    ppermute x4, starting transfers between devices, exchange(): return (swap(s_first, 1), lax.ppermute(s_second, 'tile', cross))  11.8 us
  transfers between devices with their start and end apart: 28, of which 7 were waited for; matrix products, arithmetic and copies ran while one was open for 0% of the time, Pallas kernels for 34%

profile of v7, /device:TPU:0, one launch (start us, length us, event | category | flops | bytes accessed | tf_op | source)
XLA Modules:
  0.0 71.4 jit_solution(16238759151906255984)
XLA Ops:
  0.6 1.3 %route.1 = (bf16[256,512]{1,0:T(8,128)(2,1)S(1)}, bf16[256,384]{1,0:T(8,128)(2,1)S(1)}, bf16[32,512]{1,0:T(8,128)(2,1)S(1)}, bf16[32,512]{1,0:T(8,128)(2,1)S(1)}...) custom-call(s32[4,16]{1,0:T(4,128)} %bitcast.20, ...), custom_call_target="tpu_custom_call" | custom-call | tf_op jit(solution)/shard_map/route/pallas_call | solution.py:32
  2.5 5.7 %collective-permute-start.1 = (bf16[32,512]{1,0:T(8,128)(2,1)S(1)}, bf16[32,512]{1,0:T(8,128)(2,1)S(1)}, u32[]{:S(2)}, u32[]{:S(2)}) collective-permute-start(bf16[32,512]{1,0:T(8,128)(2,1)S(1)} %get-tuple-element.79), channel_id=1, source_target_pairs={{0,15},{1,2},{2,1},{3,4},{4,3},{5,6},{6,5},{7,8},{8,7},{9,10},{10,... | collective-permute-start | bytes 98312 | tf_op jit(solution)/shard_map/ppermute | solution.py:442
  8.1 3.5 %collective-permute-start.4 = (bf16[256,384]{1,0:T(8,128)(2,1)S(1)}, bf16[256,384]{1,0:T(8,128)(2,1)S(1)}, u32[]{:S(2)}, u32[]{:S(2)}) collective-permute-start(bf16[256,384]{1,0:T(8,128)(2,1)S(1)} %get-tuple-element.114.refs_0_), channel_id=1, source_target_pairs={{0,6},{1,7},{2,4},{3,5},{4,2},{5,3},{6,0},{7,1},{8,14},{9,15},{10,... | collective-permute-start | bytes 589832 | tf_op jit(solution)/shard_map/ppermute | solution.py:439
  11.6 2.5 %load_gate.1 = (bf16[9,512,512]{2,1,0:T(8,128)(2,1)S(1)}, bf16[288,320]{1,0:T(8,128)(2,1)S(1)}, bf16[288,320]{1,0:T(8,128)(2,1)S(1)}, f32[1,512]{1,0:T(1,128)S(1)}) custom-call(bf16[9,512,512]{2,1,0:T(8,128)(2,1)} %bitcast.17, bf16[288,320]{1,0:T(8,128)(2,1)} %constant.6.clone.refs_1_, bf16[288,320]{1,0:T(8,128)(2,1)} %constant.7.clone.refs_2_, ...), custom_call_target="tpu_custom_call" | custom-call | tf_op jit(solution)/shard_map/load_gate/pallas_call | solution.py:32
  14.1 1.9 %gate.1 = (f32[256,512]{1,0:T(8,128)S(1)}, bf16[256,256]{1,0:T(8,128)(2,1)S(1)}, bf16[512,128]{1,0:T(8,128)(2,1)S(1)}, bf16[32,256]{1,0:T(8,128)(2,1)S(1)}, bf16...) custom-call(bf16[256,512]{1,0:T(8,128)(2,1)S(1)} %get-tuple-element., ...), custom_call_target="tpu_custom_call" | custom-call | flops 5000000000 | tf_op jit(solution)/shard_map/gate/pallas_call | solution.py:32
  16.1 0.6 collective-permute-start.6
  16.7 1.0 %collective-permute-done.4.refs_3_ = bf16[256,384]{1,0:T(8,128)(2,1)S(1)} collective-permute-done((bf16[256,384]{1,0:T(8,128)(2,1)S(1)}, bf16[256,384]{1,0:T(8,128)(2,1)S(1)}, u32[]{:S(2)}, u32[]{:S(2)}) %collective-permute-start.4) | collective-permute-done | bytes 196640 | tf_op jit(solution)/shard_map/ppermute | solution.py:439
  17.7 1.2 %collective-permute-start.7 = (bf16[512,128]{1,0:T(8,128)(2,1)S(1)}, bf16[512,128]{1,0:T(8,128)(2,1)S(1)}, u32[]{:S(2)}, u32[]{:S(2)}) collective-permute-start(bf16[512,128]{1,0:T(8,128)(2,1)S(1)} %get-tuple-element.102.refs_4_), channel_id=1, source_target_pairs={{0,2},{1,3},{2,0},{3,1},{4,6},{5,7},{6,4},{7,5},{8,10},{9,11},{10,... | collective-permute-start | bytes 393224 | tf_op jit(solution)/shard_map/ppermute | solution.py:439
  18.9 2.0 %collective-permute-start.8 = (bf16[512,128]{1,0:T(8,128)(2,1)S(1)}, bf16[512,128]{1,0:T(8,128)(2,1)S(1)}, u32[]{:S(2)}, u32[]{:S(2)}) collective-permute-start(bf16[512,128]{1,0:T(8,128)(2,1)S(1)} %get-tuple-element.102.refs_4_), channel_id=1, source_target_pairs={{0,4},{1,5},{2,6},{3,7},{4,0},{5,1},{6,2},{7,3},{8,12},{9,13},{10,... | collective-permute-start | bytes 393224 | tf_op jit(solution)/shard_map/ppermute | solution.py:439
  22.2 1.3 %cand.1 = (bf16[256,256]{1,0:T(8,128)(2,1)S(1)}, bf16[320,256]{1,0:T(8,128)(2,1)S(1)}, bf16[3,288,256]{2,1,0:T(8,128)(2,1)}) custom-call(f32[256,256]{1,0:T(8,128)S(1)} %cand_x.1.acc, bf16[256,256]{1,0:T(8,128)(2,1)S(1)} %get-tuple-element.92.rh.refs_8_, bf16[32,256]{1,0:T(8,128)(2,1)S(1)} %collective-permute-done.5.rp, ...), custom_call_target="tpu_custom_call" | custom-call | flops 3000000000 | tf_op jit(solution)/shard_map/cand/pallas_call | solution.py:32
  23.5 1.5 %back_rh.1 = (f32[256,256]{1,0:T(8,128)S(1)}, bf16[32,256]{1,0:T(8,128)(2,1)S(1)}, bf16[32,256]{1,0:T(8,128)(2,1)S(1)}, f32[3,288,256]{2,1,0:T(8,128)}) custom-call(bf16[256,256]{1,0:T(8,128)(2,1)S(1)} %get-tuple-element.119.d.d_c, bf16[9,512,256]{2,1,0:T(8,128)(2,1)S(1)} %get-tuple-element.90.w.wc, bf16[64,544]{1,0:T(8,128)(2,1)S(1)} %get-tuple-element.98.rim_sel), custom_call_target="tpu_custom_call" | custom-call | tf_op jit(solution)/shard_map/back_rh/pallas_call | solution.py:32
  25.0 3.1 %collective-permute-start.11 = (bf16[32,256]{1,0:T(8,128)(2,1)S(1)}, bf16[32,256]{1,0:T(8,128)(2,1)S(1)}, u32[]{:S(2)}, u32[]{:S(2)}) collective-permute-start(bf16[32,256]{1,0:T(8,128)(2,1)S(1)} %get-tuple-element.106), channel_id=1, source_target_pairs={{0,15},{1,2},{2,1},{3,4},{4,3},{5,6},{6,5},{7,8},{8,7},{9,10},{10,... | collective-permute-start | bytes 49160 | tf_op jit(solution)/shard_map/ppermute | solution.py:442
  28.3 3.4 %collective-permute-start.14 = (bf16[320,256]{1,0:T(8,128)(2,1)S(1)}, bf16[320,256]{1,0:T(8,128)(2,1)S(1)}, u32[]{:S(2)}, u32[]{:S(2)}) collective-permute-start(bf16[320,256]{1,0:T(8,128)(2,1)S(1)} %get-tuple-element.112.refs_1_.refs_10_.d_u), channel_id=1, source_target_pairs={{0,6},{1,7},{2,4},{3,5},{4,2},{5,3},{6,0},{7,1},{8,14},{9,15},{10,... | collective-permute-start | bytes 491528 | tf_op jit(solution)/shard_map/ppermute | solution.py:439
  31.7 2.9 %near_reset.1 = (bf16[3,256,256]{2,1,0:T(8,128)(2,1)S(1)}, bf16[9,320,256]{2,1,0:T(8,128)(2,1)S(1)}) custom-call(bf16[256,384]{1,0:T(8,128)(2,1)S(1)} %get-tuple-element.114.refs_0_, bf16[256,384]{1,0:T(8,128)(2,1)S(1)} %collective-permute-done.2.refs_1_, bf16[256,384]{1,0:T(8,128)(2,1)S(1)} %collective-permute-done.3.refs_2_, ...), custom_call_target="tpu_custom_call" | custom-call | tf_op jit(solution)/shard_map/near_reset/pallas_call | solution.py:32
  35.7 2.8 %collective-permute-start.19 = (bf16[512,256]{1,0:T(8,128)(2,1)S(1)}, bf16[512,256]{1,0:T(8,128)(2,1)S(1)}, u32[]{:S(2)}, u32[]{:S(2)}) collective-permute-start(bf16[512,256]{1,0:T(8,128)(2,1)S(1)} %get-tuple-element.108.d.refs_1_), channel_id=1, source_target_pairs={{0,6},{1,7},{2,4},{3,5},{4,2},{5,3},{6,0},{7,1},{8,14},{9,15},{10,... | collective-permute-start | bytes 786440 | tf_op jit(solution)/shard_map/ppermute | solution.py:439
  38.4 2.3 %lhs_gate.1.refs_0_ = bf16[4,384,1024]{2,1,0:T(8,128)(2,1)S(1)} custom-call(bf16[256,384]{1,0:T(8,128)(2,1)S(1)} %get-tuple-element.114.refs_0_, bf16[256,384]{1,0:T(8,128)(2,1)S(1)} %collective-permute-done.2.refs_1_, bf16[256,384]{1,0:T(8,128)(2,1)S(1)} %collective-permute-done.3.refs_2_, bf16[256,384]{1,0:T(8,128)(2,1)S(1)} %collective-permute-done.4.refs_3_, ...), custom_call_target="tpu_custom_call" | custom-call | tf_op jit(solution)/shard_map/lhs_gate/pallas_call | solution.py:32
  40.7 1.1 %weights_update.1 = (f32[2,288,256]{2,1,0:T(8,128)S(1)}, bf16[2,288,128]{2,1,0:T(8,128)(2,1)S(1)}, bf16[2,288,128]{2,1,0:T(8,128)(2,1)S(1)}) custom-call(bf16[4,384,1024]{2,1,0:T(8,128)(2,1)S(1)} %lhs_gate.1.refs_0_, bf16[320,256]{1,0:T(8,128)(2,1)S(1)} %get-tuple-element.112.refs_1_.refs_10_.d_u, ...), custom_call_target="tpu_custom_call" | custom-call | tf_op jit(solution)/shard_map/weights_update/pallas_call | solution.py:32
  42.4 2.3 %lhs_cand.1.refs_0_ = bf16[4,384,1024]{2,1,0:T(8,128)(2,1)S(1)} custom-call(bf16[256,384]{1,0:T(8,128)(2,1)S(1)} %get-tuple-element.114.refs_0_, bf16[256,384]{1,0:T(8,128)(2,1)S(1)} %collective-permute-done.2.refs_1_, bf16[256,384]{1,0:T(8,128)(2,1)S(1)} %collective-permute-done.3.refs_2_, bf16[256,384]{1,0:T(8,128)(2,1)S(1)} %collective-permute-done.4.refs_3_, ...), custom_call_target="tpu_custom_call" | custom-call | tf_op jit(solution)/shard_map/lhs_cand/pallas_call | solution.py:32
  44.8 0.7 collective-permute-start.20
  45.5 1.2 %back_early.1.early = f32[3,288,512]{2,1,0:T(8,128)S(1)} custom-call(bf16[256,256]{1,0:T(8,128)(2,1)S(1)} %get-tuple-element.119.d.d_c, bf16[320,256]{1,0:T(8,128)(2,1)S(1)} %get-tuple-element.112.refs_1_.refs_10_.d_u, bf16[9,512,256]{2,1,0:T(8,128)(2,1)S(1)} %get-tuple-element.90.w.wc, bf16[9,512,512]{2,1,0:T(8,128)(2,1)S(1)} %get-tuple-element.76.w.refs_10_.wg), custom_call_target="tpu_custom_call" | custom-call | tf_op jit(solution)/shard_map/back_early/pallas_call | solution.py:32
  46.6 2.3 %back_gate.1 = (f32[256,512]{1,0:T(8,128)S(1)}, bf16[32,512]{1,0:T(8,128)(2,1)S(1)}, bf16[32,512]{1,0:T(8,128)(2,1)S(1)}, f32[3,288,512]{2,1,0:T(8,128)}) custom-call(f32[3,288,512]{2,1,0:T(8,128)S(1)} %back_early.1.early, bf16[512,256]{1,0:T(8,128)(2,1)S(1)} %get-tuple-element.108.d.refs_1_, bf16[9,512,512]{2,1,0:T(8,128)(2,1)S(1)} %get-tuple-element.76.w.refs_10_.wg, ...), custom_call_target="tpu_custom_call" | custom-call | tf_op jit(solution)/shard_map/back_gate/pallas_call | solution.py:32
  49.0 1.4 %collective-permute-done.19.refs_4_ = bf16[512,256]{1,0:T(8,128)(2,1)S(1)} collective-permute-done((bf16[512,256]{1,0:T(8,128)(2,1)S(1)}, bf16[512,256]{1,0:T(8,128)(2,1)S(1)}, u32[]{:S(2)}, u32[]{:S(2)}) %collective-permute-start.19) | collective-permute-done | bytes 262176 | tf_op jit(solution)/shard_map/ppermute | solution.py:439
  50.4 1.1 %weights_reset.1 = (f32[2,288,256]{2,1,0:T(8,128)S(1)}, bf16[2,288,256]{2,1,0:T(8,128)(2,1)S(1)}) custom-call(bf16[4,384,1024]{2,1,0:T(8,128)(2,1)S(1)} %lhs_gate.1.refs_0_, bf16[512,256]{1,0:T(8,128)(2,1)S(1)} %get-tuple-element.108.d.refs_1_, bf16[512,256]{1,0:T(8,128)(2,1)S(1)} %collective-permute-done.17.refs_2_, ...), custom_call_target="tpu_custom_call" | custom-call | tf_op jit(solution)/shard_map/weights_reset/pallas_call | solution.py:32
  51.6 1.1 %weights_cand.1 = (f32[2,288,256]{2,1,0:T(8,128)S(1)}, bf16[2,288,128]{2,1,0:T(8,128)(2,1)S(1)}, bf16[2,288,128]{2,1,0:T(8,128)(2,1)S(1)}) custom-call(bf16[4,384,1024]{2,1,0:T(8,128)(2,1)S(1)} %lhs_cand.1.refs_0_, bf16[512,256]{1,0:T(8,128)(2,1)S(1)} %get-tuple-element.108.d.refs_1_, bf16[512,256]{1,0:T(8,128)(2,1)S(1)} %collective-permute-done.17.refs_2_, ...), custom_call_target="tpu_custom_call" | custom-call | tf_op jit(solution)/shard_map/weights_cand/pallas_call | solution.py:32
  53.3 1.4 %collective-permute-done.20.refs_1_ = bf16[288,256]{1,0:T(8,128)(2,1)S(1)} collective-permute-done((bf16[288,256]{1,0:T(8,128)(2,1)S(1)}, bf16[288,256]{1,0:T(8,128)(2,1)S(1)}, u32[]{:S(2)}, u32[]{:S(2)}) %collective-permute-start.20) | collective-permute-done | bytes 147488 | tf_op jit(solution)/shard_map/ppermute | solution.py:439
  55.2 2.4 %collective-permute-start.26 = (bf16[32,512]{1,0:T(8,128)(2,1)S(1)}, bf16[32,512]{1,0:T(8,128)(2,1)S(1)}, u32[]{:S(2)}, u32[]{:S(2)}) collective-permute-start(bf16[32,512]{1,0:T(8,128)(2,1)S(1)} %get-tuple-element.139), channel_id=1, source_target_pairs={{0,15},{1,2},{2,1},{3,4},{4,3},{5,6},{6,5},{7,8},{8,7},{9,10},{10,... | collective-permute-start | bytes 98312 | tf_op jit(solution)/shard_map/ppermute | solution.py:442
  57.7 2.0 %collective-permute-start.27 = (bf16[288,256]{1,0:T(8,128)(2,1)S(1)}, bf16[288,256]{1,0:T(8,128)(2,1)S(1)}, u32[]{:S(2)}, u32[]{:S(2)}) collective-permute-start(bf16[288,256]{1,0:T(8,128)(2,1)S(1)} %bitcast.16), channel_id=1, source_target_pairs={{0,8},{1,9},{2,10},{3,11},{4,12},{5,13},{6,14},{7,15},{8,0},{9,1},... | collective-permute-start | bytes 442376 | tf_op jit(solution)/shard_map/ppermute | solution.py:439
  59.7 7.7 %collective-permute-done.24.refs_1_ = bf16[288,256]{1,0:T(8,128)(2,1)S(1)} collective-permute-done((bf16[288,256]{1,0:T(8,128)(2,1)S(1)}, bf16[288,256]{1,0:T(8,128)(2,1)S(1)}, u32[]{:S(2)}, u32[]{:S(2)}) %collective-permute-start.24) | collective-permute-done | bytes 147488 | tf_op jit(solution)/shard_map/ppermute | solution.py:439
  67.4 0.9 %sum_gate.1 = f32[288,512]{1,0:T(8,128)} custom-call(f32[288,256]{1,0:T(8,128)S(1)} %sum_update.1.update, f32[288,256]{1,0:T(8,128)S(1)} %get-tuple-element.130.refs_0_, bf16[288,256]{1,0:T(8,128)(2,1)S(1)} %collective-permute-done.24.refs_1_), custom_call_target="tpu_custom_call" | custom-call | tf_op jit(solution)/shard_map/sum_gate/pallas_call | solution.py:32
  68.3 0.9 %final.1 = (bf16[256,256]{1,0:T(8,128)(2,1)}, bf16[256,256]{1,0:T(8,128)(2,1)}) custom-call(f32[256,512]{1,0:T(8,128)S(1)} %get-tuple-element.137.inner, bf16[32,512]{1,0:T(8,128)(2,1)S(1)} %collective-permute-done.25.rp, bf16[32,512]{1,0:T(8,128)(2,1)S(1)} %collective-permute-done.26.rn, bf16[256,64]{1,0:T(8,128)(2,1)S(1)} %get-tuple-element.107.place), custom_call_target="tpu_custom_call" | custom-call | flops 3000000000 | tf_op jit(solution)/shard_map/final/pallas_call | solution.py:32
  69.2 1.5 %collective-permute-done.27.refs_1_ = bf16[288,256]{1,0:T(8,128)(2,1)S(1)} collective-permute-done((bf16[288,256]{1,0:T(8,128)(2,1)S(1)}, bf16[288,256]{1,0:T(8,128)(2,1)S(1)}, u32[]{:S(2)}, u32[]{:S(2)}) %collective-permute-start.27) | collective-permute-done | bytes 147488 | tf_op jit(solution)/shard_map/ppermute | solution.py:439
  70.7 0.7 %sum_cand.1 = f32[288,256]{1,0:T(8,128)} custom-call(f32[288,256]{1,0:T(8,128)S(1)} %get-tuple-element.142.refs_0_, bf16[288,256]{1,0:T(8,128)(2,1)S(1)} %collective-permute-done.27.refs_1_), custom_call_target="tpu_custom_call" | custom-call | tf_op jit(solution)/shard_map/sum_cand/pallas_call | solution.py:32
  (46 shorter events, 4.8 us)
Async XLA Ops:
  1.9 12.1 %collective-permute-start = (bf16[32,512]{1,0:T(8,128)(2,1)S(1)}, bf16[32,512]{1,0:T(8,128)(2,1)S(1)}, u32[]{:S(2)}, u32[]{:S(2)}) collective-permute-start(bf16[32,512]{1,0:T(8,128)(2,1)S(1)} %get-tuple-element.78), channel_id=1, source_target_pairs={{0,1},{1,0},{2,3},{3,2},{4,5},{5,4},{6,7},{7,6},{8,9},{9,8},{10,11... | collective-permute-start | bytes 98312 | tf_op jit(solution)/shard_map/ppermute | solution.py:439
  2.5 11.6 %collective-permute-start.1 = (bf16[32,512]{1,0:T(8,128)(2,1)S(1)}, bf16[32,512]{1,0:T(8,128)(2,1)S(1)}, u32[]{:S(2)}, u32[]{:S(2)}) collective-permute-start(bf16[32,512]{1,0:T(8,128)(2,1)S(1)} %get-tuple-element.79), channel_id=1, source_target_pairs={{0,15},{1,2},{2,1},{3,4},{4,3},{5,6},{6,5},{7,8},{8,7},{9,10},{10,... | collective-permute-start | bytes 98312 | tf_op jit(solution)/shard_map/ppermute | solution.py:442
  8.1 8.6 %collective-permute-start.2 = (bf16[256,384]{1,0:T(8,128)(2,1)S(1)}, bf16[256,384]{1,0:T(8,128)(2,1)S(1)}, u32[]{:S(2)}, u32[]{:S(2)}) collective-permute-start(bf16[256,384]{1,0:T(8,128)(2,1)S(1)} %get-tuple-element.114.refs_0_), channel_id=1, source_target_pairs={{0,2},{1,3},{2,0},{3,1},{4,6},{5,7},{6,4},{7,5},{8,10},{9,11},{10,... | collective-permute-start | bytes 589832 | tf_op jit(solution)/shard_map/ppermute | solution.py:439
  8.1 8.6 %collective-permute-start.3 = (bf16[256,384]{1,0:T(8,128)(2,1)S(1)}, bf16[256,384]{1,0:T(8,128)(2,1)S(1)}, u32[]{:S(2)}, u32[]{:S(2)}) collective-permute-start(bf16[256,384]{1,0:T(8,128)(2,1)S(1)} %get-tuple-element.114.refs_0_), channel_id=1, source_target_pairs={{0,4},{1,5},{2,6},{3,7},{4,0},{5,1},{6,2},{7,3},{8,12},{9,13},{10,... | collective-permute-start | bytes 589832 | tf_op jit(solution)/shard_map/ppermute | solution.py:439
  8.1 9.6 %collective-permute-start.4 = (bf16[256,384]{1,0:T(8,128)(2,1)S(1)}, bf16[256,384]{1,0:T(8,128)(2,1)S(1)}, u32[]{:S(2)}, u32[]{:S(2)}) collective-permute-start(bf16[256,384]{1,0:T(8,128)(2,1)S(1)} %get-tuple-element.114.refs_0_), channel_id=1, source_target_pairs={{0,6},{1,7},{2,4},{3,5},{4,2},{5,3},{6,0},{7,1},{8,14},{9,15},{10,... | collective-permute-start | bytes 589832 | tf_op jit(solution)/shard_map/ppermute | solution.py:439
  16.1 5.7 %collective-permute-start.5 = (bf16[32,256]{1,0:T(8,128)(2,1)S(1)}, bf16[32,256]{1,0:T(8,128)(2,1)S(1)}, u32[]{:S(2)}, u32[]{:S(2)}) collective-permute-start(bf16[32,256]{1,0:T(8,128)(2,1)S(1)} %get-tuple-element.93), channel_id=1, source_target_pairs={{0,1},{1,0},{2,3},{3,2},{4,5},{5,4},{6,7},{7,6},{8,9},{9,8},{10,11... | collective-permute-start | bytes 49160 | tf_op jit(solution)/shard_map/ppermute | solution.py:439
  16.1 6.0 %collective-permute-start.6 = (bf16[32,256]{1,0:T(8,128)(2,1)S(1)}, bf16[32,256]{1,0:T(8,128)(2,1)S(1)}, u32[]{:S(2)}, u32[]{:S(2)}) collective-permute-start(bf16[32,256]{1,0:T(8,128)(2,1)S(1)} %get-tuple-element.94), channel_id=1, source_target_pairs={{0,15},{1,2},{2,1},{3,4},{4,3},{5,6},{6,5},{7,8},{8,7},{9,10},{10,... | collective-permute-start | bytes 49160 | tf_op jit(solution)/shard_map/ppermute | solution.py:442
  17.7 10.4 %collective-permute-start.7 = (bf16[512,128]{1,0:T(8,128)(2,1)S(1)}, bf16[512,128]{1,0:T(8,128)(2,1)S(1)}, u32[]{:S(2)}, u32[]{:S(2)}) collective-permute-start(bf16[512,128]{1,0:T(8,128)(2,1)S(1)} %get-tuple-element.102.refs_4_), channel_id=1, source_target_pairs={{0,2},{1,3},{2,0},{3,1},{4,6},{5,7},{6,4},{7,5},{8,10},{9,11},{10,... | collective-permute-start | bytes 393224 | tf_op jit(solution)/shard_map/ppermute | solution.py:439
  18.9 9.3 %collective-permute-start.8 = (bf16[512,128]{1,0:T(8,128)(2,1)S(1)}, bf16[512,128]{1,0:T(8,128)(2,1)S(1)}, u32[]{:S(2)}, u32[]{:S(2)}) collective-permute-start(bf16[512,128]{1,0:T(8,128)(2,1)S(1)} %get-tuple-element.102.refs_4_), channel_id=1, source_target_pairs={{0,4},{1,5},{2,6},{3,7},{4,0},{5,1},{6,2},{7,3},{8,12},{9,13},{10,... | collective-permute-start | bytes 393224 | tf_op jit(solution)/shard_map/ppermute | solution.py:439
  20.9 7.3 %collective-permute-start.9 = (bf16[512,128]{1,0:T(8,128)(2,1)S(1)}, bf16[512,128]{1,0:T(8,128)(2,1)S(1)}, u32[]{:S(2)}, u32[]{:S(2)}) collective-permute-start(bf16[512,128]{1,0:T(8,128)(2,1)S(1)} %get-tuple-element.102.refs_4_), channel_id=1, source_target_pairs={{0,6},{1,7},{2,4},{3,5},{4,2},{5,3},{6,0},{7,1},{8,14},{9,15},{10,... | collective-permute-start | bytes 393224 | tf_op jit(solution)/shard_map/ppermute | solution.py:439
  25.0 9.6 %collective-permute-start.10 = (bf16[32,256]{1,0:T(8,128)(2,1)S(1)}, bf16[32,256]{1,0:T(8,128)(2,1)S(1)}, u32[]{:S(2)}, u32[]{:S(2)}) collective-permute-start(bf16[32,256]{1,0:T(8,128)(2,1)S(1)} %get-tuple-element.105), channel_id=1, source_target_pairs={{0,1},{1,0},{2,3},{3,2},{4,5},{5,4},{6,7},{7,6},{8,9},{9,8},{10,11... | collective-permute-start | bytes 49160 | tf_op jit(solution)/shard_map/ppermute | solution.py:439
  25.0 9.6 %collective-permute-start.11 = (bf16[32,256]{1,0:T(8,128)(2,1)S(1)}, bf16[32,256]{1,0:T(8,128)(2,1)S(1)}, u32[]{:S(2)}, u32[]{:S(2)}) collective-permute-start(bf16[32,256]{1,0:T(8,128)(2,1)S(1)} %get-tuple-element.106), channel_id=1, source_target_pairs={{0,15},{1,2},{2,1},{3,4},{4,3},{5,6},{6,5},{7,8},{8,7},{9,10},{10,... | collective-permute-start | bytes 49160 | tf_op jit(solution)/shard_map/ppermute | solution.py:442
  28.2 7.5 %collective-permute-start.12 = (bf16[320,256]{1,0:T(8,128)(2,1)S(1)}, bf16[320,256]{1,0:T(8,128)(2,1)S(1)}, u32[]{:S(2)}, u32[]{:S(2)}) collective-permute-start(bf16[320,256]{1,0:T(8,128)(2,1)S(1)} %get-tuple-element.112.refs_1_.refs_10_.d_u), channel_id=1, source_target_pairs={{0,2},{1,3},{2,0},{3,1},{4,6},{5,7},{6,4},{7,5},{8,10},{9,11},{10,... | collective-permute-start | bytes 491528 | tf_op jit(solution)/shard_map/ppermute | solution.py:439
  28.2 12.5 %collective-permute-start.13 = (bf16[320,256]{1,0:T(8,128)(2,1)S(1)}, bf16[320,256]{1,0:T(8,128)(2,1)S(1)}, u32[]{:S(2)}, u32[]{:S(2)}) collective-permute-start(bf16[320,256]{1,0:T(8,128)(2,1)S(1)} %get-tuple-element.112.refs_1_.refs_10_.d_u), channel_id=1, source_target_pairs={{0,4},{1,5},{2,6},{3,7},{4,0},{5,1},{6,2},{7,3},{8,12},{9,13},{10,... | collective-permute-start | bytes 491528 | tf_op jit(solution)/shard_map/ppermute | solution.py:439
  28.3 12.5 %collective-permute-start.14 = (bf16[320,256]{1,0:T(8,128)(2,1)S(1)}, bf16[320,256]{1,0:T(8,128)(2,1)S(1)}, u32[]{:S(2)}, u32[]{:S(2)}) collective-permute-start(bf16[320,256]{1,0:T(8,128)(2,1)S(1)} %get-tuple-element.112.refs_1_.refs_10_.d_u), channel_id=1, source_target_pairs={{0,6},{1,7},{2,4},{3,5},{4,2},{5,3},{6,0},{7,1},{8,14},{9,15},{10,... | collective-permute-start | bytes 491528 | tf_op jit(solution)/shard_map/ppermute | solution.py:439
  34.9 14.1 %collective-permute-start.17 = (bf16[512,256]{1,0:T(8,128)(2,1)S(1)}, bf16[512,256]{1,0:T(8,128)(2,1)S(1)}, u32[]{:S(2)}, u32[]{:S(2)}) collective-permute-start(bf16[512,256]{1,0:T(8,128)(2,1)S(1)} %get-tuple-element.108.d.refs_1_), channel_id=1, source_target_pairs={{0,2},{1,3},{2,0},{3,1},{4,6},{5,7},{6,4},{7,5},{8,10},{9,11},{10,... | collective-permute-start | bytes 786440 | tf_op jit(solution)/shard_map/ppermute | solution.py:439
  35.0 14.0 %collective-permute-start.18 = (bf16[512,256]{1,0:T(8,128)(2,1)S(1)}, bf16[512,256]{1,0:T(8,128)(2,1)S(1)}, u32[]{:S(2)}, u32[]{:S(2)}) collective-permute-start(bf16[512,256]{1,0:T(8,128)(2,1)S(1)} %get-tuple-element.108.d.refs_1_), channel_id=1, source_target_pairs={{0,4},{1,5},{2,6},{3,7},{4,0},{5,1},{6,2},{7,3},{8,12},{9,13},{10,... | collective-permute-start | bytes 786440 | tf_op jit(solution)/shard_map/ppermute | solution.py:439
  35.7 14.7 %collective-permute-start.19 = (bf16[512,256]{1,0:T(8,128)(2,1)S(1)}, bf16[512,256]{1,0:T(8,128)(2,1)S(1)}, u32[]{:S(2)}, u32[]{:S(2)}) collective-permute-start(bf16[512,256]{1,0:T(8,128)(2,1)S(1)} %get-tuple-element.108.d.refs_1_), channel_id=1, source_target_pairs={{0,6},{1,7},{2,4},{3,5},{4,2},{5,3},{6,0},{7,1},{8,14},{9,15},{10,... | collective-permute-start | bytes 786440 | tf_op jit(solution)/shard_map/ppermute | solution.py:439
  41.8 2.9 %collective-permute-start.15 = (bf16[2,288,128]{2,1,0:T(8,128)(2,1)S(1)}, bf16[2,288,128]{2,1,0:T(8,128)(2,1)S(1)}, u32[]{:S(2)}, u32[]{:S(2)}) collective-permute-start(bf16[2,288,128]{2,1,0:T(8,128)(2,1)S(1)} %get-tuple-element.116), channel_id=1, source_target_pairs={{0,1},{1,0},{2,3},{3,2},{4,5},{5,4},{6,7},{7,6},{8,9},{9,8},{10,11... | collective-permute-start | bytes 442376 | tf_op jit(solution)/shard_map/ppermute | solution.py:439
  41.9 2.8 %collective-permute-start.16 = (bf16[2,288,128]{2,1,0:T(8,128)(2,1)S(1)}, bf16[2,288,128]{2,1,0:T(8,128)(2,1)S(1)}, u32[]{:S(2)}, u32[]{:S(2)}) collective-permute-start(bf16[2,288,128]{2,1,0:T(8,128)(2,1)S(1)} %get-tuple-element.117), channel_id=1, source_target_pairs={{0,1},{1,0},{2,3},{3,2},{4,5},{5,4},{6,7},{7,6},{8,9},{9,8},{10,11... | collective-permute-start | bytes 442376 | tf_op jit(solution)/shard_map/ppermute | solution.py:439
  44.8 10.0 %collective-permute-start.20 = (bf16[288,256]{1,0:T(8,128)(2,1)S(1)}, bf16[288,256]{1,0:T(8,128)(2,1)S(1)}, u32[]{:S(2)}, u32[]{:S(2)}) collective-permute-start(bf16[288,256]{1,0:T(8,128)(2,1)S(1)} %bitcast.14), channel_id=1, source_target_pairs={{0,8},{1,9},{2,10},{3,11},{4,12},{5,13},{6,14},{7,15},{8,0},{9,1},... | collective-permute-start | bytes 442376 | tf_op jit(solution)/shard_map/ppermute | solution.py:439
  51.5 3.3 %collective-permute-start.21 = (bf16[2,288,256]{2,1,0:T(8,128)(2,1)S(1)}, bf16[2,288,256]{2,1,0:T(8,128)(2,1)S(1)}, u32[]{:S(2)}, u32[]{:S(2)}) collective-permute-start(bf16[2,288,256]{2,1,0:T(8,128)(2,1)S(1)} %get-tuple-element.129), channel_id=1, source_target_pairs={{0,1},{1,0},{2,3},{3,2},{4,5},{5,4},{6,7},{7,6},{8,9},{9,8},{10,11... | collective-permute-start | bytes 884744 | tf_op jit(solution)/shard_map/ppermute | solution.py:439
  52.7 4.9 %collective-permute-start.22 = (bf16[2,288,128]{2,1,0:T(8,128)(2,1)S(1)}, bf16[2,288,128]{2,1,0:T(8,128)(2,1)S(1)}, u32[]{:S(2)}, u32[]{:S(2)}) collective-permute-start(bf16[2,288,128]{2,1,0:T(8,128)(2,1)S(1)} %get-tuple-element.132), channel_id=1, source_target_pairs={{0,1},{1,0},{2,3},{3,2},{4,5},{5,4},{6,7},{7,6},{8,9},{9,8},{10,11... | collective-permute-start | bytes 442376 | tf_op jit(solution)/shard_map/ppermute | solution.py:439
  53.3 4.3 %collective-permute-start.23 = (bf16[2,288,128]{2,1,0:T(8,128)(2,1)S(1)}, bf16[2,288,128]{2,1,0:T(8,128)(2,1)S(1)}, u32[]{:S(2)}, u32[]{:S(2)}) collective-permute-start(bf16[2,288,128]{2,1,0:T(8,128)(2,1)S(1)} %get-tuple-element.133), channel_id=1, source_target_pairs={{0,1},{1,0},{2,3},{3,2},{4,5},{5,4},{6,7},{7,6},{8,9},{9,8},{10,11... | collective-permute-start | bytes 442376 | tf_op jit(solution)/shard_map/ppermute | solution.py:439
  54.9 12.5 %collective-permute-start.24 = (bf16[288,256]{1,0:T(8,128)(2,1)S(1)}, bf16[288,256]{1,0:T(8,128)(2,1)S(1)}, u32[]{:S(2)}, u32[]{:S(2)}) collective-permute-start(bf16[288,256]{1,0:T(8,128)(2,1)S(1)} %bitcast.15), channel_id=1, source_target_pairs={{0,8},{1,9},{2,10},{3,11},{4,12},{5,13},{6,14},{7,15},{8,0},{9,1},... | collective-permute-start | bytes 442376 | tf_op jit(solution)/shard_map/ppermute | solution.py:439
  55.0 13.3 %collective-permute-start.25 = (bf16[32,512]{1,0:T(8,128)(2,1)S(1)}, bf16[32,512]{1,0:T(8,128)(2,1)S(1)}, u32[]{:S(2)}, u32[]{:S(2)}) collective-permute-start(bf16[32,512]{1,0:T(8,128)(2,1)S(1)} %get-tuple-element.138), channel_id=1, source_target_pairs={{0,1},{1,0},{2,3},{3,2},{4,5},{5,4},{6,7},{7,6},{8,9},{9,8},{10,11... | collective-permute-start | bytes 98312 | tf_op jit(solution)/shard_map/ppermute | solution.py:439
  55.2 13.1 %collective-permute-start.26 = (bf16[32,512]{1,0:T(8,128)(2,1)S(1)}, bf16[32,512]{1,0:T(8,128)(2,1)S(1)}, u32[]{:S(2)}, u32[]{:S(2)}) collective-permute-start(bf16[32,512]{1,0:T(8,128)(2,1)S(1)} %get-tuple-element.139), channel_id=1, source_target_pairs={{0,15},{1,2},{2,1},{3,4},{4,3},{5,6},{6,5},{7,8},{8,7},{9,10},{10,... | collective-permute-start | bytes 98312 | tf_op jit(solution)/shard_map/ppermute | solution.py:442
  57.7 13.0 %collective-permute-start.27 = (bf16[288,256]{1,0:T(8,128)(2,1)S(1)}, bf16[288,256]{1,0:T(8,128)(2,1)S(1)}, u32[]{:S(2)}, u32[]{:S(2)}) collective-permute-start(bf16[288,256]{1,0:T(8,128)(2,1)S(1)} %bitcast.16), channel_id=1, source_target_pairs={{0,8},{1,9},{2,10},{3,11},{4,12},{5,13},{6,14},{7,15},{8,0},{9,1},... | collective-permute-start | bytes 442376 | tf_op jit(solution)/shard_map/ppermute | solution.py:439
